TPU v7x, 512 devices: a whole 4x8x8 slice. The times are simulated.
512 devices in a mesh: rep: 16 (over x, z_hi), feat: 32 (over z_lo, y, core).
Axes of the slice: x: 4, y: 8, z: 8 (z_hi: 4, z_lo: 2; z = z_hi * 2 + z_lo), core: 2. Of those that a mesh axis runs over, the one named last changes fastest.
Arguments:
- basis: float32 [16, 64, 131072], P('rep', None, 'feat'), may hold values from -6 to 6
- stream: bfloat16 [16, 2, 128, 131072], P('rep', None, None, 'feat'), may hold values from -6 to 6
Outputs:
- new_basis: float32 [16, 64, 131072], P('rep', None, 'feat')
All inputs are finite; a program needn't handle non-finite values.
Results may differ from a plain program's by a relative error of at most 0.0003.
Values sent between devices are 32-bit elements; how exact they have to be, the bound alone decides.
No kernel may reach another device: no remote copies, remote signals or barrier semaphores. Data moves between devices by JAX's collectives and lax.ppermute only.
A program may use at most 64 MiB of HBM per device.

v0:
```python
import jax
import jax.numpy as jnp
from jax import lax
from jax.sharding import PartitionSpec as P

FEAT_DEV = 4096


learn_rate = 0.5


def high_dot(left, right):
    return jnp.dot(left, right, precision=lax.Precision.HIGHEST, preferred_element_type=jnp.float32)


def step_sum(partial_value):
    return lax.psum(partial_value, "feat")


def advance(current, proj, rows, step_size):
    cov = high_dot(proj.T, proj)
    drive = high_dot(proj.T, rows)
    shrink = high_dot(cov, current)
    return current + step_size * (drive - shrink)


def per_device(basis, stream):
    start = basis[0]
    batches = stream[0]
    steps_here = batches.shape[0]
    batch_rows = batches.shape[1]
    total_feat = FEAT_DEV * lax.axis_size("feat")
    scale = jnp.sqrt(jnp.float32(total_feat))
    step_size = learn_rate / batch_rows
    current = start
    for step in range(steps_here):
        rows = batches[step]
        proj = step_sum(high_dot(rows, current.T)) / scale
        current = advance(current, proj, rows, step_size)
    replicas = lax.axis_size("rep")
    average = lax.psum(basis, "rep")[0] / replicas
    mixed = current + average - start
    gram = lax.psum(high_dot(mixed, mixed.T), "feat") / total_feat
    lower = jnp.linalg.cholesky(gram)
    result = lax.linalg.triangular_solve(lower, mixed, left_side=True, lower=True)
    return result[None]


def solution(mesh):
    placed = (P("rep", None, "feat"), P("rep", None, None, "feat"))
    return jax.shard_map(
        per_device, mesh=mesh, in_specs=placed, out_specs=P("rep", None, "feat"), check_vma=False
    )
```

profile of v0, /device:TPU:1, one launch (start us, length us, event | category | flops | bytes accessed | tf_op | source)
XLA Modules:
  0.0 365.0 jit_solution(18399803514366530212)
XLA Ops:
  6.5 0.0 all-reduce.2.cloned.1.call-start
  6.5 0.7 all-reduce.2.cloned.1.call-update
  7.3 0.0 copy-start
  7.3 2.8 fusion.11
  10.1 109.9 %psum.28 = f32[128,64]{0,1:T(8,128)S(1)} all-reduce(f32[128,64]{0,1:T(8,128)S(1)} %fusion.11), channel_id=1, replica_groups=mesh['rep'=16,'feat'=32] {'feat'}, use_global_device_ids=true, to_apply=%region_0.0 | all-reduce | flops 8192 | bytes 65536 | tf_op jit(solution)/shard_map/psum | solution.py:17
  120.0 0.2 fusion.25
  120.2 1.8 fusion.9
  122.0 0.0 copy-done
  122.0 0.0 copy-start.1
  122.0 1.1 fusion.3
  123.1 0.5 copy-done.1
  123.6 1.2 convolution_bitcast_fusion.1
  124.8 108.1 %psum.29 = f32[128,64]{0,1:T(8,128)S(1)} all-reduce(f32[128,64]{0,1:T(8,128)S(1)} %convolution_bitcast_fusion.1), channel_id=1, replica_groups=mesh['rep'=16,'feat'=32] {'feat'}, use_global_device_ids=true, to_apply=%region_1.0 | all-reduce | flops 8192 | bytes 65536 | tf_op jit(solution)/shard_map/psum | solution.py:17
  232.9 0.2 fusion.22
  233.1 2.8 fusion.6
  235.8 0.0 all-reduce.2.cloned.1.call-done
  235.8 2.7 fusion.5
  238.6 1.0 fusion.36
  239.6 104.4 %psum.31 = f32[64,64]{0,1:T(8,128)S(1)} all-reduce(f32[64,64]{0,1:T(8,128)S(1)} %fusion.36), channel_id=1, replica_groups=mesh['rep'=16,'feat'=32] {'feat'}, use_global_device_ids=true, to_apply=%region_3.0 | all-reduce | flops 4096 | bytes 32768 | tf_op jit(solution)/shard_map/psum | solution.py:43
  344.0 0.1 copy.4
  344.1 5.8 %cholesky.16 = f32[64,64]{1,0:T(8,128)S(1)} custom-call(f32[64,64]{1,0:T(8,128)S(1)} %fusion.21), custom_call_target="Cholesky" | custom-call | tf_op jit(solution)/shard_map/jit(cholesky)/cholesky | solution.py:44
  350.0 0.6 compare_reduce_fusion
  350.6 0.7 fusion.19
  351.3 4.9 %custom-call.6 = f32[1,64,64]{1,2,0:T(8,128)S(1)} custom-call(f32[1,64,64]{2,1,0:T(8,128)S(1)} %fusion.19), custom_call_target="InvertDiagBlocksLowerTriangular" | custom-call | tf_op jit(solution)/shard_map/triangular_solve | solution.py:45
  356.2 2.0 convolution_bitcast_fusion
  (3 shorter events, 0.0 us)
Async XLA Ops:
  6.5 229.3 %all-reduce.2.cloned.1.call-start = ((), (), s32[]{:S(2)}) async-start(), calls=%async_computation | async-start | bytes 2097152 | tf_op jit(solution)/shard_map/psum | solution.py:41
  7.3 114.8 %copy-start = (f32[1,64,4096]{2,1,0:T(8,128)S(1)}, f32[1,64,4096]{2,1,0:T(8,128)}, u32[]{:S(2)}) copy-start(f32[1,64,4096]{2,1,0:T(8,128)} %param.2) | copy-start | bytes 3145732
  122.0 1.6 copy-start.1
Sparse Core Ops, SparseCore 0:
  10.3 171.0 all-reduce.1
where the time goes:
time: 365 us
  blocking collectives  322 us (88%)
  matrix products  15.7 us (4%)
  between operations  13.5 us (4%)
  other arithmetic  12.1 us (3%)
    psum x2, blocking collectives, step_sum(): return lax.psum(partial_value, 'feat')  218 us
    psum x1, blocking collectives, per_device(): gram = lax.psum(high_dot(mixed, mixed.T), 'feat') / total_feat  104 us
    dot_general x9, matrix products, high_dot(): jnp.dot(left, right, precision=lax.Precision.HIGHEST, preferred_element_t...  13.7 us
  transfers between devices with their start and end apart: 1, of which 0 were waited for; matrix products, arithmetic and copies ran while one was open for 3% of the time, Pallas kernels for 0%

commit v1 on v0

v1 whole, which is shorter than its diff:
```python
import jax
import jax.numpy as jnp
from jax import lax
from jax.experimental import pallas as pl
from jax.experimental.pallas import tpu as pltpu
from jax.sharding import Mesh, PartitionSpec as P

REP = ("x", "zh")
FEAT = ("zl", "y", "core")
AXES = REP + FEAT
SIZES = (4, 4, 2, 8, 2)
LEARN_RATE = 0.5
HIGHEST = lax.Precision.HIGHEST


def dot(left, right, dims):
    return lax.dot_general(
        left, right, (dims, ((), ())), precision=HIGHEST, preferred_element_type=jnp.float32
    )


def spread(value, axis, parts):
    return lax.all_to_all(jnp.broadcast_to(value, (parts,) + value.shape), axis, 0, 0)


def replica_average(start):
    rank, width = start.shape
    part = lax.all_to_all(start.reshape(4, rank // 4, width), "x", 0, 0).sum(0)
    part = lax.all_to_all(part.reshape(4, rank // 16, width), "zh", 0, 0).sum(0)
    part = spread(part * (1.0 / 16.0), "zh", 4).reshape(rank // 4, width)
    return spread(part, "x", 4).reshape(rank, width)


def feature_sum(value):
    part = lax.all_to_all(value.reshape(32, 8, 128), FEAT, 0, 0).sum(0)
    return spread(part, FEAT, 32).reshape(256, 128)


def finish_kernel(parts_ref, mixed_ref, out_ref, *, total_feat):
    packed = parts_ref[0]
    for index in range(1, parts_ref.shape[0]):
        packed = packed + parts_ref[index]
    packed = packed / total_feat
    gram = jnp.concatenate([packed[:, :64], packed[:, 64:]], axis=0)
    lanes = lax.broadcasted_iota(jnp.int32, (8, 128), 1)
    subs = lax.broadcasted_iota(jnp.int32, (8, 128), 0)
    blocks = []
    for b in range(8):
        eye = jnp.where(lanes == subs + (64 + 8 * b), 1.0, 0.0).astype(jnp.float32)
        left = jnp.concatenate([gram[8 * b : 8 * b + 8], jnp.zeros((8, 64), jnp.float32)], axis=1)
        blocks.append(left + eye)
    done = []
    for k in range(64):
        home, sub = divmod(k, 8)
        row = blocks[home][sub : sub + 1, :]
        pivot = row[:, k : k + 1]
        scaled = row / pivot
        for b in range(home, 8):
            col = blocks[b][:, k : k + 1]
            if b == home:
                col = jnp.where(subs[:, :1] > sub, col, 0.0)
            blocks[b] = blocks[b] - col * scaled
        done.append(row[:, 64:] * lax.rsqrt(pivot))
    inverse = jnp.concatenate(done, axis=0)
    out_ref[...] = jnp.dot(
        inverse, mixed_ref[...], precision=HIGHEST, preferred_element_type=jnp.float32
    )


def finish(parts, mixed, total_feat):
    import functools

    return pl.pallas_call(
        functools.partial(finish_kernel, total_feat=total_feat),
        out_shape=jax.ShapeDtypeStruct(mixed.shape, jnp.float32),
        in_specs=[pl.BlockSpec(memory_space=pltpu.VMEM)] * 2,
        out_specs=pl.BlockSpec(memory_space=pltpu.VMEM),
        compiler_params=pltpu.CompilerParams(vmem_limit_bytes=32 * 1024 * 1024),
    )(parts, mixed)


def per_device(basis, stream):
    start = basis[0]
    rows0, rows1 = stream[0, 0], stream[0, 1]
    rank = start.shape[0]
    total_feat = start.shape[1] * 32
    inv_scale = 1.0 / jnp.sqrt(jnp.float32(total_feat))
    step_size = LEARN_RATE / rows0.shape[0]

    on_cols = ((1,), (1,))
    start_t = dot(stream[0].reshape(256, -1), start, on_cols)
    cross = dot(rows1, rows0, on_cols)
    packed = jnp.concatenate([jnp.concatenate([start_t[:128], start_t[128:]], axis=1), cross], axis=0)
    average = replica_average(start)
    packed = feature_sum(packed)

    eye = jnp.eye(rank, dtype=jnp.float32)
    on_rows = ((0,), (0,))
    plain = ((1,), (0,))
    proj0 = packed[:128, :64] * inv_scale
    cov0 = dot(proj0, proj0, on_rows)
    keep0 = eye - step_size * cov0
    proj1 = (dot(packed[:128, 64:], keep0, plain) + step_size * dot(packed[128:], proj0, plain)) * inv_scale
    cov1 = dot(proj1, proj1, on_rows)
    mix_b = step_size * (step_size * dot(cov1, cov0, plain) - cov0 - cov1)
    mix_0 = step_size * (proj0.T - step_size * dot(cov1, proj0, ((1,), (1,))))
    mix_1 = step_size * proj1.T
    delta = dot(mix_b, start, plain) + dot(mix_0, rows0, plain) + dot(mix_1, rows1, plain)

    mixed = average + delta
    gram = dot(mixed, mixed, on_cols)
    gram = jnp.concatenate([gram[:32], gram[32:]], axis=1)
    gram = gram + lax.ppermute(gram, "core", [(0, 1), (1, 0)])
    parts = spread(gram, ("zl", "y"), 16)
    return finish(parts, mixed, float(total_feat))[None]


def solution(mesh):
    fine = Mesh(mesh.devices.reshape(SIZES), AXES)
    placed = (P(REP, None, FEAT), P(REP, None, None, FEAT))
    return jax.shard_map(
        per_device, mesh=fine, in_specs=placed, out_specs=P(REP, None, FEAT), check_vma=False
    )
```

time: 365 us -> 136 us (0.37)
  blocking collectives: 322 us -> 46.8 us
  waiting for transfers between devices: 0.71 us -> 33.4 us
  starting transfers between devices: 0.01 us -> 29.2 us
  between operations: 13.5 us -> 0.21 us
  other arithmetic: 12.1 us -> 0.34 us
  Pallas kernels: 0 us -> 7.3 us
    psum x3 -> x0, blocking collectives: 322 us -> none  [the longest x2 218 us: step_sum(): return lax.psum(partial_value, 'feat')]
    all_to_all x0 -> x3, blocking collectives: none -> 46.8 us  [the longest x2 27.4 us: spread(): lax.all_to_all(jnp.broadcast_to(value, (parts,) + value.shape), axis, 0, 0)]
    all_to_all x0 -> x4, waiting for transfers between devices: none -> 32.6 us  [the longest x2 14.4 us: spread(): lax.all_to_all(jnp.broadcast_to(value, (parts,) + value.shape), axis, 0, 0)]
    all_to_all x0 -> x4, starting transfers between devices: none -> 20.8 us  [the longest x1 9.12 us: replica_average(): part = lax.all_to_all(part.reshape(4, rank // 16, width), 'zh', 0, 0).sum(0)]
    another operation x5 -> x0, other arithmetic: 12.1 us -> none  [the longest x3 6.52 us: per_device(): lower = jnp.linalg.cholesky(gram)]
    ppermute x0 -> x1, starting transfers between devices: none -> 8.46 us  [per_device(): gram = gram + lax.ppermute(gram, 'core', [(0, 1), (1, 0)])]
    pallas_call x0 -> x1, Pallas kernels: none -> 7.3 us  [finish(): pl.pallas_call(functools.partial(finish_kernel, total_feat=total_feat), o...]
    dot_general x9 -> x12, matrix products: 13.7 us -> 14.3 us  [dot(): lax.dot_general(left, right, (dims, ((), ())), precision=HIGHEST, preferr...]
  transfers between devices with their start and end apart: 1 -> 5, of which waited for: 0 -> 5; matrix products, arithmetic and copies ran while one was open for 3% -> 5% of each run, Pallas kernels for 0% -> 0%
where the time goes in v1:
time: 136 us; the launch traced here: 135 us
  blocking collectives  46.8 us (34%)
  waiting for transfers between devices  33.4 us (25%)
  starting transfers between devices  29.2 us (21%)
  matrix products  14.3 us (11%)
  Pallas kernels  7.3 us (5%)
  local copies, waits for them, and re-layouts  2.96 us (2%)
    all_to_all x2, blocking collectives, spread(): lax.all_to_all(jnp.broadcast_to(value, (parts,) + value.shape), axis, 0, 0)  27.4 us
    all_to_all x1, blocking collectives, feature_sum(): part = lax.all_to_all(value.reshape(32, 8, 128), FEAT, 0, 0).sum(0)  19.4 us
    all_to_all x2, waiting for transfers between devices, spread(): lax.all_to_all(jnp.broadcast_to(value, (parts,) + value.shape), axis, 0, 0)  14.4 us
    dot_general x12, matrix products, dot(): lax.dot_general(left, right, (dims, ((), ())), precision=HIGHEST, preferr...  14.3 us
    all_to_all x1, waiting for transfers between devices, replica_average(): part = lax.all_to_all(start.reshape(4, rank // 4, width), 'x', 0, 0).sum(0)  12.3 us
    all_to_all x1, starting transfers between devices, replica_average(): part = lax.all_to_all(part.reshape(4, rank // 16, width), 'zh', 0, 0).sum(0)  9.12 us
    ppermute x1, starting transfers between devices, per_device(): gram = gram + lax.ppermute(gram, 'core', [(0, 1), (1, 0)])  8.46 us
    all_to_all x2, starting transfers between devices, spread(): lax.all_to_all(jnp.broadcast_to(value, (parts,) + value.shape), axis, 0, 0)  7.65 us
  transfers between devices with their start and end apart: 5, of which 5 were waited for; matrix products, arithmetic and copies ran while one was open for 5% of the time, Pallas kernels for 0%

profile of v1, /device:TPU:1, one launch (start us, length us, event | category | flops | bytes accessed | tf_op | source)
XLA Modules:
  0.0 134.6 jit_solution(2957870756856937845)
XLA Ops:
  0.0 0.0 copy-start
  0.0 2.1 %fusion.8 = f32[128,128]{0,1:T(8,128)S(1)} fusion(bf16[1,2,128,4096]{3,2,1,0:T(8,128)(2,1)} %param.3), kind=kOutput, calls=%fused_computation.13 | convolution fusion | flops 134217728 | bytes 2162688 | tf_op jit(solution)/shard_map/dot_general | solution.py:17
  2.1 0.1 copy-done
  2.2 3.2 %fusion.14 = f32[256,64]{0,1:T(8,128)S(1)} fusion(bf16[256,4096]{1,0:T(8,128)(2,1)S(1)} %bitcast.34, f32[1,64,4096]{2,1,0:T(8,128)} %param.2), kind=kOutput, calls=%fused_computation.19 | convolution fusion | flops 805306368 | bytes 3211264 | tf_op jit(solution)/shard_map/dot_general | solution.py:17
  5.5 0.1 copy.8
  5.6 19.4 %all_to_all.35 = f32[32,8,128]{2,1,0:T(8,128)S(1)} all-to-all(f32[32,8,128]{2,1,0:T(8,128)S(1)} %bitcast.37), channel_id=1, replica_groups=mesh['x'=4,'zh'=4,'zl'=2,'y'=8,'core'=2] {'zl','y','core'}, dimensions={0} | all-to-all | bytes 262144 | tf_op jit(solution)/shard_map/all_to_all | solution.py:35
  25.1 13.4 %all_to_all.36 = f32[32,8,128]{2,1,0:T(8,128)S(1)} all-to-all(f32[32,8,128]{2,1,0:T(8,128)S(1)} %broadcast_in_dim.17), channel_id=1, replica_groups=mesh['x'=4,'zh'=4,'zl'=2,'y'=8,'core'=2] {'zl','y','core'}, dimensions={0} | all-to-all | bytes 262144 | tf_op jit(solution)/shard_map/all_to_all | solution.py:23
  38.5 4.0 %all-to-all-start = ((f32[4,16,4096]{2,1,0:T(8,128)}), f32[4,16,4096]{2,1,0:T(8,128)S(1)}, u32[]{:S(2)}, u32[]{:S(2)}) async-start(f32[4,16,4096]{2,1,0:T(8,128)} %bitcast), calls=%async_computation | async-start | bytes 2097152 | tf_op jit(solution)/shard_map/all_to_all | solution.py:28
  42.5 0.1 copy.11
  42.6 0.0 copy-start.1
  42.6 0.8 fusion.30
  43.4 0.0 copy-done.1
  43.4 12.3 %all-to-all-done = f32[4,16,4096]{2,1,0:T(8,128)S(1)} async-done(((f32[4,16,4096]{2,1,0:T(8,128)}), f32[4,16,4096]{2,1,0:T(8,128)S(1)}, u32[]{:S(2)}, u32[]{:S(2)}) %all-to-all-start) | async-done | bytes 1048608 | tf_op jit(solution)/shard_map/all_to_all | solution.py:28
  55.7 0.1 reduce_sum.27
  55.8 0.0 copy-start.3
  55.8 0.8 reshape.16
  56.6 9.1 %all-to-all-start.1 = ((f32[4,4,4096]{2,1,0:T(4,128)}), f32[4,4,4096]{2,1,0:T(4,128)S(1)}, u32[]{:S(2)}, u32[]{:S(2)}) async-start(f32[4,4,4096]{2,1,0:T(4,128)} %reshape.16), calls=%async_computation.1 | async-start | bytes 524288 | tf_op jit(solution)/shard_map/all_to_all | solution.py:29
  65.7 1.1 fusion.20
  66.8 1.0 fusion.6
  67.8 5.9 %all-to-all-done.1 = f32[4,4,4096]{2,1,0:T(4,128)S(1)} async-done(((f32[4,4,4096]{2,1,0:T(4,128)}), f32[4,4,4096]{2,1,0:T(4,128)S(1)}, u32[]{:S(2)}, u32[]{:S(2)}) %all-to-all-start.1) | async-done | bytes 262176 | tf_op jit(solution)/shard_map/all_to_all | solution.py:29
  73.7 0.1 reduce_sum.28
  73.8 0.7 broadcast_in_dim.15
  74.5 3.4 %all-to-all-start.2 = ((f32[4,4,4096]{2,1,0:T(4,128)}), f32[4,4,4096]{2,1,0:T(4,128)S(1)}, u32[]{:S(2)}, u32[]{:S(2)}) async-start(f32[4,4,4096]{2,1,0:T(4,128)} %broadcast_in_dim.15), calls=%async_computation.2 | async-start | bytes 524288 | tf_op jit(solution)/shard_map/all_to_all | solution.py:23
  77.9 0.0 copy-start.2
  77.9 0.2 fusion.23
  78.1 0.0 copy-done.3
  78.1 0.2 fusion.5
  78.3 7.6 %all-to-all-done.2 = f32[4,4,4096]{2,1,0:T(4,128)S(1)} async-done(((f32[4,4,4096]{2,1,0:T(4,128)}), f32[4,4,4096]{2,1,0:T(4,128)S(1)}, u32[]{:S(2)}, u32[]{:S(2)}) %all-to-all-start.2) | async-done | bytes 262176 | tf_op jit(solution)/shard_map/all_to_all | solution.py:23
  85.9 0.1 reshape.17
  86.0 1.0 broadcast_in_dim.16
  87.0 4.2 %all-to-all-start.3 = ((f32[4,16,4096]{2,1,0:T(8,128)}), f32[4,16,4096]{2,1,0:T(8,128)}, u32[]{:S(2)}, u32[]{:S(2)}) async-start(f32[4,16,4096]{2,1,0:T(8,128)} %broadcast_in_dim.16), calls=%async_computation.3 | async-start | bytes 2097152 | tf_op jit(solution)/shard_map/all_to_all | solution.py:23
  91.3 0.0 copy-done.2
  91.3 0.2 fusion.2
  91.5 2.2 %fusion.12 = f32[64,4096]{1,0:T(8,128)S(1)} fusion(f32[64,64]{1,0:T(8,128)S(1)} %fusion.5, f32[1,64,4096]{2,1,0:T(8,128)} %param.2), kind=kOutput, calls=%fused_computation.17 | convolution fusion | flops 201326592 | bytes 2113536 | tf_op jit(solution)/shard_map/dot_general | solution.py:17
  93.7 0.6 convolution_add_fusion.1
  94.3 6.8 %all-to-all-done.3 = f32[4,16,4096]{2,1,0:T(8,128)} async-done(((f32[4,16,4096]{2,1,0:T(8,128)}), f32[4,16,4096]{2,1,0:T(8,128)}, u32[]{:S(2)}, u32[]{:S(2)}) %all-to-all-start.3) | async-done | bytes 1048608 | tf_op jit(solution)/shard_map/all_to_all | solution.py:23
  101.1 1.8 %fusion.mixed_ref = f32[64,4096]{1,0:T(8,128)S(1)} fusion(f32[64,4096]{1,0:T(8,128)} %bitcast.1, f32[64,4096]{1,0:T(8,128)S(1)} %convolution_add_fusion.1, bf16[1,2,128,4096]{3,2,1,0:T(8,128)(2,1)S(1)} %copy-done, f32[128,64]{0,1:T(8,128)S(1)} %fusion.6), kind=kOutput, calls=%fused_computation.1 | convolution fusion | flops 403185664 | bytes 4227072 | tf_op jit(solution)/shard_map/dot_general | solution.py:17
  102.9 1.0 fusion.46
  103.9 0.1 pad_maximum_fusion.1
  104.0 8.5 %collective-permute-start = (f32[32,128]{1,0:T(8,128)S(1)}, f32[32,128]{1,0:T(8,128)S(1)}, u32[]{:S(2)}, u32[]{:S(2)}) collective-permute-start(f32[32,128]{1,0:T(8,128)S(1)} %pad_maximum_fusion.1), channel_id=1, source_target_pairs={{0,1},{1,0},{2,3},{3,2},{4,5},{5,4},{6,7},{7,6},{8,9},{9,8},{10,11... | collective-permute-start | bytes 49160 | tf_op jit(solution)/shard_map/ppermute | solution.py:113
  112.4 0.8 collective-permute-done
  113.2 0.1 fusion.55
  113.3 14.0 %all_to_all.37.parts_ref = f32[16,32,128]{2,1,0:T(8,128)S(1)} all-to-all(f32[16,32,128]{2,1,0:T(8,128)S(1)} %broadcast_in_dim.18), channel_id=1, replica_groups=mesh['x'=4,'zh'=4,'zl'=2,'y'=8,'core'=2] {'zl','y'}, dimensions={0} | all-to-all | bytes 524288 | tf_op jit(solution)/shard_map/all_to_all | solution.py:23
  127.3 7.3 %shard_map.28 = f32[64,4096]{1,0:T(8,128)} custom-call(f32[16,32,128]{2,1,0:T(8,128)S(1)} %all_to_all.37.parts_ref, f32[64,4096]{1,0:T(8,128)S(1)} %fusion.mixed_ref), custom_call_target="tpu_custom_call" | custom-call | tf_op jit(solution)/shard_map/pallas_call | solution.py:73
  (8 shorter events, 0.1 us)
Async XLA Ops:
  0.0 2.2 %copy-start = (bf16[1,2,128,4096]{3,2,1,0:T(8,128)(2,1)S(1)}, bf16[1,2,128,4096]{3,2,1,0:T(8,128)(2,1)}, u32[]{:S(2)}) copy-start(bf16[1,2,128,4096]{3,2,1,0:T(8,128)(2,1)} %param.3) | copy-start | bytes 6291460
  38.5 17.2 %all-to-all-start = ((f32[4,16,4096]{2,1,0:T(8,128)}), f32[4,16,4096]{2,1,0:T(8,128)S(1)}, u32[]{:S(2)}, u32[]{:S(2)}) async-start(f32[4,16,4096]{2,1,0:T(8,128)} %bitcast), calls=%async_computation | async-start | bytes 2097152 | tf_op jit(solution)/shard_map/all_to_all | solution.py:28
  42.6 0.8 copy-start.1
  55.8 22.3 %copy-start.3 = (f32[64,64]{1,0:T(8,128)S(1)}, f32[64,64]{1,0:T(8,128)}, u32[]{:S(2)}) copy-start(f32[64,64]{1,0:T(8,128)} %fusion.30) | copy-start | bytes 49156
  56.6 17.1 %all-to-all-start.1 = ((f32[4,4,4096]{2,1,0:T(4,128)}), f32[4,4,4096]{2,1,0:T(4,128)S(1)}, u32[]{:S(2)}, u32[]{:S(2)}) async-start(f32[4,4,4096]{2,1,0:T(4,128)} %reshape.16), calls=%async_computation.1 | async-start | bytes 524288 | tf_op jit(solution)/shard_map/all_to_all | solution.py:29
  74.5 11.4 %all-to-all-start.2 = ((f32[4,4,4096]{2,1,0:T(4,128)}), f32[4,4,4096]{2,1,0:T(4,128)S(1)}, u32[]{:S(2)}, u32[]{:S(2)}) async-start(f32[4,4,4096]{2,1,0:T(4,128)} %broadcast_in_dim.15), calls=%async_computation.2 | async-start | bytes 524288 | tf_op jit(solution)/shard_map/all_to_all | solution.py:23
  77.9 13.4 %copy-start.2 = (f32[128,64]{0,1:T(8,128)S(1)}, f32[128,64]{0,1:T(8,128)}, u32[]{:S(2)}) copy-start(f32[128,64]{0,1:T(8,128)} %copy-done.1) | copy-start | bytes 98308
  87.0 14.1 %all-to-all-start.3 = ((f32[4,16,4096]{2,1,0:T(8,128)}), f32[4,16,4096]{2,1,0:T(8,128)}, u32[]{:S(2)}, u32[]{:S(2)}) async-start(f32[4,16,4096]{2,1,0:T(8,128)} %broadcast_in_dim.16), calls=%async_computation.3 | async-start | bytes 2097152 | tf_op jit(solution)/shard_map/all_to_all | solution.py:23
  104.0 9.3 %collective-permute-start = (f32[32,128]{1,0:T(8,128)S(1)}, f32[32,128]{1,0:T(8,128)S(1)}, u32[]{:S(2)}, u32[]{:S(2)}) collective-permute-start(f32[32,128]{1,0:T(8,128)S(1)} %pad_maximum_fusion.1), channel_id=1, source_target_pairs={{0,1},{1,0},{2,3},{3,2},{4,5},{5,4},{6,7},{7,6},{8,9},{9,8},{10,11... | collective-permute-start | bytes 49160 | tf_op jit(solution)/shard_map/ppermute | solution.py:113

commit v2 on v1

v2 whole, which is shorter than its diff:
```python
import functools

import jax
import jax.numpy as jnp
from jax import lax
from jax.experimental import pallas as pl
from jax.experimental.pallas import tpu as pltpu
from jax.sharding import Mesh, PartitionSpec as P

REP = ("x", "zh")
FEAT = ("zl", "y", "core")
AXES = REP + FEAT
SIZES = (4, 4, 2, 8, 2)
LEARN_RATE = 0.5
HIGHEST = lax.Precision.HIGHEST
SWAP = [(0, 1), (1, 0)]
PLAIN = ((1,), (0,))
ON_ROWS = ((0,), (0,))
ON_COLS = ((1,), (1,))


def dot(left, right, dims, precision=HIGHEST):
    return lax.dot_general(
        left, right, (dims, ((), ())), precision=precision, preferred_element_type=jnp.float32
    )


def split3(value):
    high = value.astype(jnp.bfloat16)
    rest = value - high.astype(jnp.float32)
    middle = rest.astype(jnp.bfloat16)
    low = (rest - middle.astype(jnp.float32)).astype(jnp.bfloat16)
    return high, middle, low


def kernel_call(body, shapes, args, flops, moved):
    return pl.pallas_call(
        body,
        out_shape=shapes,
        in_specs=[pl.BlockSpec(memory_space=pltpu.VMEM)] * len(args),
        out_specs=jax.tree.map(lambda _: pl.BlockSpec(memory_space=pltpu.VMEM), shapes),
        cost_estimate=pl.CostEstimate(flops=flops, bytes_accessed=moved, transcendentals=0),
        compiler_params=pltpu.CompilerParams(vmem_limit_bytes=40 * 1024 * 1024),
    )(*args)


def f32(*shape):
    return jax.ShapeDtypeStruct(shape, jnp.float32)


def products_kernel(start_ref, stream_ref, out_ref):
    rows = jnp.concatenate([stream_ref[0], stream_ref[1]], axis=0)
    right = jnp.concatenate(split3(start_ref[...]) + (stream_ref[0],), axis=0)
    both = dot(rows, right, ON_COLS, None)
    onto = both[:, :64] + (both[:, 64:128] + both[:, 128:192])
    out_ref[:128] = jnp.concatenate([onto[:128], onto[128:]], axis=1)
    out_ref[128:] = both[128:, 192:]


def pack_kernel(received_ref, feat_ref, other_ref, out_ref):
    for piece in range(32):
        cols = slice(128 * piece, 128 * piece + 128)
        out_ref[piece, :16] = (received_ref[0, :, cols] + received_ref[1, :, cols]) + (
            received_ref[2, :, cols] + received_ref[3, :, cols]
        )
        rows = slice(8 * piece, 8 * piece + 8)
        out_ref[piece, 16:] = feat_ref[rows] + other_ref[rows]


def turn_kernel(received_ref, out_ref):
    for y in range(8):
        part = (received_ref[y, :16] + received_ref[8 + y, :16]) + (
            received_ref[16 + y, :16] + received_ref[24 + y, :16]
        )
        part = part * (1.0 / 16.0)
        for zh in range(4):
            out_ref[8 * zh + y, :16] = part
    for zh in range(4):
        part = received_ref[8 * zh, 16:]
        for y in range(1, 8):
            part = part + received_ref[8 * zh + y, 16:]
        for y in range(8):
            out_ref[8 * zh + y, 16:] = part


def unpack_kernel(received_ref, chunk_ref, feat_ref):
    for piece in range(32):
        part = received_ref[piece, :16]
        for x in range(4):
            chunk_ref[x, :, 128 * piece : 128 * piece + 128] = part
        feat_ref[8 * piece : 8 * piece + 8] = received_ref[piece, 16:]


def delta_kernel(packed_ref, start_ref, stream_ref, out_ref, *, inv_scale, step_size):
    rank = start_ref.shape[0]
    index = lax.broadcasted_iota(jnp.int32, (rank, rank), 0)
    eye = jnp.where(index == lax.broadcasted_iota(jnp.int32, (rank, rank), 1), 1.0, 0.0)
    onto0 = packed_ref[:128, :64]
    onto1 = packed_ref[:128, 64:]
    cross = packed_ref[128:]
    proj0 = onto0 * inv_scale
    cov0 = dot(proj0, proj0, ON_ROWS)
    proj1 = (dot(onto1, eye - step_size * cov0, PLAIN) + step_size * dot(cross, proj0, PLAIN)) * inv_scale
    cov1 = dot(proj1, proj1, ON_ROWS)
    mix_b = step_size * (step_size * dot(cov1, cov0, PLAIN) - cov0 - cov1)
    turned0 = proj0.T
    mix_0 = step_size * (turned0 - step_size * dot(cov1, turned0, PLAIN))
    mix_1 = step_size * proj1.T
    left = jnp.concatenate(split3(jnp.concatenate([mix_0, mix_1], axis=1)), axis=0)
    rows = jnp.concatenate([stream_ref[0], stream_ref[1]], axis=0)
    three = dot(left, rows, PLAIN, None)
    out_ref[...] = dot(mix_b, start_ref[...], PLAIN) + (
        three[:64] + (three[64:128] + three[128:])
    )


def gram_kernel(average_ref, delta_ref, mixed_ref, gram_ref):
    mixed = average_ref[...] + delta_ref[...]
    mixed_ref[...] = mixed
    stacked = jnp.concatenate(split3(mixed), axis=0)
    both = dot(stacked, stacked, ON_COLS, None)
    high_mid = both[:64, 64:128]
    high_low = both[:64, 128:192]
    small = both[64:128, 64:128] + (high_low + both[128:192, :64])
    gram = both[:64, :64] + ((high_mid + both[64:128, :64]) + small)
    gram_ref[...] = jnp.concatenate([gram[:32], gram[32:]], axis=1)


def finish_kernel(parts_ref, mixed_ref, out_ref, *, total_feat):
    packed = parts_ref[0]
    for index in range(1, parts_ref.shape[0]):
        packed = packed + parts_ref[index]
    packed = packed / total_feat
    gram = jnp.concatenate([packed[:, :64], packed[:, 64:]], axis=0)
    lanes = lax.broadcasted_iota(jnp.int32, (8, 128), 1)
    subs = lax.broadcasted_iota(jnp.int32, (8, 128), 0)
    blocks = []
    for b in range(8):
        eye = jnp.where(lanes == subs + (64 + 8 * b), 1.0, 0.0).astype(jnp.float32)
        left = jnp.concatenate([gram[8 * b : 8 * b + 8], jnp.zeros((8, 64), jnp.float32)], axis=1)
        blocks.append(left + eye)
    done = []
    for k in range(64):
        home, sub = divmod(k, 8)
        row = blocks[home][sub : sub + 1, :]
        pivot = row[:, k : k + 1]
        scaled = row / pivot
        for b in range(home, 8):
            col = blocks[b][:, k : k + 1]
            if b == home:
                col = jnp.where(subs[:, :1] > sub, col, 0.0)
            blocks[b] = blocks[b] - col * scaled
        done.append(row[:, 64:] * lax.rsqrt(pivot))
    inverse = jnp.concatenate(done, axis=0)
    out_ref[...] = dot(inverse, mixed_ref[...], PLAIN)


def per_device(basis, stream):
    start, batches = basis[0], stream[0]
    rank, width = start.shape
    total_feat = float(width * 32)
    mega = 1 << 20

    arrived = lax.all_to_all(start.reshape(4, 16, width), "x", 0, 0)
    feat = kernel_call(products_kernel, f32(256, 128), (start, batches), 700 * mega, 8 * mega)
    feat = feat + lax.ppermute(feat, "core", SWAP)
    other = lax.ppermute(feat, "zl", SWAP)
    packed = kernel_call(pack_kernel, f32(32, 24, 128), (arrived, feat, other), mega, mega)
    packed = lax.all_to_all(packed, ("zh", "y"), 0, 0)
    packed = kernel_call(turn_kernel, f32(32, 24, 128), (packed,), mega, mega)
    packed = lax.all_to_all(packed, ("zh", "y"), 0, 0)
    chunk, feat = kernel_call(
        unpack_kernel, (f32(4, 16, width), f32(256, 128)), (packed,), mega, mega
    )
    average = lax.all_to_all(chunk, "x", 0, 0).reshape(rank, width)
    delta = kernel_call(
        functools.partial(
            delta_kernel, inv_scale=total_feat**-0.5, step_size=LEARN_RATE / batches.shape[1]
        ),
        f32(rank, width),
        (feat, start, batches),
        700 * mega,
        8 * mega,
    )
    mixed, gram = kernel_call(
        gram_kernel, (f32(rank, width), f32(32, 128)), (average, delta), 400 * mega, 3 * mega
    )
    gram = gram + lax.ppermute(gram, "core", SWAP)
    parts = lax.all_to_all(jnp.broadcast_to(gram, (16, 32, 128)), ("zl", "y"), 0, 0)
    return kernel_call(
        functools.partial(finish_kernel, total_feat=total_feat),
        f32(rank, width),
        (parts, mixed),
        400 * mega,
        3 * mega,
    )[None]


def solution(mesh):
    fine = Mesh(mesh.devices.reshape(SIZES), AXES)
    placed = (P(REP, None, FEAT), P(REP, None, None, FEAT))
    return jax.shard_map(
        per_device, mesh=fine, in_specs=placed, out_specs=P(REP, None, FEAT), check_vma=False
    )
```

time: 136 us -> 120 us (0.88)
  waiting for transfers between devices: 33.4 us -> 13.2 us
  matrix products: 14.3 us -> 0 us
  blocking collectives: 46.8 us -> 60.3 us
  Pallas kernels: 7.3 us -> 13.3 us
  starting transfers between devices: 29.2 us -> 26.6 us
  local copies, waits for them, and re-layouts: 2.96 us -> 4.8 us
    all_to_all x4 -> x2, waiting for transfers between devices: 32.6 us -> 6.69 us  [the longest x1 6.69 us: per_device(): average = lax.all_to_all(chunk, 'x', 0, 0).reshape(rank, width)]
    dot_general x12 -> x0, matrix products: 14.3 us -> none  [dot(): lax.dot_general(left, right, (dims, ((), ())), precision=HIGHEST, preferr...]
    all_to_all x3, blocking collectives: 46.8 us -> 60.3 us  [the longest x2 45.6 us: per_device(): packed = lax.all_to_all(packed, ('zh', 'y'), 0, 0)]
    all_to_all x4 -> x2, starting transfers between devices: 20.8 us -> 9.22 us  [the longest x1 4.97 us: per_device(): arrived = lax.all_to_all(start.reshape(4, 16, width), 'x', 0, 0)]
    ppermute x1 -> x3, starting transfers between devices: 8.46 us -> 17.4 us  [the longest x1 7.99 us: per_device(): gram = gram + lax.ppermute(gram, 'core', SWAP)]
    pallas_call x1 -> x7, Pallas kernels: 7.3 us -> 13.3 us  [kernel_call(): pl.pallas_call(body, out_shape=shapes, in_specs=[pl.BlockSpec(memory_spac...]
    ppermute x1 -> x3, waiting for transfers between devices: 0.82 us -> 6.47 us  [the longest x1 4.69 us: per_device(): other = lax.ppermute(feat, 'zl', SWAP)]
    unnamed x9 -> x12, local copies, waits for them, and re-layouts: 0.18 us -> 4.78 us
  transfers between devices with their start and end apart: 5 -> 5, of which waited for: 5 -> 4; matrix products, arithmetic and copies ran while one was open for 5% -> 0% of each run, Pallas kernels for 0% -> 3%
where the time goes in v2:
time: 120 us; the launch traced here: 118 us
  blocking collectives  60.3 us (50%)
  starting transfers between devices  26.6 us (22%)
  Pallas kernels  13.3 us (11%)
  waiting for transfers between devices  13.2 us (11%)
  local copies, waits for them, and re-layouts  4.8 us (4%)
    all_to_all x2, blocking collectives, per_device(): packed = lax.all_to_all(packed, ('zh', 'y'), 0, 0)  45.6 us
    all_to_all x1, blocking collectives, per_device(): lax.all_to_all(jnp.broadcast_to(gram, (16, 32, 128)), ('zl', 'y'), 0, 0)  14.7 us
    pallas_call x7, Pallas kernels, kernel_call(): pl.pallas_call(body, out_shape=shapes, in_specs=[pl.BlockSpec(memory_spac...  13.3 us
    ppermute x1, starting transfers between devices, per_device(): gram = gram + lax.ppermute(gram, 'core', SWAP)  7.99 us
    ppermute x1, starting transfers between devices, per_device(): feat = feat + lax.ppermute(feat, 'core', SWAP)  7.48 us
    all_to_all x1, waiting for transfers between devices, per_device(): average = lax.all_to_all(chunk, 'x', 0, 0).reshape(rank, width)  6.69 us
    all_to_all x1, starting transfers between devices, per_device(): arrived = lax.all_to_all(start.reshape(4, 16, width), 'x', 0, 0)  4.97 us
    unnamed x12, local copies, waits for them, and re-layouts  4.78 us
  transfers between devices with their start and end apart: 5, of which 4 were waited for; matrix products, arithmetic and copies ran while one was open for 0% of the time, Pallas kernels for 3%

profile of v2, /device:TPU:1, one launch (start us, length us, event | category | flops | bytes accessed | tf_op | source)
XLA Modules:
  0.0 118.3 jit_solution(498744002669349969)
XLA Ops:
  0.0 0.0 copy-start
  0.0 5.0 %all-to-all-start = ((f32[4,16,4096]{2,1,0:T(8,128)}), f32[4,16,4096]{2,1,0:T(8,128)S(1)}, u32[]{:S(2)}, u32[]{:S(2)}) async-start(f32[4,16,4096]{2,1,0:T(8,128)} %bitcast.5), calls=%async_computation | async-start | bytes 2097152 | tf_op jit(solution)/shard_map/all_to_all | solution.py:164
  5.0 0.0 copy-done
  5.0 0.0 copy-start.1
  5.0 1.6 %copy-done.1 = bf16[1,2,128,4096]{3,2,1,0:T(8,128)(2,1)S(1)} copy-done((bf16[1,2,128,4096]{3,2,1,0:T(8,128)(2,1)S(1)}, bf16[1,2,128,4096]{3,2,1,0:T(8,128)(2,1)}, u32[]{:S(2)}) %copy-start.1) | copy-done | bytes 2097176
  6.6 1.5 %shard_map.28 = f32[256,128]{1,0:T(8,128)S(1)} custom-call(f32[64,4096]{1,0:T(8,128)S(1)} %bitcast.6, bf16[2,128,4096]{2,1,0:T(8,128)(2,1)S(1)} %bitcast.8), custom_call_target="tpu_custom_call" | custom-call | flops 734003200 | bytes 8388608 | tf_op jit(solution)/shard_map/pallas_call | solution.py:37
  8.1 7.5 %collective-permute-start = (f32[256,128]{1,0:T(8,128)S(1)}, f32[256,128]{1,0:T(8,128)S(1)}, u32[]{:S(2)}, u32[]{:S(2)}) collective-permute-start(f32[256,128]{1,0:T(8,128)S(1)} %shard_map.28), channel_id=1, source_target_pairs={{0,1},{1,0},{2,3},{3,2},{4,5},{5,4},{6,7},{7,6},{8,9},{9,8},{10,11... | collective-permute-start | bytes 393224 | tf_op jit(solution)/shard_map/ppermute | solution.py:166
  15.6 1.0 collective-permute-done
  16.5 1.9 %collective-permute-start.1 = (f32[256,128]{1,0:T(8,128)S(1)}, f32[256,128]{1,0:T(8,128)S(1)}, u32[]{:S(2)}, u32[]{:S(2)}) collective-permute-start(f32[256,128]{1,0:T(8,128)S(1)} %add.6.feat_ref), channel_id=1, source_target_pairs={{0,16},{16,0},{1,17},{17,1},{2,18},{18,2},{3,19},{19,3},{4,20},{20... | collective-permute-start | bytes 393224 | tf_op jit(solution)/shard_map/ppermute | solution.py:167
  18.5 4.7 %collective-permute-done.1.other_ref = f32[256,128]{1,0:T(8,128)S(1)} collective-permute-done((f32[256,128]{1,0:T(8,128)S(1)}, f32[256,128]{1,0:T(8,128)S(1)}, u32[]{:S(2)}, u32[]{:S(2)}) %collective-permute-start.1) | collective-permute-done | bytes 131104 | tf_op jit(solution)/shard_map/ppermute | solution.py:167
  23.2 0.0 all-to-all-done.received_ref
  23.2 0.1 shard_map.29
  23.2 24.7 %all_to_all.25.received_ref = f32[32,24,128]{2,1,0:T(8,128)S(1)} all-to-all(f32[32,24,128]{2,1,0:T(8,128)S(1)} %shard_map.29), channel_id=1, replica_groups=mesh['x'=4,'zh'=4,'zl'=2,'y'=8,'core'=2] {'zh','y'}, dimensions={0} | all-to-all | bytes 786432 | tf_op jit(solution)/shard_map/all_to_all | solution.py:169
  48.0 0.0 copy-start.2
  48.0 20.8 %all_to_all.26.received_ref = f32[32,24,128]{2,1,0:T(8,128)S(1)} all-to-all(f32[32,24,128]{2,1,0:T(8,128)S(1)} %shard_map.30), channel_id=1, replica_groups=mesh['x'=4,'zh'=4,'zl'=2,'y'=8,'core'=2] {'zh','y'}, dimensions={0} | all-to-all | bytes 786432 | tf_op jit(solution)/shard_map/all_to_all | solution.py:171
  68.9 0.1 shard_map.31
  69.0 0.0 copy-start.5
  69.0 1.0 copy-done.5
  69.9 4.2 %all-to-all-start.3 = ((f32[4,16,4096]{2,1,0:T(8,128)}), f32[4,16,4096]{2,1,0:T(8,128)}, u32[]{:S(2)}, u32[]{:S(2)}) async-start(f32[4,16,4096]{2,1,0:T(8,128)} %copy-done.5), calls=%async_computation.3 | async-start | bytes 2097152 | tf_op jit(solution)/shard_map/all_to_all | solution.py:175
  74.2 0.0 copy-done.2
  74.2 2.3 %shard_map.32.delta_ref = f32[64,4096]{1,0:T(8,128)S(1)} custom-call(f32[256,128]{1,0:T(8,128)S(1)} %get-tuple-element.10.packed_ref, f32[64,4096]{1,0:T(8,128)S(1)} %bitcast.7, bf16[2,128,4096]{2,1,0:T(8,128)(2,1)S(1)} %bitcast.9), custom_call_target="tpu_custom_call" | custom-call | flops 734003200 | bytes 8388608 | tf_op jit(solution)/shard_map/pallas_call | solution.py:37
  76.5 0.0 copy-start.3
  76.5 1.0 copy-done.3
  77.5 6.7 %all-to-all-done.3 = f32[4,16,4096]{2,1,0:T(8,128)} async-done(((f32[4,16,4096]{2,1,0:T(8,128)}), f32[4,16,4096]{2,1,0:T(8,128)}, u32[]{:S(2)}, u32[]{:S(2)}) %all-to-all-start.3) | async-done | bytes 1048608 | tf_op jit(solution)/shard_map/all_to_all | solution.py:175
  84.2 0.0 copy-start.4
  84.2 1.2 %copy-done.4 = f32[64,4096]{1,0:T(8,128)S(1)} copy-done((f32[64,4096]{1,0:T(8,128)S(1)}, f32[64,4096]{1,0:T(8,128)}, u32[]{:S(2)}) %copy-start.4) | copy-done | bytes 1048600
  85.4 2.0 %shard_map.33 = (f32[64,4096]{1,0:T(8,128)S(1)}, f32[32,128]{1,0:T(8,128)S(1)}) custom-call(f32[64,4096]{1,0:T(8,128)} %bitcast.3.average_ref, f32[64,4096]{1,0:T(8,128)S(1)} %copy-done.4), custom_call_target="tpu_custom_call" | custom-call | flops 419430400 | bytes 3145728 | tf_op jit(solution)/shard_map/pallas_call | solution.py:37
  87.5 8.0 %collective-permute-start.2 = (f32[32,128]{1,0:T(8,128)S(1)}, f32[32,128]{1,0:T(8,128)S(1)}, u32[]{:S(2)}, u32[]{:S(2)}) collective-permute-start(f32[32,128]{1,0:T(8,128)S(1)} %get-tuple-element.11), channel_id=1, source_target_pairs={{0,1},{1,0},{2,3},{3,2},{4,5},{5,4},{6,7},{7,6},{8,9},{9,8},{10,11... | collective-permute-start | bytes 49160 | tf_op jit(solution)/shard_map/ppermute | solution.py:188
  95.5 0.8 collective-permute-done.2
  96.3 14.7 %all_to_all.27.parts_ref = f32[16,32,128]{2,1,0:T(8,128)S(1)} all-to-all(f32[16,32,128]{2,1,0:T(8,128)S(1)} %broadcast_in_dim.6), channel_id=1, replica_groups=mesh['x'=4,'zh'=4,'zl'=2,'y'=8,'core'=2] {'zl','y'}, dimensions={0} | all-to-all | bytes 524288 | tf_op jit(solution)/shard_map/all_to_all | solution.py:189
  111.1 7.3 %shard_map.34 = f32[64,4096]{1,0:T(8,128)} custom-call(f32[16,32,128]{2,1,0:T(8,128)S(1)} %all_to_all.27.parts_ref, f32[64,4096]{1,0:T(8,128)S(1)} %get-tuple-element.12.mixed_ref), custom_call_target="tpu_custom_call" | custom-call | flops 419430400 | bytes 3145728 | tf_op jit(solution)/shard_map/pallas_call | solution.py:37
  (4 shorter events, 0.1 us)
Async XLA Ops:
  0.0 5.0 %copy-start = (f32[1,64,4096]{2,1,0:T(8,128)S(1)}, f32[1,64,4096]{2,1,0:T(8,128)}, u32[]{:S(2)}) copy-start(f32[1,64,4096]{2,1,0:T(8,128)} %param.2) | copy-start | bytes 3145732
  0.0 23.2 %all-to-all-start = ((f32[4,16,4096]{2,1,0:T(8,128)}), f32[4,16,4096]{2,1,0:T(8,128)S(1)}, u32[]{:S(2)}, u32[]{:S(2)}) async-start(f32[4,16,4096]{2,1,0:T(8,128)} %bitcast.5), calls=%async_computation | async-start | bytes 2097152 | tf_op jit(solution)/shard_map/all_to_all | solution.py:164
  5.0 1.6 %copy-start.1 = (bf16[1,2,128,4096]{3,2,1,0:T(8,128)(2,1)S(1)}, bf16[1,2,128,4096]{3,2,1,0:T(8,128)(2,1)}, u32[]{:S(2)}) copy-start(bf16[1,2,128,4096]{3,2,1,0:T(8,128)(2,1)} %param.3) | copy-start | bytes 6291460
  8.1 8.4 %collective-permute-start = (f32[256,128]{1,0:T(8,128)S(1)}, f32[256,128]{1,0:T(8,128)S(1)}, u32[]{:S(2)}, u32[]{:S(2)}) collective-permute-start(f32[256,128]{1,0:T(8,128)S(1)} %shard_map.28), channel_id=1, source_target_pairs={{0,1},{1,0},{2,3},{3,2},{4,5},{5,4},{6,7},{7,6},{8,9},{9,8},{10,11... | collective-permute-start | bytes 393224 | tf_op jit(solution)/shard_map/ppermute | solution.py:166
  16.5 6.6 %collective-permute-start.1 = (f32[256,128]{1,0:T(8,128)S(1)}, f32[256,128]{1,0:T(8,128)S(1)}, u32[]{:S(2)}, u32[]{:S(2)}) collective-permute-start(f32[256,128]{1,0:T(8,128)S(1)} %add.6.feat_ref), channel_id=1, source_target_pairs={{0,16},{16,0},{1,17},{17,1},{2,18},{18,2},{3,19},{19,3},{4,20},{20... | collective-permute-start | bytes 393224 | tf_op jit(solution)/shard_map/ppermute | solution.py:167
  48.0 26.2 %copy-start.2 = (bf16[1,2,128,4096]{3,2,1,0:T(8,128)(2,1)S(1)}, bf16[1,2,128,4096]{3,2,1,0:T(8,128)(2,1)}, u32[]{:S(2)}) copy-start(bf16[1,2,128,4096]{3,2,1,0:T(8,128)(2,1)} %param.3) | copy-start | bytes 6291460
  69.0 1.0 copy-start.5
  69.9 14.3 %all-to-all-start.3 = ((f32[4,16,4096]{2,1,0:T(8,128)}), f32[4,16,4096]{2,1,0:T(8,128)}, u32[]{:S(2)}, u32[]{:S(2)}) async-start(f32[4,16,4096]{2,1,0:T(8,128)} %copy-done.5), calls=%async_computation.3 | async-start | bytes 2097152 | tf_op jit(solution)/shard_map/all_to_all | solution.py:175
  76.5 1.0 copy-start.3
  84.2 1.2 %copy-start.4 = (f32[64,4096]{1,0:T(8,128)S(1)}, f32[64,4096]{1,0:T(8,128)}, u32[]{:S(2)}) copy-start(f32[64,4096]{1,0:T(8,128)} %copy-done.3) | copy-start | bytes 3145732
  87.5 8.8 %collective-permute-start.2 = (f32[32,128]{1,0:T(8,128)S(1)}, f32[32,128]{1,0:T(8,128)S(1)}, u32[]{:S(2)}, u32[]{:S(2)}) collective-permute-start(f32[32,128]{1,0:T(8,128)S(1)} %get-tuple-element.11), channel_id=1, source_target_pairs={{0,1},{1,0},{2,3},{3,2},{4,5},{5,4},{6,7},{7,6},{8,9},{9,8},{10,11... | collective-permute-start | bytes 49160 | tf_op jit(solution)/shard_map/ppermute | solution.py:188

commit v3 on v2

--- a/solution.py
+++ b/solution.py
@@ -40,7 +40,7 @@
         in_specs=[pl.BlockSpec(memory_space=pltpu.VMEM)] * len(args),
         out_specs=jax.tree.map(lambda _: pl.BlockSpec(memory_space=pltpu.VMEM), shapes),
         cost_estimate=pl.CostEstimate(flops=flops, bytes_accessed=moved, transcendentals=0),
-        compiler_params=pltpu.CompilerParams(vmem_limit_bytes=40 * 1024 * 1024),
+        compiler_params=pltpu.CompilerParams(vmem_limit_bytes=20 * 1024 * 1024),
     )(*args)
 
 
@@ -57,47 +57,41 @@
     out_ref[128:] = both[128:, 192:]
 
 
-def pack_kernel(received_ref, feat_ref, other_ref, out_ref):
-    for piece in range(32):
-        cols = slice(128 * piece, 128 * piece + 128)
-        out_ref[piece, :16] = (received_ref[0, :, cols] + received_ref[1, :, cols]) + (
+def pack_kernel(received_ref, feat_ref, other_ref, out_ref, sum_ref):
+    width = out_ref.shape[2]
+    sum_ref[...] = feat_ref[...] + other_ref[...]
+    for piece in range(4):
+        cols = slice(width * piece, width * piece + width)
+        out_ref[piece] = (received_ref[0, :, cols] + received_ref[1, :, cols]) + (
             received_ref[2, :, cols] + received_ref[3, :, cols]
         )
-        rows = slice(8 * piece, 8 * piece + 8)
-        out_ref[piece, 16:] = feat_ref[rows] + other_ref[rows]
-
-
-def turn_kernel(received_ref, out_ref):
-    for y in range(8):
-        part = (received_ref[y, :16] + received_ref[8 + y, :16]) + (
-            received_ref[16 + y, :16] + received_ref[24 + y, :16]
-        )
-        part = part * (1.0 / 16.0)
-        for zh in range(4):
-            out_ref[8 * zh + y, :16] = part
-    for zh in range(4):
-        part = received_ref[8 * zh, 16:]
-        for y in range(1, 8):
-            part = part + received_ref[8 * zh + y, 16:]
-        for y in range(8):
-            out_ref[8 * zh + y, 16:] = part
-
-
-def unpack_kernel(received_ref, chunk_ref, feat_ref):
-    for piece in range(32):
-        part = received_ref[piece, :16]
+
+
+def turn_kernel(received_ref, feat_ref, other_ref, out_ref, sum_ref):
+    sum_ref[...] = feat_ref[...] + other_ref[...]
+    part = (received_ref[0] + received_ref[1]) + (received_ref[2] + received_ref[3])
+    part = part * (1.0 / 16.0)
+    for piece in range(4):
+        out_ref[piece] = part
+
+
+def unpack_kernel(received_ref, feat_ref, other_ref, chunk_ref, sum_ref):
+    width = received_ref.shape[2]
+    sum_ref[...] = feat_ref[...] + other_ref[...]
+    for piece in range(4):
+        part = received_ref[piece]
         for x in range(4):
-            chunk_ref[x, :, 128 * piece : 128 * piece + 128] = part
-        feat_ref[8 * piece : 8 * piece + 8] = received_ref[piece, 16:]
-
-
-def delta_kernel(packed_ref, start_ref, stream_ref, out_ref, *, inv_scale, step_size):
+            chunk_ref[x, :, width * piece : width * piece + width] = part
+
+
+def delta_kernel(feat_ref, other_ref, start_ref, stream_ref, out_ref, *, inv_scale, step_size):
     rank = start_ref.shape[0]
     index = lax.broadcasted_iota(jnp.int32, (rank, rank), 0)
     eye = jnp.where(index == lax.broadcasted_iota(jnp.int32, (rank, rank), 1), 1.0, 0.0)
-    onto0 = packed_ref[:128, :64]
-    onto1 = packed_ref[:128, 64:]
-    cross = packed_ref[128:]
+    packed = feat_ref[...] + other_ref[...]
+    onto0 = packed[:128, :64]
+    onto1 = packed[:128, 64:]
+    cross = packed[128:]
     proj0 = onto0 * inv_scale
     cov0 = dot(proj0, proj0, ON_ROWS)
     proj1 = (dot(onto1, eye - step_size * cov0, PLAIN) + step_size * dot(cross, proj0, PLAIN)) * inv_scale
@@ -123,7 +117,8 @@
     high_low = both[:64, 128:192]
     small = both[64:128, 64:128] + (high_low + both[128:192, :64])
     gram = both[:64, :64] + ((high_mid + both[64:128, :64]) + small)
-    gram_ref[...] = jnp.concatenate([gram[:32], gram[32:]], axis=1)
+    lower = jnp.concatenate([gram[:32, :32], gram[32:, :32], gram[32:, 32:]], axis=0)
+    gram_ref[...] = jnp.concatenate([lower[24 * part : 24 * part + 24] for part in range(4)], axis=1)
 
 
 def finish_kernel(parts_ref, mixed_ref, out_ref, *, total_feat):
@@ -131,7 +126,14 @@
     for index in range(1, parts_ref.shape[0]):
         packed = packed + parts_ref[index]
     packed = packed / total_feat
-    gram = jnp.concatenate([packed[:, :64], packed[:, 64:]], axis=0)
+    lower = jnp.concatenate([packed[:, 32 * part : 32 * part + 32] for part in range(4)], axis=0)
+    gram = jnp.concatenate(
+        [
+            jnp.concatenate([lower[:32], lower[32:64].T], axis=1),
+            jnp.concatenate([lower[32:64], lower[64:]], axis=1),
+        ],
+        axis=0,
+    )
     lanes = lax.broadcasted_iota(jnp.int32, (8, 128), 1)
     subs = lax.broadcasted_iota(jnp.int32, (8, 128), 0)
     blocks = []
@@ -155,6 +157,10 @@
     out_ref[...] = dot(inverse, mixed_ref[...], PLAIN)
 
 
+def across(value, distance):
+    return lax.ppermute(value, "y", [(y, y ^ distance) for y in range(8)])
+
+
 def per_device(basis, stream):
     start, batches = basis[0], stream[0]
     rank, width = start.shape
@@ -165,12 +171,17 @@
     feat = kernel_call(products_kernel, f32(256, 128), (start, batches), 700 * mega, 8 * mega)
     feat = feat + lax.ppermute(feat, "core", SWAP)
     other = lax.ppermute(feat, "zl", SWAP)
-    packed = kernel_call(pack_kernel, f32(32, 24, 128), (arrived, feat, other), mega, mega)
-    packed = lax.all_to_all(packed, ("zh", "y"), 0, 0)
-    packed = kernel_call(turn_kernel, f32(32, 24, 128), (packed,), mega, mega)
-    packed = lax.all_to_all(packed, ("zh", "y"), 0, 0)
+    sums = f32(256, 128)
+    pieces, feat = kernel_call(
+        pack_kernel, (f32(4, 16, width // 4), sums), (arrived, feat, other), mega, mega
+    )
+    pieces = lax.all_to_all(pieces, "zh", 0, 0)
+    pieces, feat = kernel_call(
+        turn_kernel, (f32(4, 16, width // 4), sums), (pieces, feat, across(feat, 4)), mega, mega
+    )
+    pieces = lax.all_to_all(pieces, "zh", 0, 0)
     chunk, feat = kernel_call(
-        unpack_kernel, (f32(4, 16, width), f32(256, 128)), (packed,), mega, mega
+        unpack_kernel, (f32(4, 16, width), sums), (pieces, feat, across(feat, 2)), mega, mega
     )
     average = lax.all_to_all(chunk, "x", 0, 0).reshape(rank, width)
     delta = kernel_call(
@@ -178,15 +189,15 @@
             delta_kernel, inv_scale=total_feat**-0.5, step_size=LEARN_RATE / batches.shape[1]
         ),
         f32(rank, width),
-        (feat, start, batches),
+        (feat, across(feat, 1), start, batches),
         700 * mega,
         8 * mega,
     )
     mixed, gram = kernel_call(
-        gram_kernel, (f32(rank, width), f32(32, 128)), (average, delta), 400 * mega, 3 * mega
+        gram_kernel, (f32(rank, width), f32(24, 128)), (average, delta), 400 * mega, 3 * mega
     )
     gram = gram + lax.ppermute(gram, "core", SWAP)
-    parts = lax.all_to_all(jnp.broadcast_to(gram, (16, 32, 128)), ("zl", "y"), 0, 0)
+    parts = lax.all_to_all(jnp.broadcast_to(gram, (16, 24, 128)), ("zl", "y"), 0, 0)
     return kernel_call(
         functools.partial(finish_kernel, total_feat=total_feat),
         f32(rank, width),

time: 120 us -> 113 us (0.942)
  blocking collectives: 60.3 us -> 14.1 us
  starting transfers between devices: 26.6 us -> 55.4 us
  local copies, waits for them, and re-layouts: 4.8 us -> 10.8 us
  waiting for transfers between devices: 13.2 us -> 17.2 us
    all_to_all x3 -> x1, blocking collectives: 60.3 us -> 14.1 us  [per_device(): lax.all_to_all(jnp.broadcast_to(gram, (16, 24, 128)), ('zl', 'y'), 0, 0)]
    ppermute x0 -> x3, starting transfers between devices: none -> 15.5 us  [across(): return lax.ppermute(value, 'y', [(y, y ^ distance) for y in range(8)])]
    all_to_all x0 -> x2, starting transfers between devices: none -> 12.8 us  [per_device(): pieces = lax.all_to_all(pieces, 'zh', 0, 0)]
    ppermute x0 -> x3, waiting for transfers between devices: none -> 9.07 us  [across(): return lax.ppermute(value, 'y', [(y, y ^ distance) for y in range(8)])]
    unnamed x12 -> x28, local copies, waits for them, and re-layouts: 4.78 us -> 10.8 us
    all_to_all x1, waiting for transfers between devices: 6.69 us -> 1.66 us  [per_device(): average = lax.all_to_all(chunk, 'x', 0, 0).reshape(rank, width)]
  transfers between devices with their start and end apart: 5 -> 10, of which waited for: 4 -> 7; matrix products, arithmetic and copies ran while one was open for 0% -> 0% of each run, Pallas kernels for 3% -> 3%
where the time goes in v3:
time: 113 us; the launch traced here: 111 us
  starting transfers between devices  55.4 us (49%)
  waiting for transfers between devices  17.2 us (15%)
  blocking collectives  14.1 us (12%)
  Pallas kernels  13.6 us (12%)
  local copies, waits for them, and re-layouts  10.8 us (10%)
    ppermute x3, starting transfers between devices, across(): return lax.ppermute(value, 'y', [(y, y ^ distance) for y in range(8)])  15.5 us
    all_to_all x1, blocking collectives, per_device(): lax.all_to_all(jnp.broadcast_to(gram, (16, 24, 128)), ('zl', 'y'), 0, 0)  14.1 us
    pallas_call x7, Pallas kernels, kernel_call(): pl.pallas_call(body, out_shape=shapes, in_specs=[pl.BlockSpec(memory_spac...  13.6 us
    all_to_all x2, starting transfers between devices, per_device(): pieces = lax.all_to_all(pieces, 'zh', 0, 0)  12.8 us
    unnamed x28, local copies, waits for them, and re-layouts  10.8 us
    ppermute x3, waiting for transfers between devices, across(): return lax.ppermute(value, 'y', [(y, y ^ distance) for y in range(8)])  9.07 us
    ppermute x1, starting transfers between devices, per_device(): feat = feat + lax.ppermute(feat, 'core', SWAP)  7.48 us
    ppermute x1, starting transfers between devices, per_device(): gram = gram + lax.ppermute(gram, 'core', SWAP)  7.41 us
  transfers between devices with their start and end apart: 10, of which 7 were waited for; matrix products, arithmetic and copies ran while one was open for 0% of the time, Pallas kernels for 3%

profile of v3, /device:TPU:1, one launch (start us, length us, event | category | flops | bytes accessed | tf_op | source)
XLA Modules:
  0.0 111.3 jit_solution(16044952425585571224)
XLA Ops:
  0.0 0.0 copy-start
  0.0 5.0 %all-to-all-start = ((f32[4,16,4096]{2,1,0:T(8,128)}), f32[4,16,4096]{2,1,0:T(8,128)S(1)}, u32[]{:S(2)}, u32[]{:S(2)}) async-start(f32[4,16,4096]{2,1,0:T(8,128)} %bitcast.5), calls=%async_computation | async-start | bytes 2097152 | tf_op jit(solution)/shard_map/all_to_all | solution.py:170
  5.0 0.0 copy-done
  5.0 0.0 copy-start.1
  5.0 1.6 %copy-done.1 = bf16[1,2,128,4096]{3,2,1,0:T(8,128)(2,1)S(1)} copy-done((bf16[1,2,128,4096]{3,2,1,0:T(8,128)(2,1)S(1)}, bf16[1,2,128,4096]{3,2,1,0:T(8,128)(2,1)}, u32[]{:S(2)}) %copy-start.1) | copy-done | bytes 2097176
  6.6 1.5 %shard_map.28 = f32[256,128]{1,0:T(8,128)S(1)} custom-call(f32[64,4096]{1,0:T(8,128)S(1)} %bitcast.6, bf16[2,128,4096]{2,1,0:T(8,128)(2,1)S(1)} %bitcast.8), custom_call_target="tpu_custom_call" | custom-call | flops 734003200 | bytes 8388608 | tf_op jit(solution)/shard_map/pallas_call | solution.py:37
  8.1 7.5 %collective-permute-start = (f32[256,128]{1,0:T(8,128)S(1)}, f32[256,128]{1,0:T(8,128)S(1)}, u32[]{:S(2)}, u32[]{:S(2)}) collective-permute-start(f32[256,128]{1,0:T(8,128)S(1)} %shard_map.28), channel_id=1, source_target_pairs={{0,1},{1,0},{2,3},{3,2},{4,5},{5,4},{6,7},{7,6},{8,9},{9,8},{10,11... | collective-permute-start | bytes 393224 | tf_op jit(solution)/shard_map/ppermute | solution.py:172
  15.6 1.0 collective-permute-done
  16.5 1.9 %collective-permute-start.1 = (f32[256,128]{1,0:T(8,128)S(1)}, f32[256,128]{1,0:T(8,128)S(1)}, u32[]{:S(2)}, u32[]{:S(2)}) collective-permute-start(f32[256,128]{1,0:T(8,128)S(1)} %add.6.feat_ref), channel_id=1, source_target_pairs={{0,16},{16,0},{1,17},{17,1},{2,18},{18,2},{3,19},{19,3},{4,20},{20... | collective-permute-start | bytes 393224 | tf_op jit(solution)/shard_map/ppermute | solution.py:173
  18.5 4.7 %collective-permute-done.1.other_ref = f32[256,128]{1,0:T(8,128)S(1)} collective-permute-done((f32[256,128]{1,0:T(8,128)S(1)}, f32[256,128]{1,0:T(8,128)S(1)}, u32[]{:S(2)}, u32[]{:S(2)}) %collective-permute-start.1) | collective-permute-done | bytes 131104 | tf_op jit(solution)/shard_map/ppermute | solution.py:173
  23.2 0.0 all-to-all-done.received_ref
  23.2 0.1 shard_map.29
  23.2 0.0 copy-start.6
  23.2 0.7 copy-done.6
  23.9 6.1 %all-to-all-start.1 = ((f32[4,16,1024]{2,1,0:T(8,128)}), f32[4,16,1024]{2,1,0:T(8,128)S(1)}, u32[]{:S(2)}, u32[]{:S(2)}) async-start(f32[4,16,1024]{2,1,0:T(8,128)} %copy-done.6), calls=%async_computation.1 | async-start | bytes 524288 | tf_op jit(solution)/shard_map/all_to_all | solution.py:178
  30.1 7.4 %collective-permute-start.2 = (f32[256,128]{1,0:T(8,128)S(1)}, f32[256,128]{1,0:T(8,128)S(1)}, u32[]{:S(2)}, u32[]{:S(2)}) collective-permute-start(f32[256,128]{1,0:T(8,128)S(1)} %get-tuple-element.14.feat_ref), channel_id=1, source_target_pairs={{0,8},{2,10},{4,12},{6,14},{8,0},{10,2},{12,4},{14,6},{1,9},{3,11}... | collective-permute-start | bytes 393224 | tf_op jit(solution)/shard_map/ppermute | solution.py:161
  37.5 2.4 %collective-permute-done.2.other_ref = f32[256,128]{1,0:T(8,128)S(1)} collective-permute-done((f32[256,128]{1,0:T(8,128)S(1)}, f32[256,128]{1,0:T(8,128)S(1)}, u32[]{:S(2)}, u32[]{:S(2)}) %collective-permute-start.2) | collective-permute-done | bytes 131104 | tf_op jit(solution)/shard_map/ppermute | solution.py:161
  40.0 0.0 copy-start.10
  40.0 0.6 copy-done.10
  40.6 0.0 all-to-all-done.1.received_ref
  40.6 0.9 copy-done.11
  41.6 0.0 copy-start.7
  41.6 0.7 copy-done.7
  42.3 0.6 copy-done.8
  42.9 6.6 %all-to-all-start.2 = ((f32[4,16,1024]{2,1,0:T(8,128)}), f32[4,16,1024]{2,1,0:T(8,128)S(1)}, u32[]{:S(2)}, u32[]{:S(2)}) async-start(f32[4,16,1024]{2,1,0:T(8,128)} %copy-done.7), calls=%async_computation.2 | async-start | bytes 524288 | tf_op jit(solution)/shard_map/all_to_all | solution.py:182
  49.6 6.2 %collective-permute-start.3 = (f32[256,128]{1,0:T(8,128)}, f32[256,128]{1,0:T(8,128)S(1)}, u32[]{:S(2)}, u32[]{:S(2)}) collective-permute-start(f32[256,128]{1,0:T(8,128)} %copy-done.8), channel_id=1, source_target_pairs={{0,4},{2,6},{4,0},{6,2},{8,12},{10,14},{12,8},{14,10},{1,5},{3,7},... | collective-permute-start | bytes 393224 | tf_op jit(solution)/shard_map/ppermute | solution.py:161
  55.8 2.8 %collective-permute-done.3.other_ref = f32[256,128]{1,0:T(8,128)S(1)} collective-permute-done((f32[256,128]{1,0:T(8,128)}, f32[256,128]{1,0:T(8,128)S(1)}, u32[]{:S(2)}, u32[]{:S(2)}) %collective-permute-start.3) | collective-permute-done | bytes 131104 | tf_op jit(solution)/shard_map/ppermute | solution.py:161
  58.6 0.6 copy-done.12
  59.3 0.0 all-to-all-done.2.received_ref
  59.3 0.9 copy-done.9
  60.2 0.9 copy-done.13
  61.1 0.1 shard_map.31
  61.2 0.0 copy-start.5
  61.2 1.0 copy-done.5
  62.1 5.3 %all-to-all-start.3 = ((f32[4,16,4096]{2,1,0:T(8,128)}), f32[4,16,4096]{2,1,0:T(8,128)}, u32[]{:S(2)}, u32[]{:S(2)}) async-start(f32[4,16,4096]{2,1,0:T(8,128)} %copy-done.5), calls=%async_computation.3 | async-start | bytes 2097152 | tf_op jit(solution)/shard_map/all_to_all | solution.py:186
  67.4 1.9 %collective-permute-start.4 = (f32[256,128]{1,0:T(8,128)S(1)}, f32[256,128]{1,0:T(8,128)S(1)}, u32[]{:S(2)}, u32[]{:S(2)}) collective-permute-start(f32[256,128]{1,0:T(8,128)S(1)} %get-tuple-element.18.feat_ref), channel_id=1, source_target_pairs={{0,2},{2,0},{4,6},{6,4},{8,10},{10,8},{12,14},{14,12},{1,3},{3,1},... | collective-permute-start | bytes 393224 | tf_op jit(solution)/shard_map/ppermute | solution.py:161
  69.4 3.8 %collective-permute-done.4.other_ref = f32[256,128]{1,0:T(8,128)S(1)} collective-permute-done((f32[256,128]{1,0:T(8,128)S(1)}, f32[256,128]{1,0:T(8,128)S(1)}, u32[]{:S(2)}, u32[]{:S(2)}) %collective-permute-start.4) | collective-permute-done | bytes 131104 | tf_op jit(solution)/shard_map/ppermute | solution.py:161
  73.1 0.0 copy-done.2
  73.1 2.3 %shard_map.32.delta_ref = f32[64,4096]{1,0:T(8,128)S(1)} custom-call(f32[256,128]{1,0:T(8,128)S(1)} %get-tuple-element.18.feat_ref, f32[256,128]{1,0:T(8,128)S(1)} %collective-permute-done.4.other_ref, f32[64,4096]{1,0:T(8,128)S(1)} %bitcast.7, bf16[2,128,4096]{2,1,0:T(8,128)(2,1)S(1)} %bitcast.9), custom_call_target="tpu_custom_call" | custom-call | flops 734003200 | bytes 8388608 | tf_op jit(solution)/shard_map/pallas_call | solution.py:37
  75.5 0.0 copy-start.3
  75.5 1.0 copy-done.3
  76.4 1.7 %all-to-all-done.3 = f32[4,16,4096]{2,1,0:T(8,128)} async-done(((f32[4,16,4096]{2,1,0:T(8,128)}), f32[4,16,4096]{2,1,0:T(8,128)}, u32[]{:S(2)}, u32[]{:S(2)}) %all-to-all-start.3) | async-done | bytes 1048608 | tf_op jit(solution)/shard_map/all_to_all | solution.py:186
  78.1 1.2 %copy-done.4 = f32[64,4096]{1,0:T(8,128)S(1)} copy-done((f32[64,4096]{1,0:T(8,128)S(1)}, f32[64,4096]{1,0:T(8,128)}, u32[]{:S(2)}) %copy-start.4) | copy-done | bytes 1048600
  79.3 2.1 %shard_map.33 = (f32[64,4096]{1,0:T(8,128)S(1)}, f32[24,128]{1,0:T(8,128)S(1)}) custom-call(f32[64,4096]{1,0:T(8,128)} %bitcast.3.average_ref, f32[64,4096]{1,0:T(8,128)S(1)} %copy-done.4), custom_call_target="tpu_custom_call" | custom-call | flops 419430400 | bytes 3145728 | tf_op jit(solution)/shard_map/pallas_call | solution.py:37
  81.4 7.4 %collective-permute-start.5 = (f32[24,128]{1,0:T(8,128)S(1)}, f32[24,128]{1,0:T(8,128)S(1)}, u32[]{:S(2)}, u32[]{:S(2)}) collective-permute-start(f32[24,128]{1,0:T(8,128)S(1)} %get-tuple-element.19), channel_id=1, source_target_pairs={{0,1},{1,0},{2,3},{3,2},{4,5},{5,4},{6,7},{7,6},{8,9},{9,8},{10,11... | collective-permute-start | bytes 36872 | tf_op jit(solution)/shard_map/ppermute | solution.py:199
  88.9 0.8 collective-permute-done.5
  89.7 14.1 %all_to_all.25.parts_ref = f32[16,24,128]{2,1,0:T(8,128)S(1)} all-to-all(f32[16,24,128]{2,1,0:T(8,128)S(1)} %broadcast_in_dim.6), channel_id=1, replica_groups=mesh['x'=4,'zh'=4,'zl'=2,'y'=8,'core'=2] {'zl','y'}, dimensions={0} | all-to-all | bytes 393216 | tf_op jit(solution)/shard_map/all_to_all | solution.py:200
  103.8 7.5 %shard_map.34 = f32[64,4096]{1,0:T(8,128)} custom-call(f32[16,24,128]{2,1,0:T(8,128)S(1)} %all_to_all.25.parts_ref, f32[64,4096]{1,0:T(8,128)S(1)} %get-tuple-element.20.mixed_ref), custom_call_target="tpu_custom_call" | custom-call | flops 419430400 | bytes 3145728 | tf_op jit(solution)/shard_map/pallas_call | solution.py:37
  (11 shorter events, 0.1 us)
Async XLA Ops:
  0.0 5.0 %copy-start = (f32[1,64,4096]{2,1,0:T(8,128)S(1)}, f32[1,64,4096]{2,1,0:T(8,128)}, u32[]{:S(2)}) copy-start(f32[1,64,4096]{2,1,0:T(8,128)} %param.2) | copy-start | bytes 3145732
  0.0 23.2 %all-to-all-start = ((f32[4,16,4096]{2,1,0:T(8,128)}), f32[4,16,4096]{2,1,0:T(8,128)S(1)}, u32[]{:S(2)}, u32[]{:S(2)}) async-start(f32[4,16,4096]{2,1,0:T(8,128)} %bitcast.5), calls=%async_computation | async-start | bytes 2097152 | tf_op jit(solution)/shard_map/all_to_all | solution.py:170
  5.0 1.6 %copy-start.1 = (bf16[1,2,128,4096]{3,2,1,0:T(8,128)(2,1)S(1)}, bf16[1,2,128,4096]{3,2,1,0:T(8,128)(2,1)}, u32[]{:S(2)}) copy-start(bf16[1,2,128,4096]{3,2,1,0:T(8,128)(2,1)} %param.3) | copy-start | bytes 6291460
  8.1 8.4 %collective-permute-start = (f32[256,128]{1,0:T(8,128)S(1)}, f32[256,128]{1,0:T(8,128)S(1)}, u32[]{:S(2)}, u32[]{:S(2)}) collective-permute-start(f32[256,128]{1,0:T(8,128)S(1)} %shard_map.28), channel_id=1, source_target_pairs={{0,1},{1,0},{2,3},{3,2},{4,5},{5,4},{6,7},{7,6},{8,9},{9,8},{10,11... | collective-permute-start | bytes 393224 | tf_op jit(solution)/shard_map/ppermute | solution.py:172
  16.5 6.6 %collective-permute-start.1 = (f32[256,128]{1,0:T(8,128)S(1)}, f32[256,128]{1,0:T(8,128)S(1)}, u32[]{:S(2)}, u32[]{:S(2)}) collective-permute-start(f32[256,128]{1,0:T(8,128)S(1)} %add.6.feat_ref), channel_id=1, source_target_pairs={{0,16},{16,0},{1,17},{17,1},{2,18},{18,2},{3,19},{19,3},{4,20},{20... | collective-permute-start | bytes 393224 | tf_op jit(solution)/shard_map/ppermute | solution.py:173
  23.2 0.7 copy-start.6
  23.9 49.2 %copy-start.2 = (bf16[1,2,128,4096]{3,2,1,0:T(8,128)(2,1)S(1)}, bf16[1,2,128,4096]{3,2,1,0:T(8,128)(2,1)}, u32[]{:S(2)}) copy-start(bf16[1,2,128,4096]{3,2,1,0:T(8,128)(2,1)} %param.3) | copy-start | bytes 6291460
  23.9 16.7 %all-to-all-start.1 = ((f32[4,16,1024]{2,1,0:T(8,128)}), f32[4,16,1024]{2,1,0:T(8,128)S(1)}, u32[]{:S(2)}, u32[]{:S(2)}) async-start(f32[4,16,1024]{2,1,0:T(8,128)} %copy-done.6), calls=%async_computation.1 | async-start | bytes 524288 | tf_op jit(solution)/shard_map/all_to_all | solution.py:178
  30.1 9.9 %collective-permute-start.2 = (f32[256,128]{1,0:T(8,128)S(1)}, f32[256,128]{1,0:T(8,128)S(1)}, u32[]{:S(2)}, u32[]{:S(2)}) collective-permute-start(f32[256,128]{1,0:T(8,128)S(1)} %get-tuple-element.14.feat_ref), channel_id=1, source_target_pairs={{0,8},{2,10},{4,12},{6,14},{8,0},{10,2},{12,4},{14,6},{1,9},{3,11}... | collective-permute-start | bytes 393224 | tf_op jit(solution)/shard_map/ppermute | solution.py:161
  40.0 0.7 copy-start.10
  40.6 0.9 copy-start.11
  41.6 0.7 copy-start.7
  42.3 0.7 copy-start.8
  42.9 16.3 %all-to-all-start.2 = ((f32[4,16,1024]{2,1,0:T(8,128)}), f32[4,16,1024]{2,1,0:T(8,128)S(1)}, u32[]{:S(2)}, u32[]{:S(2)}) async-start(f32[4,16,1024]{2,1,0:T(8,128)} %copy-done.7), calls=%async_computation.2 | async-start | bytes 524288 | tf_op jit(solution)/shard_map/all_to_all | solution.py:182
  49.6 9.0 %collective-permute-start.3 = (f32[256,128]{1,0:T(8,128)}, f32[256,128]{1,0:T(8,128)S(1)}, u32[]{:S(2)}, u32[]{:S(2)}) collective-permute-start(f32[256,128]{1,0:T(8,128)} %copy-done.8), channel_id=1, source_target_pairs={{0,4},{2,6},{4,0},{6,2},{8,12},{10,14},{12,8},{14,10},{1,5},{3,7},... | collective-permute-start | bytes 393224 | tf_op jit(solution)/shard_map/ppermute | solution.py:161
  58.6 0.6 copy-start.12
  59.3 0.9 copy-start.9
  60.2 0.9 copy-start.13
  61.2 1.0 copy-start.5
  62.1 16.0 %all-to-all-start.3 = ((f32[4,16,4096]{2,1,0:T(8,128)}), f32[4,16,4096]{2,1,0:T(8,128)}, u32[]{:S(2)}, u32[]{:S(2)}) async-start(f32[4,16,4096]{2,1,0:T(8,128)} %copy-done.5), calls=%async_computation.3 | async-start | bytes 2097152 | tf_op jit(solution)/shard_map/all_to_all | solution.py:186
  67.4 5.7 %collective-permute-start.4 = (f32[256,128]{1,0:T(8,128)S(1)}, f32[256,128]{1,0:T(8,128)S(1)}, u32[]{:S(2)}, u32[]{:S(2)}) collective-permute-start(f32[256,128]{1,0:T(8,128)S(1)} %get-tuple-element.18.feat_ref), channel_id=1, source_target_pairs={{0,2},{2,0},{4,6},{6,4},{8,10},{10,8},{12,14},{14,12},{1,3},{3,1},... | collective-permute-start | bytes 393224 | tf_op jit(solution)/shard_map/ppermute | solution.py:161
  75.5 1.0 copy-start.3
  78.1 1.2 %copy-start.4 = (f32[64,4096]{1,0:T(8,128)S(1)}, f32[64,4096]{1,0:T(8,128)}, u32[]{:S(2)}) copy-start(f32[64,4096]{1,0:T(8,128)} %copy-done.3) | copy-start | bytes 3145732
  81.4 8.2 %collective-permute-start.5 = (f32[24,128]{1,0:T(8,128)S(1)}, f32[24,128]{1,0:T(8,128)S(1)}, u32[]{:S(2)}, u32[]{:S(2)}) collective-permute-start(f32[24,128]{1,0:T(8,128)S(1)} %get-tuple-element.19), channel_id=1, source_target_pairs={{0,1},{1,0},{2,3},{3,2},{4,5},{5,4},{6,7},{7,6},{8,9},{9,8},{10,11... | collective-permute-start | bytes 36872 | tf_op jit(solution)/shard_map/ppermute | solution.py:199

commit v4 on v3

v4 whole, which is shorter than its diff:
```python
import functools

import jax
import jax.numpy as jnp
from jax import lax
from jax.experimental import pallas as pl
from jax.experimental.pallas import tpu as pltpu
from jax.sharding import Mesh, PartitionSpec as P

REP = ("x", "zh")
FEAT = ("zl", "y", "core")
AXES = REP + FEAT
SIZES = (4, 4, 2, 8, 2)
LEARN_RATE = 0.5
HIGHEST = lax.Precision.HIGHEST
SWAP = [(0, 1), (1, 0)]
PAIRS = (
    [(1, 6), (2, 5), (0, 3), (4, 7)],
    [(1, 2), (3, 4), (5, 6), (7, 0)],
    [(0, 1), (2, 3), (4, 5), (6, 7)],
)
PLAIN = ((1,), (0,))
ON_ROWS = ((0,), (0,))
ON_COLS = ((1,), (1,))


def dot(left, right, dims, precision=HIGHEST):
    return lax.dot_general(
        left, right, (dims, ((), ())), precision=precision, preferred_element_type=jnp.float32
    )


def split3(value):
    high = value.astype(jnp.bfloat16)
    rest = value - high.astype(jnp.float32)
    middle = rest.astype(jnp.bfloat16)
    low = (rest - middle.astype(jnp.float32)).astype(jnp.bfloat16)
    return high, middle, low


def exact_dot(left, right):
    high, middle, low = split3(left)
    left = jnp.concatenate([high, high, high, middle, middle, low], axis=1)
    high, middle, low = split3(right)
    right = jnp.concatenate([high, middle, low, high, middle, high], axis=0)
    return dot(left, right, PLAIN, None)


IN_HBM = pl.BlockSpec(memory_space=pltpu.HBM)
IN_VMEM = pl.BlockSpec(memory_space=pltpu.VMEM)
CHUNKS = 4
LARGE = 55000 << 10
DELTA_LIMIT = 54500 << 10
GRAM_LIMIT = 53000 << 10
FINISH_LIMIT = 53000 << 10


def kernel_call(body, ins, outs, args, flops, moved, scratch=(), limit=20 << 20):
    return pl.pallas_call(
        body,
        out_shape=tuple(f32(*shape) for shape, _ in outs),
        in_specs=list(ins),
        out_specs=tuple(space for _, space in outs),
        scratch_shapes=list(scratch),
        cost_estimate=pl.CostEstimate(flops=flops, bytes_accessed=moved, transcendentals=0),
        compiler_params=pltpu.CompilerParams(vmem_limit_bytes=limit),
    )(*args)


def fetch(pairs, sems):
    copies = [
        pltpu.make_async_copy(source, target, sems.at[index])
        for index, (source, target) in enumerate(pairs)
    ]
    for copy in copies:
        copy.start()
    return copies


def f32(*shape):
    return jax.ShapeDtypeStruct(shape, jnp.float32)


def products_kernel(start_ref, stream_ref, out_ref, start_vmem, stream_vmem, sems):
    width = start_vmem.shape[1] // CHUNKS
    spans = [slice(width * c, width * c + width) for c in range(CHUNKS)]
    copies = fetch(
        [(start_ref.at[:, s], start_vmem.at[:, s]) for s in spans]
        + [(stream_ref.at[:, :, s], stream_vmem.at[:, :, s]) for s in spans],
        sems,
    )
    both = None
    for c, span in enumerate(spans):
        copies[c].wait()
        copies[CHUNKS + c].wait()
        first = stream_vmem[0, :, span]
        rows = jnp.concatenate([first, stream_vmem[1, :, span]], axis=0)
        right = jnp.concatenate(split3(start_vmem[:, span]) + (first,), axis=0)
        part = dot(rows, right, ON_COLS, None)
        both = part if both is None else both + part
    onto = both[:, :64] + (both[:, 64:128] + both[:, 128:192])
    out_ref[:128] = jnp.concatenate([onto[:128], onto[128:]], axis=1)
    out_ref[128:] = both[128:, 192:]


def pack_kernel(received_ref, feat_ref, other_ref, out_ref, sum_ref, total, sems):
    sum_ref[...] = feat_ref[...] + other_ref[...]
    width = total.shape[2]
    copies = []
    for piece in range(4):
        cols = slice(width * piece, width * piece + width)
        total[piece] = (received_ref[0, :, cols] + received_ref[1, :, cols]) + (
            received_ref[2, :, cols] + received_ref[3, :, cols]
        )
        copy = pltpu.make_async_copy(total.at[piece], out_ref.at[piece], sems.at[piece])
        copy.start()
        copies.append(copy)
    for copy in copies:
        copy.wait()


def turn_kernel(received_ref, feat_ref, other_ref, out_ref, sum_ref, total, sems):
    sum_ref[...] = feat_ref[...] + other_ref[...]
    part = (received_ref[0] + received_ref[1]) + (received_ref[2] + received_ref[3])
    total[...] = part * (1.0 / 16.0)
    for copy in fetch([(total, out_ref.at[piece]) for piece in range(4)], sems):
        copy.wait()


def unpack_kernel(received_ref, feat_ref, other_ref, out_ref, sum_ref, sems):
    width = received_ref.shape[2]
    pairs = []
    for piece in range(4):
        for x in range(4):
            pairs.append(
                (received_ref.at[piece], out_ref.at[x, :, width * piece : width * piece + width])
            )
    copies = fetch(pairs, sems)
    sum_ref[...] = feat_ref[...] + other_ref[...]
    for copy in copies:
        copy.wait()


def delta_kernel(
    feat_ref, other_ref, start_ref, stream_ref, out_ref, start_vmem, stream_vmem, delta, sems, out_sems,
    *, inv_scale, step_size
):
    width = delta.shape[1] // CHUNKS
    spans = [slice(width * c, width * c + width) for c in range(CHUNKS)]
    pairs = []
    for span in spans:
        pairs.append((start_ref.at[:, span], start_vmem.at[:, span]))
        pairs.append((stream_ref.at[:, :, span], stream_vmem.at[:, :, span]))
    arriving = fetch(pairs, sems)
    rank = start_ref.shape[0]
    index = lax.broadcasted_iota(jnp.int32, (rank, rank), 0)
    eye = jnp.where(index == lax.broadcasted_iota(jnp.int32, (rank, rank), 1), 1.0, 0.0)
    onto0 = feat_ref[:128, :64] + other_ref[:128, :64]
    onto1 = feat_ref[:128, 64:] + other_ref[:128, 64:]
    cross = feat_ref[128:] + other_ref[128:]
    proj0 = onto0 * inv_scale
    cov0 = dot(proj0, proj0, ON_ROWS)
    proj1 = (dot(onto1, eye - step_size * cov0, PLAIN) + step_size * dot(cross, proj0, PLAIN)) * inv_scale
    cov1 = dot(proj1, proj1, ON_ROWS)
    mix_b = step_size * (step_size * dot(cov1, cov0, PLAIN) - cov0 - cov1)
    turned0 = proj0.T
    mix_0 = step_size * (turned0 - step_size * dot(cov1, turned0, PLAIN))
    mix_1 = step_size * proj1.T
    left = jnp.concatenate(split3(jnp.concatenate([mix_0, mix_1], axis=1)), axis=0)
    copies = []
    for c, span in enumerate(spans):
        arriving[2 * c].wait()
        arriving[2 * c + 1].wait()
        rows = jnp.concatenate([stream_vmem[0, :, span], stream_vmem[1, :, span]], axis=0)
        three = dot(left, rows, PLAIN, None)
        delta[:, span] = exact_dot(mix_b, start_vmem[:, span]) + (
            three[:64] + (three[64:128] + three[128:])
        )
        copy = pltpu.make_async_copy(delta.at[:, span], out_ref.at[:, span], out_sems.at[c])
        copy.start()
        copies.append(copy)
    for copy in copies:
        copy.wait()


def gram_kernel(average_ref, delta_ref, mixed_ref, gram_ref, delta, sems):
    width = delta.shape[1] // CHUNKS
    spans = [slice(width * c, width * c + width) for c in range(CHUNKS)]
    copies = fetch([(delta_ref.at[:, s], delta.at[:, s]) for s in spans], sems)
    both = None
    for copy, span in zip(copies, spans):
        copy.wait()
        mixed = average_ref[:, span] + delta[:, span]
        mixed_ref[:, span] = mixed
        stacked = jnp.concatenate(split3(mixed), axis=0)
        part = dot(stacked, stacked, ON_COLS, None)
        both = part if both is None else both + part
    high_mid = both[:64, 64:128]
    high_low = both[:64, 128:192]
    small = both[64:128, 64:128] + (high_low + both[128:192, :64])
    gram = both[:64, :64] + ((high_mid + both[64:128, :64]) + small)
    lower = jnp.concatenate([gram[:32, :32], gram[32:, :32], gram[32:, 32:]], axis=0)
    packed = jnp.concatenate([lower[24 * part : 24 * part + 24] for part in range(4)], axis=1)
    for copy in range(4):
        gram_ref[copy] = packed


def inverse_factor(gram):
    lanes = lax.broadcasted_iota(jnp.int32, (8, 128), 1)
    subs = lax.broadcasted_iota(jnp.int32, (8, 128), 0)
    blocks = []
    for b in range(8):
        eye = jnp.where(lanes == subs + (64 + 8 * b), 1.0, 0.0).astype(jnp.float32)
        left = jnp.concatenate([gram[8 * b : 8 * b + 8], jnp.zeros((8, 64), jnp.float32)], axis=1)
        blocks.append(left + eye)
    done = []
    for panel in range(8):
        cols = []
        for j in range(8):
            k = 8 * panel + j
            cols.append([jnp.broadcast_to(block[:, k : k + 1], (8, 128)) for block in blocks[panel:]])
        for j in range(8):
            row = jnp.broadcast_to(blocks[panel][j : j + 1, :], (8, 128))
            pivot = jnp.broadcast_to(cols[j][0][j : j + 1, :], (8, 128))
            done.append((row * lax.rsqrt(pivot))[:1, 64:])
            inverse = 1.0 / pivot
            factors = [col * inverse for col in cols[j]]
            factors[0] = jnp.where(subs > j, factors[0], 0.0)
            for later in range(j + 1, 8):
                entry = jnp.broadcast_to(cols[later][0][j : j + 1, :], (8, 128))
                cols[later] = [col - f * entry for col, f in zip(cols[later], factors)]
            for i, f in enumerate(factors):
                blocks[panel + i] = blocks[panel + i] - f * row
    return jnp.concatenate(done, axis=0)


def finish_kernel(parts_ref, mixed_ref, out_ref, result, sems, *, total_feat):
    packed = parts_ref[0]
    for index in range(1, parts_ref.shape[0]):
        packed = packed + parts_ref[index]
    packed = packed / total_feat
    lower = jnp.concatenate([packed[:, 32 * part : 32 * part + 32] for part in range(4)], axis=0)
    gram = jnp.concatenate(
        [
            jnp.concatenate([lower[:32], lower[32:64].T], axis=1),
            jnp.concatenate([lower[32:64], lower[64:]], axis=1),
        ],
        axis=0,
    )
    inverse = inverse_factor(gram)
    width = result.shape[1] // CHUNKS
    copies = []
    for c in range(CHUNKS):
        span = slice(width * c, width * c + width)
        result[:, span] = exact_dot(inverse, mixed_ref[:, span])
        copy = pltpu.make_async_copy(result.at[:, span], out_ref.at[:, span], sems.at[c])
        copy.start()
        copies.append(copy)
    for copy in copies:
        copy.wait()


def fold_kernel(parts_ref, out_ref):
    total = (parts_ref[0] + parts_ref[1]) + (parts_ref[2] + parts_ref[3])
    for index in range(8):
        out_ref[index] = total


def across(value, pairs):
    return lax.ppermute(value, "y", pairs + [(b, a) for a, b in pairs])


def per_device(basis, stream):
    start, batches = basis[0], stream[0]
    rank, width = start.shape
    total_feat = float(width * 32)
    mega = 1 << 20
    dma = pltpu.SemaphoreType.DMA
    held_start = pltpu.VMEM(start.shape, jnp.float32)
    held_stream = pltpu.VMEM(batches.shape, jnp.bfloat16)
    quarter = (4, 16, width // 4)

    arrived = lax.all_to_all(start.reshape(4, 16, width), "x", 0, 0)
    (feat,) = kernel_call(
        products_kernel,
        (IN_HBM, IN_HBM),
        [((256, 128), IN_VMEM)],
        (start, batches),
        700 * mega,
        8 * mega,
        (held_start, held_stream, dma((2 * CHUNKS,))),
        LARGE,
    )
    feat = feat + lax.ppermute(feat, "core", SWAP)
    pieces, feat = kernel_call(
        pack_kernel,
        (IN_VMEM,) * 3,
        [(quarter, IN_HBM), ((256, 128), IN_VMEM)],
        (arrived, feat, lax.ppermute(feat, "zl", SWAP)),
        mega,
        2 * mega,
        (pltpu.VMEM(quarter, jnp.float32), dma((4,))),
    )
    pieces = lax.all_to_all(pieces, "zh", 0, 0)
    pieces, feat = kernel_call(
        turn_kernel,
        (IN_VMEM,) * 3,
        [(quarter, IN_HBM), ((256, 128), IN_VMEM)],
        (pieces, feat, across(feat, PAIRS[0])),
        mega,
        2 * mega,
        (pltpu.VMEM(quarter[1:], jnp.float32), dma((4,))),
    )
    pieces = lax.all_to_all(pieces, "zh", 0, 0)
    chunk, feat = kernel_call(
        unpack_kernel,
        (IN_VMEM,) * 3,
        [((4, 16, width), IN_HBM), ((256, 128), IN_VMEM)],
        (pieces, feat, across(feat, PAIRS[1])),
        mega,
        2 * mega,
        (dma((16,)),),
        53500 << 10,
    )
    average = lax.all_to_all(chunk, "x", 0, 0).reshape(rank, width)
    (delta,) = kernel_call(
        functools.partial(
            delta_kernel, inv_scale=total_feat**-0.5, step_size=LEARN_RATE / batches.shape[1]
        ),
        (IN_VMEM, IN_VMEM, IN_HBM, IN_HBM),
        [((rank, width), IN_HBM)],
        (feat, across(feat, PAIRS[2]), start, batches),
        700 * mega,
        8 * mega,
        (held_start, held_stream, held_start, dma((2 * CHUNKS,)), dma((CHUNKS,))),
        DELTA_LIMIT,
    )
    mixed, gram = kernel_call(
        gram_kernel,
        (IN_VMEM, IN_HBM),
        [((rank, width), IN_VMEM), ((4, 24, 128), IN_VMEM)],
        (average, delta),
        400 * mega,
        3 * mega,
        (held_start, dma((CHUNKS,))),
        GRAM_LIMIT,
    )
    gram = lax.all_to_all(gram, ("zl", "core"), 0, 0)
    (gram,) = kernel_call(fold_kernel, (IN_VMEM,), [((8, 24, 128), IN_VMEM)], (gram,), mega, mega)
    parts = lax.all_to_all(gram, "y", 0, 0)
    (result,) = kernel_call(
        functools.partial(finish_kernel, total_feat=total_feat),
        (IN_VMEM, IN_VMEM),
        [((rank, width), IN_HBM)],
        (parts, mixed),
        400 * mega,
        3 * mega,
        (held_start, dma((CHUNKS,))),
        FINISH_LIMIT,
    )
    return result[None]


def solution(mesh):
    fine = Mesh(mesh.devices.reshape(SIZES), AXES)
    placed = (P(REP, None, FEAT), P(REP, None, None, FEAT))
    return jax.shard_map(
        per_device, mesh=fine, in_specs=placed, out_specs=P(REP, None, FEAT), check_vma=False
    )
```

time: 113 us -> 104 us (0.920)
  blocking collectives: 14.1 us -> 26.9 us
  starting transfers between devices: 55.4 us -> 43.6 us
  local copies, waits for them, and re-layouts: 10.8 us -> 0 us
  Pallas kernels: 13.6 us -> 15.4 us
    all_to_all x1 -> x2, blocking collectives: 14.1 us -> 26.9 us  [the longest x1 14.8 us: per_device(): parts = lax.all_to_all(gram, 'y', 0, 0)]
    unnamed x28 -> x0, local copies, waits for them, and re-layouts: 10.8 us -> none
    ppermute x5 -> x4, starting transfers between devices: 24.9 us -> 14.8 us  [the longest x3 12.9 us: across(): return lax.ppermute(value, 'y', pairs + [(b, a) for a, b in pairs])]
    all_to_all x2, waiting for transfers between devices: 0.01 us -> 1.94 us  [per_device(): pieces = lax.all_to_all(pieces, 'zh', 0, 0)]
    pallas_call x7 -> x8, Pallas kernels: 13.6 us -> 15.4 us  [kernel_call(): pl.pallas_call(body, out_shape=tuple((f32(*shape) for shape, _ in outs)),...]
    ppermute x5 -> x4, waiting for transfers between devices: 14.6 us -> 13.2 us  [the longest x3 8.47 us: across(): return lax.ppermute(value, 'y', pairs + [(b, a) for a, b in pairs])]
    all_to_all x1, waiting for transfers between devices: 1.66 us -> 0.25 us  [per_device(): average = lax.all_to_all(chunk, 'x', 0, 0).reshape(rank, width)]
  transfers between devices with their start and end apart: 10 -> 9, of which waited for: 7 -> 8; matrix products, arithmetic and copies ran while one was open for 0% -> 0% of each run, Pallas kernels for 3% -> 7%
where the time goes in v4:
time: 104 us; the launch traced here: 102 us
  starting transfers between devices  43.6 us (42%)
  blocking collectives  26.9 us (26%)
  waiting for transfers between devices  16.3 us (16%)
  Pallas kernels  15.4 us (15%)
    pallas_call x8, Pallas kernels, kernel_call(): pl.pallas_call(body, out_shape=tuple((f32(*shape) for shape, _ in outs)),...  15.4 us
    all_to_all x1, blocking collectives, per_device(): parts = lax.all_to_all(gram, 'y', 0, 0)  14.8 us
    ppermute x3, starting transfers between devices, across(): return lax.ppermute(value, 'y', pairs + [(b, a) for a, b in pairs])  12.9 us
    all_to_all x2, starting transfers between devices, per_device(): pieces = lax.all_to_all(pieces, 'zh', 0, 0)  12.3 us
    all_to_all x1, blocking collectives, per_device(): gram = lax.all_to_all(gram, ('zl', 'core'), 0, 0)  12 us
    ppermute x3, waiting for transfers between devices, across(): return lax.ppermute(value, 'y', pairs + [(b, a) for a, b in pairs])  8.47 us
    ppermute x1, starting transfers between devices, per_device(): feat = feat + lax.ppermute(feat, 'core', SWAP)  7.48 us
    all_to_all x1, starting transfers between devices, per_device(): arrived = lax.all_to_all(start.reshape(4, 16, width), 'x', 0, 0)  4.84 us
  transfers between devices with their start and end apart: 9, of which 8 were waited for; matrix products, arithmetic and copies ran while one was open for 0% of the time, Pallas kernels for 7%

profile of v4, /device:TPU:1, one launch (start us, length us, event | category | flops | bytes accessed | tf_op | source)
XLA Modules:
  0.0 102.4 jit_solution(7272995551514518632)
XLA Ops:
  0.0 4.8 %all-to-all-start = ((f32[4,16,4096]{2,1,0:T(8,128)}), f32[4,16,4096]{2,1,0:T(8,128)S(1)}, u32[]{:S(2)}, u32[]{:S(2)}) async-start(f32[4,16,4096]{2,1,0:T(8,128)} %bitcast.6), calls=%async_computation | async-start | bytes 2097152 | tf_op jit(solution)/shard_map/all_to_all | solution.py:283
  4.8 3.3 %shard_map.28 = f32[256,128]{1,0:T(8,128)S(1)} custom-call(f32[64,4096]{1,0:T(8,128)} %bitcast.7, bf16[2,128,4096]{2,1,0:T(8,128)(2,1)} %bitcast.9), custom_call_target="tpu_custom_call" | custom-call | flops 734003200 | bytes 8388608 | tf_op jit(solution)/shard_map/pallas_call | solution.py:59
  8.1 7.5 %collective-permute-start = (f32[256,128]{1,0:T(8,128)S(1)}, f32[256,128]{1,0:T(8,128)S(1)}, u32[]{:S(2)}, u32[]{:S(2)}) collective-permute-start(f32[256,128]{1,0:T(8,128)S(1)} %shard_map.28), channel_id=1, source_target_pairs={{0,1},{1,0},{2,3},{3,2},{4,5},{5,4},{6,7},{7,6},{8,9},{9,8},{10,11... | collective-permute-start | bytes 393224 | tf_op jit(solution)/shard_map/ppermute | solution.py:294
  15.6 1.0 collective-permute-done
  16.6 1.9 %collective-permute-start.1 = (f32[256,128]{1,0:T(8,128)S(1)}, f32[256,128]{1,0:T(8,128)S(1)}, u32[]{:S(2)}, u32[]{:S(2)}) collective-permute-start(f32[256,128]{1,0:T(8,128)S(1)} %add.3.feat_ref), channel_id=1, source_target_pairs={{0,16},{16,0},{1,17},{17,1},{2,18},{18,2},{3,19},{19,3},{4,20},{20... | collective-permute-start | bytes 393224 | tf_op jit(solution)/shard_map/ppermute | solution.py:299
  18.5 4.7 %collective-permute-done.1.other_ref = f32[256,128]{1,0:T(8,128)S(1)} collective-permute-done((f32[256,128]{1,0:T(8,128)S(1)}, f32[256,128]{1,0:T(8,128)S(1)}, u32[]{:S(2)}, u32[]{:S(2)}) %collective-permute-start.1) | collective-permute-done | bytes 131104 | tf_op jit(solution)/shard_map/ppermute | solution.py:299
  23.2 0.0 all-to-all-done.received_ref
  23.2 0.7 shard_map.29
  24.0 5.8 %all-to-all-start.1 = ((f32[4,16,1024]{2,1,0:T(8,128)}), f32[4,16,1024]{2,1,0:T(8,128)S(1)}, u32[]{:S(2)}, u32[]{:S(2)}) async-start(f32[4,16,1024]{2,1,0:T(8,128)} %get-tuple-element.13), calls=%async_computation.1 | async-start | bytes 524288 | tf_op jit(solution)/shard_map/all_to_all | solution.py:304
  29.8 5.2 %collective-permute-start.2 = (f32[256,128]{1,0:T(8,128)S(1)}, f32[256,128]{1,0:T(8,128)S(1)}, u32[]{:S(2)}, u32[]{:S(2)}) collective-permute-start(f32[256,128]{1,0:T(8,128)S(1)} %get-tuple-element.14.feat_ref), channel_id=1, source_target_pairs={{2,12},{4,10},{0,6},{8,14},{12,2},{10,4},{6,0},{14,8},{3,13},{5,11... | collective-permute-start | bytes 393224 | tf_op jit(solution)/shard_map/ppermute | solution.py:270
  35.0 3.3 %collective-permute-done.2.other_ref = f32[256,128]{1,0:T(8,128)S(1)} collective-permute-done((f32[256,128]{1,0:T(8,128)S(1)}, f32[256,128]{1,0:T(8,128)S(1)}, u32[]{:S(2)}, u32[]{:S(2)}) %collective-permute-start.2) | collective-permute-done | bytes 131104 | tf_op jit(solution)/shard_map/ppermute | solution.py:270
  38.3 0.2 all-to-all-done.1.received_ref
  38.5 0.7 shard_map.30
  39.3 6.4 %all-to-all-start.2 = ((f32[4,16,1024]{2,1,0:T(8,128)}), f32[4,16,1024]{2,1,0:T(8,128)S(1)}, u32[]{:S(2)}, u32[]{:S(2)}) async-start(f32[4,16,1024]{2,1,0:T(8,128)} %get-tuple-element.15), calls=%async_computation.2 | async-start | bytes 524288 | tf_op jit(solution)/shard_map/all_to_all | solution.py:314
  45.7 4.1 %collective-permute-start.3 = (f32[256,128]{1,0:T(8,128)S(1)}, f32[256,128]{1,0:T(8,128)S(1)}, u32[]{:S(2)}, u32[]{:S(2)}) collective-permute-start(f32[256,128]{1,0:T(8,128)S(1)} %get-tuple-element.16.feat_ref), channel_id=1, source_target_pairs={{2,4},{6,8},{10,12},{14,0},{4,2},{8,6},{12,10},{0,14},{3,5},{7,9},... | collective-permute-start | bytes 393224 | tf_op jit(solution)/shard_map/ppermute | solution.py:270
  49.8 2.8 %collective-permute-done.3.other_ref = f32[256,128]{1,0:T(8,128)S(1)} collective-permute-done((f32[256,128]{1,0:T(8,128)S(1)}, f32[256,128]{1,0:T(8,128)S(1)}, u32[]{:S(2)}, u32[]{:S(2)}) %collective-permute-start.3) | collective-permute-done | bytes 131104 | tf_op jit(solution)/shard_map/ppermute | solution.py:270
  52.6 1.7 %all-to-all-done.2.received_ref = f32[4,16,1024]{2,1,0:T(8,128)S(1)} async-done(((f32[4,16,1024]{2,1,0:T(8,128)}), f32[4,16,1024]{2,1,0:T(8,128)S(1)}, u32[]{:S(2)}, u32[]{:S(2)}) %all-to-all-start.2) | async-done | bytes 262176 | tf_op jit(solution)/shard_map/all_to_all | solution.py:314
  54.4 1.1 %shard_map.31 = (f32[4,16,4096]{2,1,0:T(8,128)}, f32[256,128]{1,0:T(8,128)S(1)}) custom-call(f32[4,16,1024]{2,1,0:T(8,128)S(1)} %all-to-all-done.2.received_ref, f32[256,128]{1,0:T(8,128)S(1)} %get-tuple-element.16.feat_ref, f32[256,128]{1,0:T(8,128)S(1)} %collective-permute-done.3.other_ref), custom_call_target="tpu_custom_call" | custom-call | flops 1048576 | bytes 2097152 | tf_op jit(solution)/shard_map/pallas_call | solution.py:59
  55.5 4.2 %all-to-all-start.3 = ((f32[4,16,4096]{2,1,0:T(8,128)}), f32[4,16,4096]{2,1,0:T(8,128)S(1)}, u32[]{:S(2)}, u32[]{:S(2)}) async-start(f32[4,16,4096]{2,1,0:T(8,128)} %get-tuple-element.17), calls=%async_computation.3 | async-start | bytes 2097152 | tf_op jit(solution)/shard_map/all_to_all | solution.py:325
  59.7 3.6 %collective-permute-start.4 = (f32[256,128]{1,0:T(8,128)S(1)}, f32[256,128]{1,0:T(8,128)S(1)}, u32[]{:S(2)}, u32[]{:S(2)}) collective-permute-start(f32[256,128]{1,0:T(8,128)S(1)} %get-tuple-element.18.feat_ref), channel_id=1, source_target_pairs={{0,2},{4,6},{8,10},{12,14},{2,0},{6,4},{10,8},{14,12},{1,3},{5,7},... | collective-permute-start | bytes 393224 | tf_op jit(solution)/shard_map/ppermute | solution.py:270
  63.3 2.3 %collective-permute-done.4.other_ref = f32[256,128]{1,0:T(8,128)S(1)} collective-permute-done((f32[256,128]{1,0:T(8,128)S(1)}, f32[256,128]{1,0:T(8,128)S(1)}, u32[]{:S(2)}, u32[]{:S(2)}) %collective-permute-start.4) | collective-permute-done | bytes 131104 | tf_op jit(solution)/shard_map/ppermute | solution.py:270
  65.6 3.6 %shard_map.32.delta_ref = f32[64,4096]{1,0:T(8,128)} custom-call(f32[256,128]{1,0:T(8,128)S(1)} %get-tuple-element.18.feat_ref, f32[256,128]{1,0:T(8,128)S(1)} %collective-permute-done.4.other_ref, f32[64,4096]{1,0:T(8,128)} %bitcast.8, bf16[2,128,4096]{2,1,0:T(8,128)(2,1)} %bitcast.10), custom_call_target="tpu_custom_call" | custom-call | flops 734003200 | bytes 8388608 | tf_op jit(solution)/shard_map/pallas_call | solution.py:59
  69.2 0.3 all-to-all-done.3
  69.4 2.5 %shard_map.33 = (f32[64,4096]{1,0:T(8,128)S(1)}, f32[4,24,128]{2,1,0:T(8,128)S(1)}) custom-call(f32[64,4096]{1,0:T(8,128)S(1)} %bitcast.5, f32[64,4096]{1,0:T(8,128)} %shard_map.32.delta_ref), custom_call_target="tpu_custom_call" | custom-call | flops 419430400 | bytes 3145728 | tf_op jit(solution)/shard_map/pallas_call | solution.py:59
  72.0 12.0 %all_to_all.30.parts_ref = f32[4,24,128]{2,1,0:T(8,128)S(1)} all-to-all(f32[4,24,128]{2,1,0:T(8,128)S(1)} %get-tuple-element.19), channel_id=1, replica_groups=mesh['x'=4,'zh'=4,'zl'=2,'y'=8,'core'=2] {'zl','core'}, dimensions={0} | all-to-all | bytes 98304 | tf_op jit(solution)/shard_map/all_to_all | solution.py:348
  84.0 14.8 %all_to_all.31.parts_ref = f32[8,24,128]{2,1,0:T(8,128)S(1)} all-to-all(f32[8,24,128]{2,1,0:T(8,128)S(1)} %shard_map.34), channel_id=1, replica_groups=mesh['x'=4,'zh'=4,'zl'=2,'y'=8,'core'=2] {'y'}, dimensions={0} | all-to-all | bytes 196608 | tf_op jit(solution)/shard_map/all_to_all | solution.py:350
  98.9 3.5 %shard_map.35 = f32[64,4096]{1,0:T(8,128)} custom-call(f32[8,24,128]{2,1,0:T(8,128)S(1)} %all_to_all.31.parts_ref, f32[64,4096]{1,0:T(8,128)S(1)} %get-tuple-element.20.mixed_ref), custom_call_target="tpu_custom_call" | custom-call | flops 419430400 | bytes 3145728 | tf_op jit(solution)/shard_map/pallas_call | solution.py:59
  (2 shorter events, 0.0 us)
Async XLA Ops:
  0.0 23.2 %all-to-all-start = ((f32[4,16,4096]{2,1,0:T(8,128)}), f32[4,16,4096]{2,1,0:T(8,128)S(1)}, u32[]{:S(2)}, u32[]{:S(2)}) async-start(f32[4,16,4096]{2,1,0:T(8,128)} %bitcast.6), calls=%async_computation | async-start | bytes 2097152 | tf_op jit(solution)/shard_map/all_to_all | solution.py:283
  8.1 8.4 %collective-permute-start = (f32[256,128]{1,0:T(8,128)S(1)}, f32[256,128]{1,0:T(8,128)S(1)}, u32[]{:S(2)}, u32[]{:S(2)}) collective-permute-start(f32[256,128]{1,0:T(8,128)S(1)} %shard_map.28), channel_id=1, source_target_pairs={{0,1},{1,0},{2,3},{3,2},{4,5},{5,4},{6,7},{7,6},{8,9},{9,8},{10,11... | collective-permute-start | bytes 393224 | tf_op jit(solution)/shard_map/ppermute | solution.py:294
  16.6 6.6 %collective-permute-start.1 = (f32[256,128]{1,0:T(8,128)S(1)}, f32[256,128]{1,0:T(8,128)S(1)}, u32[]{:S(2)}, u32[]{:S(2)}) collective-permute-start(f32[256,128]{1,0:T(8,128)S(1)} %add.3.feat_ref), channel_id=1, source_target_pairs={{0,16},{16,0},{1,17},{17,1},{2,18},{18,2},{3,19},{19,3},{4,20},{20... | collective-permute-start | bytes 393224 | tf_op jit(solution)/shard_map/ppermute | solution.py:299
  24.0 14.6 %all-to-all-start.1 = ((f32[4,16,1024]{2,1,0:T(8,128)}), f32[4,16,1024]{2,1,0:T(8,128)S(1)}, u32[]{:S(2)}, u32[]{:S(2)}) async-start(f32[4,16,1024]{2,1,0:T(8,128)} %get-tuple-element.13), calls=%async_computation.1 | async-start | bytes 524288 | tf_op jit(solution)/shard_map/all_to_all | solution.py:304
  29.8 8.5 %collective-permute-start.2 = (f32[256,128]{1,0:T(8,128)S(1)}, f32[256,128]{1,0:T(8,128)S(1)}, u32[]{:S(2)}, u32[]{:S(2)}) collective-permute-start(f32[256,128]{1,0:T(8,128)S(1)} %get-tuple-element.14.feat_ref), channel_id=1, source_target_pairs={{2,12},{4,10},{0,6},{8,14},{12,2},{10,4},{6,0},{14,8},{3,13},{5,11... | collective-permute-start | bytes 393224 | tf_op jit(solution)/shard_map/ppermute | solution.py:270
  39.3 15.1 %all-to-all-start.2 = ((f32[4,16,1024]{2,1,0:T(8,128)}), f32[4,16,1024]{2,1,0:T(8,128)S(1)}, u32[]{:S(2)}, u32[]{:S(2)}) async-start(f32[4,16,1024]{2,1,0:T(8,128)} %get-tuple-element.15), calls=%async_computation.2 | async-start | bytes 524288 | tf_op jit(solution)/shard_map/all_to_all | solution.py:314
  45.7 6.9 %collective-permute-start.3 = (f32[256,128]{1,0:T(8,128)S(1)}, f32[256,128]{1,0:T(8,128)S(1)}, u32[]{:S(2)}, u32[]{:S(2)}) collective-permute-start(f32[256,128]{1,0:T(8,128)S(1)} %get-tuple-element.16.feat_ref), channel_id=1, source_target_pairs={{2,4},{6,8},{10,12},{14,0},{4,2},{8,6},{12,10},{0,14},{3,5},{7,9},... | collective-permute-start | bytes 393224 | tf_op jit(solution)/shard_map/ppermute | solution.py:270
  55.5 14.0 %all-to-all-start.3 = ((f32[4,16,4096]{2,1,0:T(8,128)}), f32[4,16,4096]{2,1,0:T(8,128)S(1)}, u32[]{:S(2)}, u32[]{:S(2)}) async-start(f32[4,16,4096]{2,1,0:T(8,128)} %get-tuple-element.17), calls=%async_computation.3 | async-start | bytes 2097152 | tf_op jit(solution)/shard_map/all_to_all | solution.py:325
  59.7 6.0 %collective-permute-start.4 = (f32[256,128]{1,0:T(8,128)S(1)}, f32[256,128]{1,0:T(8,128)S(1)}, u32[]{:S(2)}, u32[]{:S(2)}) collective-permute-start(f32[256,128]{1,0:T(8,128)S(1)} %get-tuple-element.18.feat_ref), channel_id=1, source_target_pairs={{0,2},{4,6},{8,10},{12,14},{2,0},{6,4},{10,8},{14,12},{1,3},{5,7},... | collective-permute-start | bytes 393224 | tf_op jit(solution)/shard_map/ppermute | solution.py:270

commit v5 on v4

--- a/solution.py
+++ b/solution.py
@@ -50,8 +50,9 @@
 IN_VMEM = pl.BlockSpec(memory_space=pltpu.VMEM)
 CHUNKS = 4
 LARGE = 55000 << 10
-DELTA_LIMIT = 54500 << 10
-GRAM_LIMIT = 53000 << 10
+FIRST_LIMIT = 53000 << 10
+DELTA_LIMIT = 53000 << 10
+GRAM_LIMIT = 50000 << 10
 FINISH_LIMIT = 53000 << 10
 
 
@@ -81,21 +82,16 @@
     return jax.ShapeDtypeStruct(shape, jnp.float32)
 
 
-def products_kernel(start_ref, stream_ref, out_ref, start_vmem, stream_vmem, sems):
-    width = start_vmem.shape[1] // CHUNKS
+def products_kernel(start_ref, stream_ref, out_ref, stream_vmem, sems):
+    width = start_ref.shape[1] // CHUNKS
     spans = [slice(width * c, width * c + width) for c in range(CHUNKS)]
-    copies = fetch(
-        [(start_ref.at[:, s], start_vmem.at[:, s]) for s in spans]
-        + [(stream_ref.at[:, :, s], stream_vmem.at[:, :, s]) for s in spans],
-        sems,
-    )
+    copies = fetch([(stream_ref.at[:, :, s], stream_vmem.at[:, :, s]) for s in spans], sems)
     both = None
     for c, span in enumerate(spans):
         copies[c].wait()
-        copies[CHUNKS + c].wait()
         first = stream_vmem[0, :, span]
         rows = jnp.concatenate([first, stream_vmem[1, :, span]], axis=0)
-        right = jnp.concatenate(split3(start_vmem[:, span]) + (first,), axis=0)
+        right = jnp.concatenate(split3(start_ref[:, span]) + (first,), axis=0)
         part = dot(rows, right, ON_COLS, None)
         both = part if both is None else both + part
     onto = both[:, :64] + (both[:, 64:128] + both[:, 128:192])
@@ -142,10 +138,10 @@
 
 
 def delta_kernel(
-    feat_ref, other_ref, start_ref, stream_ref, out_ref, start_vmem, stream_vmem, delta, sems, out_sems,
+    feat_ref, other_ref, start_ref, stream_ref, out_ref, start_vmem, stream_vmem, sems,
     *, inv_scale, step_size
 ):
-    width = delta.shape[1] // CHUNKS
+    width = out_ref.shape[1] // CHUNKS
     spans = [slice(width * c, width * c + width) for c in range(CHUNKS)]
     pairs = []
     for span in spans:
@@ -167,34 +163,21 @@
     mix_0 = step_size * (turned0 - step_size * dot(cov1, turned0, PLAIN))
     mix_1 = step_size * proj1.T
     left = jnp.concatenate(split3(jnp.concatenate([mix_0, mix_1], axis=1)), axis=0)
-    copies = []
     for c, span in enumerate(spans):
         arriving[2 * c].wait()
         arriving[2 * c + 1].wait()
         rows = jnp.concatenate([stream_vmem[0, :, span], stream_vmem[1, :, span]], axis=0)
         three = dot(left, rows, PLAIN, None)
-        delta[:, span] = exact_dot(mix_b, start_vmem[:, span]) + (
+        out_ref[:, span] = exact_dot(mix_b, start_vmem[:, span]) + (
             three[:64] + (three[64:128] + three[128:])
         )
-        copy = pltpu.make_async_copy(delta.at[:, span], out_ref.at[:, span], out_sems.at[c])
-        copy.start()
-        copies.append(copy)
-    for copy in copies:
-        copy.wait()
-
-
-def gram_kernel(average_ref, delta_ref, mixed_ref, gram_ref, delta, sems):
-    width = delta.shape[1] // CHUNKS
-    spans = [slice(width * c, width * c + width) for c in range(CHUNKS)]
-    copies = fetch([(delta_ref.at[:, s], delta.at[:, s]) for s in spans], sems)
-    both = None
-    for copy, span in zip(copies, spans):
-        copy.wait()
-        mixed = average_ref[:, span] + delta[:, span]
-        mixed_ref[:, span] = mixed
-        stacked = jnp.concatenate(split3(mixed), axis=0)
-        part = dot(stacked, stacked, ON_COLS, None)
-        both = part if both is None else both + part
+
+
+def gram_kernel(average_ref, delta_ref, mixed_ref, gram_ref):
+    mixed = average_ref[...] + delta_ref[...]
+    mixed_ref[...] = mixed
+    stacked = jnp.concatenate(split3(mixed), axis=0)
+    both = dot(stacked, stacked, ON_COLS, None)
     high_mid = both[:64, 64:128]
     high_low = both[:64, 128:192]
     small = both[64:128, 64:128] + (high_low + both[128:192, :64])
@@ -283,13 +266,13 @@
     arrived = lax.all_to_all(start.reshape(4, 16, width), "x", 0, 0)
     (feat,) = kernel_call(
         products_kernel,
-        (IN_HBM, IN_HBM),
+        (IN_VMEM, IN_HBM),
         [((256, 128), IN_VMEM)],
         (start, batches),
         700 * mega,
         8 * mega,
-        (held_start, held_stream, dma((2 * CHUNKS,))),
-        LARGE,
+        (held_stream, dma((CHUNKS,))),
+        FIRST_LIMIT,
     )
     feat = feat + lax.ppermute(feat, "core", SWAP)
     pieces, feat = kernel_call(
@@ -328,21 +311,21 @@
             delta_kernel, inv_scale=total_feat**-0.5, step_size=LEARN_RATE / batches.shape[1]
         ),
         (IN_VMEM, IN_VMEM, IN_HBM, IN_HBM),
-        [((rank, width), IN_HBM)],
+        [((rank, width), IN_VMEM)],
         (feat, across(feat, PAIRS[2]), start, batches),
         700 * mega,
         8 * mega,
-        (held_start, held_stream, held_start, dma((2 * CHUNKS,)), dma((CHUNKS,))),
+        (held_start, held_stream, dma((2 * CHUNKS,))),
         DELTA_LIMIT,
     )
     mixed, gram = kernel_call(
         gram_kernel,
-        (IN_VMEM, IN_HBM),
+        (IN_VMEM, IN_VMEM),
         [((rank, width), IN_VMEM), ((4, 24, 128), IN_VMEM)],
         (average, delta),
         400 * mega,
         3 * mega,
-        (held_start, dma((CHUNKS,))),
+        (),
         GRAM_LIMIT,
     )
     gram = lax.all_to_all(gram, ("zl", "core"), 0, 0)

time: 104 us -> 101 us (0.971); the launches traced: 102 us -> 100 us
  Pallas kernels: 15.4 us -> 12.7 us
    pallas_call x8, Pallas kernels: 15.4 us -> 12.7 us  [kernel_call(): pl.pallas_call(body, out_shape=tuple((f32(*shape) for shape, _ in outs)),...]
  transfers between devices with their start and end apart: 9 -> 9, of which waited for: 8 -> 8; matrix products, arithmetic and copies ran while one was open for 0% -> 0% of each run, Pallas kernels for 7% -> 6%
where the time goes in v5:
time: 101 us; the launch traced here: 100 us
  starting transfers between devices  43.7 us (43%)
  blocking collectives  26.9 us (27%)
  waiting for transfers between devices  17.1 us (17%)
  Pallas kernels  12.7 us (13%)
    all_to_all x1, blocking collectives, per_device(): parts = lax.all_to_all(gram, 'y', 0, 0)  14.9 us
    ppermute x3, starting transfers between devices, across(): return lax.ppermute(value, 'y', pairs + [(b, a) for a, b in pairs])  12.9 us
    pallas_call x8, Pallas kernels, kernel_call(): pl.pallas_call(body, out_shape=tuple((f32(*shape) for shape, _ in outs)),...  12.7 us
    all_to_all x2, starting transfers between devices, per_device(): pieces = lax.all_to_all(pieces, 'zh', 0, 0)  12.6 us
    all_to_all x1, blocking collectives, per_device(): gram = lax.all_to_all(gram, ('zl', 'core'), 0, 0)  12 us
    ppermute x3, waiting for transfers between devices, across(): return lax.ppermute(value, 'y', pairs + [(b, a) for a, b in pairs])  8.47 us
    ppermute x1, starting transfers between devices, per_device(): feat = feat + lax.ppermute(feat, 'core', SWAP)  7.48 us
    all_to_all x1, starting transfers between devices, per_device(): arrived = lax.all_to_all(start.reshape(4, 16, width), 'x', 0, 0)  4.97 us
  transfers between devices with their start and end apart: 9, of which 8 were waited for; matrix products, arithmetic and copies ran while one was open for 0% of the time, Pallas kernels for 6%

profile of v5, /device:TPU:1, one launch (start us, length us, event | category | flops | bytes accessed | tf_op | source)
XLA Modules:
  0.0 100.5 jit_solution(5579851697512124789)
XLA Ops:
  0.0 0.0 copy-start
  0.0 5.0 %all-to-all-start = ((f32[4,16,4096]{2,1,0:T(8,128)}), f32[4,16,4096]{2,1,0:T(8,128)S(1)}, u32[]{:S(2)}, u32[]{:S(2)}) async-start(f32[4,16,4096]{2,1,0:T(8,128)} %bitcast.5), calls=%async_computation | async-start | bytes 2097152 | tf_op jit(solution)/shard_map/all_to_all | solution.py:266
  5.0 0.0 copy-done
  5.0 2.9 %shard_map.28 = f32[256,128]{1,0:T(8,128)S(1)} custom-call(f32[64,4096]{1,0:T(8,128)S(1)} %bitcast.7, bf16[2,128,4096]{2,1,0:T(8,128)(2,1)} %bitcast.9), custom_call_target="tpu_custom_call" | custom-call | flops 734003200 | bytes 8388608 | tf_op jit(solution)/shard_map/pallas_call | solution.py:60
  7.9 7.5 %collective-permute-start = (f32[256,128]{1,0:T(8,128)S(1)}, f32[256,128]{1,0:T(8,128)S(1)}, u32[]{:S(2)}, u32[]{:S(2)}) collective-permute-start(f32[256,128]{1,0:T(8,128)S(1)} %shard_map.28), channel_id=1, source_target_pairs={{0,1},{1,0},{2,3},{3,2},{4,5},{5,4},{6,7},{7,6},{8,9},{9,8},{10,11... | collective-permute-start | bytes 393224 | tf_op jit(solution)/shard_map/ppermute | solution.py:277
  15.4 1.0 collective-permute-done
  16.4 1.9 %collective-permute-start.1 = (f32[256,128]{1,0:T(8,128)S(1)}, f32[256,128]{1,0:T(8,128)S(1)}, u32[]{:S(2)}, u32[]{:S(2)}) collective-permute-start(f32[256,128]{1,0:T(8,128)S(1)} %add.3.feat_ref), channel_id=1, source_target_pairs={{0,16},{16,0},{1,17},{17,1},{2,18},{18,2},{3,19},{19,3},{4,20},{20... | collective-permute-start | bytes 393224 | tf_op jit(solution)/shard_map/ppermute | solution.py:282
  18.3 4.7 %collective-permute-done.1.other_ref = f32[256,128]{1,0:T(8,128)S(1)} collective-permute-done((f32[256,128]{1,0:T(8,128)S(1)}, f32[256,128]{1,0:T(8,128)S(1)}, u32[]{:S(2)}, u32[]{:S(2)}) %collective-permute-start.1) | collective-permute-done | bytes 131104 | tf_op jit(solution)/shard_map/ppermute | solution.py:282
  23.0 0.0 all-to-all-done.received_ref
  23.0 0.7 shard_map.29
  23.8 6.2 %all-to-all-start.1 = ((f32[4,16,1024]{2,1,0:T(8,128)}), f32[4,16,1024]{2,1,0:T(8,128)S(1)}, u32[]{:S(2)}, u32[]{:S(2)}) async-start(f32[4,16,1024]{2,1,0:T(8,128)} %get-tuple-element.13), calls=%async_computation.1 | async-start | bytes 524288 | tf_op jit(solution)/shard_map/all_to_all | solution.py:287
  29.9 5.2 %collective-permute-start.2 = (f32[256,128]{1,0:T(8,128)S(1)}, f32[256,128]{1,0:T(8,128)S(1)}, u32[]{:S(2)}, u32[]{:S(2)}) collective-permute-start(f32[256,128]{1,0:T(8,128)S(1)} %get-tuple-element.14.feat_ref), channel_id=1, source_target_pairs={{2,12},{4,10},{0,6},{8,14},{12,2},{10,4},{6,0},{14,8},{3,13},{5,11... | collective-permute-start | bytes 393224 | tf_op jit(solution)/shard_map/ppermute | solution.py:253
  35.2 3.3 %collective-permute-done.2.other_ref = f32[256,128]{1,0:T(8,128)S(1)} collective-permute-done((f32[256,128]{1,0:T(8,128)S(1)}, f32[256,128]{1,0:T(8,128)S(1)}, u32[]{:S(2)}, u32[]{:S(2)}) %collective-permute-start.2) | collective-permute-done | bytes 131104 | tf_op jit(solution)/shard_map/ppermute | solution.py:253
  38.5 0.2 all-to-all-done.1.received_ref
  38.7 0.7 shard_map.30
  39.4 6.4 %all-to-all-start.2 = ((f32[4,16,1024]{2,1,0:T(8,128)}), f32[4,16,1024]{2,1,0:T(8,128)S(1)}, u32[]{:S(2)}, u32[]{:S(2)}) async-start(f32[4,16,1024]{2,1,0:T(8,128)} %get-tuple-element.15), calls=%async_computation.2 | async-start | bytes 524288 | tf_op jit(solution)/shard_map/all_to_all | solution.py:297
  45.9 4.1 %collective-permute-start.3 = (f32[256,128]{1,0:T(8,128)S(1)}, f32[256,128]{1,0:T(8,128)S(1)}, u32[]{:S(2)}, u32[]{:S(2)}) collective-permute-start(f32[256,128]{1,0:T(8,128)S(1)} %get-tuple-element.16.feat_ref), channel_id=1, source_target_pairs={{2,4},{6,8},{10,12},{14,0},{4,2},{8,6},{12,10},{0,14},{3,5},{7,9},... | collective-permute-start | bytes 393224 | tf_op jit(solution)/shard_map/ppermute | solution.py:253
  49.9 2.8 %collective-permute-done.3.other_ref = f32[256,128]{1,0:T(8,128)S(1)} collective-permute-done((f32[256,128]{1,0:T(8,128)S(1)}, f32[256,128]{1,0:T(8,128)S(1)}, u32[]{:S(2)}, u32[]{:S(2)}) %collective-permute-start.3) | collective-permute-done | bytes 131104 | tf_op jit(solution)/shard_map/ppermute | solution.py:253
  52.8 1.7 %all-to-all-done.2.received_ref = f32[4,16,1024]{2,1,0:T(8,128)S(1)} async-done(((f32[4,16,1024]{2,1,0:T(8,128)}), f32[4,16,1024]{2,1,0:T(8,128)S(1)}, u32[]{:S(2)}, u32[]{:S(2)}) %all-to-all-start.2) | async-done | bytes 262176 | tf_op jit(solution)/shard_map/all_to_all | solution.py:297
  54.5 1.1 %shard_map.31 = (f32[4,16,4096]{2,1,0:T(8,128)}, f32[256,128]{1,0:T(8,128)S(1)}) custom-call(f32[4,16,1024]{2,1,0:T(8,128)S(1)} %all-to-all-done.2.received_ref, f32[256,128]{1,0:T(8,128)S(1)} %get-tuple-element.16.feat_ref, f32[256,128]{1,0:T(8,128)S(1)} %collective-permute-done.3.other_ref), custom_call_target="tpu_custom_call" | custom-call | flops 1048576 | bytes 2097152 | tf_op jit(solution)/shard_map/pallas_call | solution.py:60
  55.6 3.9 %all-to-all-start.3 = ((f32[4,16,4096]{2,1,0:T(8,128)}), f32[4,16,4096]{2,1,0:T(8,128)S(1)}, u32[]{:S(2)}, u32[]{:S(2)}) async-start(f32[4,16,4096]{2,1,0:T(8,128)} %get-tuple-element.17), calls=%async_computation.3 | async-start | bytes 2097152 | tf_op jit(solution)/shard_map/all_to_all | solution.py:308
  59.5 3.6 %collective-permute-start.4 = (f32[256,128]{1,0:T(8,128)S(1)}, f32[256,128]{1,0:T(8,128)S(1)}, u32[]{:S(2)}, u32[]{:S(2)}) collective-permute-start(f32[256,128]{1,0:T(8,128)S(1)} %get-tuple-element.18.feat_ref), channel_id=1, source_target_pairs={{0,2},{4,6},{8,10},{12,14},{2,0},{6,4},{10,8},{14,12},{1,3},{5,7},... | collective-permute-start | bytes 393224 | tf_op jit(solution)/shard_map/ppermute | solution.py:253
  63.1 2.3 %collective-permute-done.4.other_ref = f32[256,128]{1,0:T(8,128)S(1)} collective-permute-done((f32[256,128]{1,0:T(8,128)S(1)}, f32[256,128]{1,0:T(8,128)S(1)}, u32[]{:S(2)}, u32[]{:S(2)}) %collective-permute-start.4) | collective-permute-done | bytes 131104 | tf_op jit(solution)/shard_map/ppermute | solution.py:253
  65.4 2.8 %shard_map.32.delta_ref = f32[64,4096]{1,0:T(8,128)S(1)} custom-call(f32[256,128]{1,0:T(8,128)S(1)} %get-tuple-element.18.feat_ref, f32[256,128]{1,0:T(8,128)S(1)} %collective-permute-done.4.other_ref, f32[64,4096]{1,0:T(8,128)} %bitcast.6, bf16[2,128,4096]{2,1,0:T(8,128)(2,1)} %bitcast.10), custom_call_target="tpu_custom_call" | custom-call | flops 734003200 | bytes 8388608 | tf_op jit(solution)/shard_map/pallas_call | solution.py:60
  68.2 1.0 %all-to-all-done.3 = f32[4,16,4096]{2,1,0:T(8,128)S(1)} async-done(((f32[4,16,4096]{2,1,0:T(8,128)}), f32[4,16,4096]{2,1,0:T(8,128)S(1)}, u32[]{:S(2)}, u32[]{:S(2)}) %all-to-all-start.3) | async-done | bytes 1048608 | tf_op jit(solution)/shard_map/all_to_all | solution.py:308
  69.2 0.9 shard_map.33
  70.1 12.0 %all_to_all.30.parts_ref = f32[4,24,128]{2,1,0:T(8,128)S(1)} all-to-all(f32[4,24,128]{2,1,0:T(8,128)S(1)} %get-tuple-element.19), channel_id=1, replica_groups=mesh['x'=4,'zh'=4,'zl'=2,'y'=8,'core'=2] {'zl','core'}, dimensions={0} | all-to-all | bytes 98304 | tf_op jit(solution)/shard_map/all_to_all | solution.py:331
  82.1 14.9 %all_to_all.31.parts_ref = f32[8,24,128]{2,1,0:T(8,128)S(1)} all-to-all(f32[8,24,128]{2,1,0:T(8,128)S(1)} %shard_map.34), channel_id=1, replica_groups=mesh['x'=4,'zh'=4,'zl'=2,'y'=8,'core'=2] {'y'}, dimensions={0} | all-to-all | bytes 196608 | tf_op jit(solution)/shard_map/all_to_all | solution.py:333
  97.0 3.5 %shard_map.35 = f32[64,4096]{1,0:T(8,128)} custom-call(f32[8,24,128]{2,1,0:T(8,128)S(1)} %all_to_all.31.parts_ref, f32[64,4096]{1,0:T(8,128)S(1)} %get-tuple-element.20.mixed_ref), custom_call_target="tpu_custom_call" | custom-call | flops 419430400 | bytes 3145728 | tf_op jit(solution)/shard_map/pallas_call | solution.py:60
  (2 shorter events, 0.0 us)
Async XLA Ops:
  0.0 5.0 %copy-start = (f32[1,64,4096]{2,1,0:T(8,128)S(1)}, f32[1,64,4096]{2,1,0:T(8,128)}, u32[]{:S(2)}) copy-start(f32[1,64,4096]{2,1,0:T(8,128)} %param.2) | copy-start | bytes 3145732
  0.0 23.0 %all-to-all-start = ((f32[4,16,4096]{2,1,0:T(8,128)}), f32[4,16,4096]{2,1,0:T(8,128)S(1)}, u32[]{:S(2)}, u32[]{:S(2)}) async-start(f32[4,16,4096]{2,1,0:T(8,128)} %bitcast.5), calls=%async_computation | async-start | bytes 2097152 | tf_op jit(solution)/shard_map/all_to_all | solution.py:266
  7.9 8.5 %collective-permute-start = (f32[256,128]{1,0:T(8,128)S(1)}, f32[256,128]{1,0:T(8,128)S(1)}, u32[]{:S(2)}, u32[]{:S(2)}) collective-permute-start(f32[256,128]{1,0:T(8,128)S(1)} %shard_map.28), channel_id=1, source_target_pairs={{0,1},{1,0},{2,3},{3,2},{4,5},{5,4},{6,7},{7,6},{8,9},{9,8},{10,11... | collective-permute-start | bytes 393224 | tf_op jit(solution)/shard_map/ppermute | solution.py:277
  16.4 6.6 %collective-permute-start.1 = (f32[256,128]{1,0:T(8,128)S(1)}, f32[256,128]{1,0:T(8,128)S(1)}, u32[]{:S(2)}, u32[]{:S(2)}) collective-permute-start(f32[256,128]{1,0:T(8,128)S(1)} %add.3.feat_ref), channel_id=1, source_target_pairs={{0,16},{16,0},{1,17},{17,1},{2,18},{18,2},{3,19},{19,3},{4,20},{20... | collective-permute-start | bytes 393224 | tf_op jit(solution)/shard_map/ppermute | solution.py:282
  23.8 14.9 %all-to-all-start.1 = ((f32[4,16,1024]{2,1,0:T(8,128)}), f32[4,16,1024]{2,1,0:T(8,128)S(1)}, u32[]{:S(2)}, u32[]{:S(2)}) async-start(f32[4,16,1024]{2,1,0:T(8,128)} %get-tuple-element.13), calls=%async_computation.1 | async-start | bytes 524288 | tf_op jit(solution)/shard_map/all_to_all | solution.py:287
  29.9 8.5 %collective-permute-start.2 = (f32[256,128]{1,0:T(8,128)S(1)}, f32[256,128]{1,0:T(8,128)S(1)}, u32[]{:S(2)}, u32[]{:S(2)}) collective-permute-start(f32[256,128]{1,0:T(8,128)S(1)} %get-tuple-element.14.feat_ref), channel_id=1, source_target_pairs={{2,12},{4,10},{0,6},{8,14},{12,2},{10,4},{6,0},{14,8},{3,13},{5,11... | collective-permute-start | bytes 393224 | tf_op jit(solution)/shard_map/ppermute | solution.py:253
  39.4 15.1 %all-to-all-start.2 = ((f32[4,16,1024]{2,1,0:T(8,128)}), f32[4,16,1024]{2,1,0:T(8,128)S(1)}, u32[]{:S(2)}, u32[]{:S(2)}) async-start(f32[4,16,1024]{2,1,0:T(8,128)} %get-tuple-element.15), calls=%async_computation.2 | async-start | bytes 524288 | tf_op jit(solution)/shard_map/all_to_all | solution.py:297
  45.9 6.9 %collective-permute-start.3 = (f32[256,128]{1,0:T(8,128)S(1)}, f32[256,128]{1,0:T(8,128)S(1)}, u32[]{:S(2)}, u32[]{:S(2)}) collective-permute-start(f32[256,128]{1,0:T(8,128)S(1)} %get-tuple-element.16.feat_ref), channel_id=1, source_target_pairs={{2,4},{6,8},{10,12},{14,0},{4,2},{8,6},{12,10},{0,14},{3,5},{7,9},... | collective-permute-start | bytes 393224 | tf_op jit(solution)/shard_map/ppermute | solution.py:253
  55.6 13.6 %all-to-all-start.3 = ((f32[4,16,4096]{2,1,0:T(8,128)}), f32[4,16,4096]{2,1,0:T(8,128)S(1)}, u32[]{:S(2)}, u32[]{:S(2)}) async-start(f32[4,16,4096]{2,1,0:T(8,128)} %get-tuple-element.17), calls=%async_computation.3 | async-start | bytes 2097152 | tf_op jit(solution)/shard_map/all_to_all | solution.py:308
  59.5 5.9 %collective-permute-start.4 = (f32[256,128]{1,0:T(8,128)S(1)}, f32[256,128]{1,0:T(8,128)S(1)}, u32[]{:S(2)}, u32[]{:S(2)}) collective-permute-start(f32[256,128]{1,0:T(8,128)S(1)} %get-tuple-element.18.feat_ref), channel_id=1, source_target_pairs={{0,2},{4,6},{8,10},{12,14},{2,0},{6,4},{10,8},{14,12},{1,3},{5,7},... | collective-permute-start | bytes 393224 | tf_op jit(solution)/shard_map/ppermute | solution.py:253

commit v6 on v5

--- a/solution.py
+++ b/solution.py
@@ -15,9 +15,9 @@
 HIGHEST = lax.Precision.HIGHEST
 SWAP = [(0, 1), (1, 0)]
 PAIRS = (
+    [(0, 1), (2, 3), (4, 5), (6, 7)],
+    [(1, 2), (3, 4), (5, 6), (7, 0)],
     [(1, 6), (2, 5), (0, 3), (4, 7)],
-    [(1, 2), (3, 4), (5, 6), (7, 0)],
-    [(0, 1), (2, 3), (4, 5), (6, 7)],
 )
 PLAIN = ((1,), (0,))
 ON_ROWS = ((0,), (0,))
@@ -51,7 +51,7 @@
 CHUNKS = 4
 LARGE = 55000 << 10
 FIRST_LIMIT = 53000 << 10
-DELTA_LIMIT = 53000 << 10
+DELTA_LIMIT = 52000 << 10
 GRAM_LIMIT = 50000 << 10
 FINISH_LIMIT = 53000 << 10
 
@@ -124,30 +124,19 @@
 
 
 def unpack_kernel(received_ref, feat_ref, other_ref, out_ref, sum_ref, sems):
-    width = received_ref.shape[2]
-    pairs = []
-    for piece in range(4):
-        for x in range(4):
-            pairs.append(
-                (received_ref.at[piece], out_ref.at[x, :, width * piece : width * piece + width])
-            )
-    copies = fetch(pairs, sems)
+    copies = fetch([(received_ref, out_ref.at[x]) for x in range(4)], sems)
     sum_ref[...] = feat_ref[...] + other_ref[...]
     for copy in copies:
         copy.wait()
 
 
 def delta_kernel(
-    feat_ref, other_ref, start_ref, stream_ref, out_ref, start_vmem, stream_vmem, sems,
+    feat_ref, other_ref, start_ref, stream_ref, out_ref, stream_vmem, sems,
     *, inv_scale, step_size
 ):
     width = out_ref.shape[1] // CHUNKS
     spans = [slice(width * c, width * c + width) for c in range(CHUNKS)]
-    pairs = []
-    for span in spans:
-        pairs.append((start_ref.at[:, span], start_vmem.at[:, span]))
-        pairs.append((stream_ref.at[:, :, span], stream_vmem.at[:, :, span]))
-    arriving = fetch(pairs, sems)
+    arriving = fetch([(stream_ref.at[:, :, s], stream_vmem.at[:, :, s]) for s in spans], sems)
     rank = start_ref.shape[0]
     index = lax.broadcasted_iota(jnp.int32, (rank, rank), 0)
     eye = jnp.where(index == lax.broadcasted_iota(jnp.int32, (rank, rank), 1), 1.0, 0.0)
@@ -162,21 +151,22 @@
     turned0 = proj0.T
     mix_0 = step_size * (turned0 - step_size * dot(cov1, turned0, PLAIN))
     mix_1 = step_size * proj1.T
-    left = jnp.concatenate(split3(jnp.concatenate([mix_0, mix_1], axis=1)), axis=0)
+    left = jnp.concatenate([mix_b, mix_b, mix_b, mix_0, mix_1], axis=1)
+    left = jnp.concatenate(split3(left), axis=0)
     for c, span in enumerate(spans):
-        arriving[2 * c].wait()
-        arriving[2 * c + 1].wait()
-        rows = jnp.concatenate([stream_vmem[0, :, span], stream_vmem[1, :, span]], axis=0)
-        three = dot(left, rows, PLAIN, None)
-        out_ref[:, span] = exact_dot(mix_b, start_vmem[:, span]) + (
-            three[:64] + (three[64:128] + three[128:])
-        )
+        arriving[c].wait()
+        right = split3(start_ref[:, span]) + (stream_vmem[0, :, span], stream_vmem[1, :, span])
+        three = dot(left, jnp.concatenate(right, axis=0), PLAIN, None)
+        out_ref[:, span] = three[:64] + (three[64:128] + three[128:])
 
 
 def gram_kernel(average_ref, delta_ref, mixed_ref, gram_ref):
-    mixed = average_ref[...] + delta_ref[...]
-    mixed_ref[...] = mixed
-    stacked = jnp.concatenate(split3(mixed), axis=0)
+    parts, pieces, rows, width = average_ref.shape
+    for part in range(parts):
+        for piece in range(pieces):
+            place = (slice(rows * part, rows * part + rows), slice(width * piece, width * piece + width))
+            mixed_ref[place] = average_ref[part, piece] + delta_ref[place]
+    stacked = jnp.concatenate(split3(mixed_ref[...]), axis=0)
     both = dot(stacked, stacked, ON_COLS, None)
     high_mid = both[:64, 64:128]
     high_low = both[:64, 128:192]
@@ -298,24 +288,24 @@
     chunk, feat = kernel_call(
         unpack_kernel,
         (IN_VMEM,) * 3,
-        [((4, 16, width), IN_HBM), ((256, 128), IN_VMEM)],
+        [((4,) + quarter, IN_HBM), ((256, 128), IN_VMEM)],
         (pieces, feat, across(feat, PAIRS[1])),
         mega,
         2 * mega,
-        (dma((16,)),),
+        (dma((4,)),),
         53500 << 10,
     )
-    average = lax.all_to_all(chunk, "x", 0, 0).reshape(rank, width)
+    average = lax.all_to_all(chunk, "x", 0, 0)
     (delta,) = kernel_call(
         functools.partial(
             delta_kernel, inv_scale=total_feat**-0.5, step_size=LEARN_RATE / batches.shape[1]
         ),
-        (IN_VMEM, IN_VMEM, IN_HBM, IN_HBM),
+        (IN_VMEM, IN_VMEM, IN_VMEM, IN_HBM),
         [((rank, width), IN_VMEM)],
         (feat, across(feat, PAIRS[2]), start, batches),
         700 * mega,
         8 * mega,
-        (held_start, held_stream, dma((2 * CHUNKS,))),
+        (held_stream, dma((CHUNKS,))),
         DELTA_LIMIT,
     )
     mixed, gram = kernel_call(

time: 101 us -> 100 us (0.990); the launches traced: 100 us -> 98.2 us
  starting transfers between devices: 43.7 us -> 41.9 us
  blocking collectives: 26.9 us -> 25.5 us
    all_to_all x2, starting transfers between devices: 12.6 us -> 10.1 us  [per_device(): pieces = lax.all_to_all(pieces, 'zh', 0, 0)]
    all_to_all x2, waiting for transfers between devices: 1.94 us -> 4.23 us  [per_device(): pieces = lax.all_to_all(pieces, 'zh', 0, 0)]
    all_to_all x1, waiting for transfers between devices: 1.02 us -> 0.01 us  [per_device(): average = lax.all_to_all(chunk, 'x', 0, 0)]
  transfers between devices with their start and end apart: 9 -> 9, of which waited for: 8 -> 7; matrix products, arithmetic and copies ran while one was open for 0% -> 0% of each run, Pallas kernels for 6% -> 6%
where the time goes in v6:
time: 100 us; the launch traced here: 98.2 us
  starting transfers between devices  41.9 us (42%)
  blocking collectives  25.5 us (26%)
  waiting for transfers between devices  18 us (18%)
  Pallas kernels  12.7 us (13%)
    all_to_all x1, blocking collectives, per_device(): parts = lax.all_to_all(gram, 'y', 0, 0)  14.5 us
    ppermute x3, starting transfers between devices, across(): return lax.ppermute(value, 'y', pairs + [(b, a) for a, b in pairs])  13.5 us
    pallas_call x8, Pallas kernels, kernel_call(): pl.pallas_call(body, out_shape=tuple((f32(*shape) for shape, _ in outs)),...  12.7 us
    all_to_all x1, blocking collectives, per_device(): gram = lax.all_to_all(gram, ('zl', 'core'), 0, 0)  11 us
    all_to_all x2, starting transfers between devices, per_device(): pieces = lax.all_to_all(pieces, 'zh', 0, 0)  10.1 us
    ppermute x3, waiting for transfers between devices, across(): return lax.ppermute(value, 'y', pairs + [(b, a) for a, b in pairs])  8.14 us
    ppermute x1, starting transfers between devices, per_device(): feat = feat + lax.ppermute(feat, 'core', SWAP)  7.48 us
    all_to_all x1, starting transfers between devices, per_device(): arrived = lax.all_to_all(start.reshape(4, 16, width), 'x', 0, 0)  4.97 us
  transfers between devices with their start and end apart: 9, of which 7 were waited for; matrix products, arithmetic and copies ran while one was open for 0% of the time, Pallas kernels for 6%

profile of v6, /device:TPU:1, one launch (start us, length us, event | category | flops | bytes accessed | tf_op | source)
XLA Modules:
  0.0 98.2 jit_solution(10853138106806454761)
XLA Ops:
  0.0 0.0 copy-start
  0.0 5.0 %all-to-all-start = ((f32[4,16,4096]{2,1,0:T(8,128)}), f32[4,16,4096]{2,1,0:T(8,128)S(1)}, u32[]{:S(2)}, u32[]{:S(2)}) async-start(f32[4,16,4096]{2,1,0:T(8,128)} %bitcast.4), calls=%async_computation | async-start | bytes 2097152 | tf_op jit(solution)/shard_map/all_to_all | solution.py:256
  5.0 0.0 copy-done
  5.0 2.9 %shard_map.28 = f32[256,128]{1,0:T(8,128)S(1)} custom-call(f32[64,4096]{1,0:T(8,128)S(1)} %bitcast.5, bf16[2,128,4096]{2,1,0:T(8,128)(2,1)} %bitcast.7), custom_call_target="tpu_custom_call" | custom-call | flops 734003200 | bytes 8388608 | tf_op jit(solution)/shard_map/pallas_call | solution.py:60
  7.9 7.5 %collective-permute-start = (f32[256,128]{1,0:T(8,128)S(1)}, f32[256,128]{1,0:T(8,128)S(1)}, u32[]{:S(2)}, u32[]{:S(2)}) collective-permute-start(f32[256,128]{1,0:T(8,128)S(1)} %shard_map.28), channel_id=1, source_target_pairs={{0,1},{1,0},{2,3},{3,2},{4,5},{5,4},{6,7},{7,6},{8,9},{9,8},{10,11... | collective-permute-start | bytes 393224 | tf_op jit(solution)/shard_map/ppermute | solution.py:267
  15.4 1.0 collective-permute-done
  16.4 1.9 %collective-permute-start.1 = (f32[256,128]{1,0:T(8,128)S(1)}, f32[256,128]{1,0:T(8,128)S(1)}, u32[]{:S(2)}, u32[]{:S(2)}) collective-permute-start(f32[256,128]{1,0:T(8,128)S(1)} %add.3.feat_ref), channel_id=1, source_target_pairs={{0,16},{16,0},{1,17},{17,1},{2,18},{18,2},{3,19},{19,3},{4,20},{20... | collective-permute-start | bytes 393224 | tf_op jit(solution)/shard_map/ppermute | solution.py:272
  18.3 4.7 %collective-permute-done.1.other_ref = f32[256,128]{1,0:T(8,128)S(1)} collective-permute-done((f32[256,128]{1,0:T(8,128)S(1)}, f32[256,128]{1,0:T(8,128)S(1)}, u32[]{:S(2)}, u32[]{:S(2)}) %collective-permute-start.1) | collective-permute-done | bytes 131104 | tf_op jit(solution)/shard_map/ppermute | solution.py:272
  23.0 0.0 all-to-all-done.received_ref
  23.0 0.7 shard_map.29
  23.7 6.2 %all-to-all-start.1 = ((f32[4,16,1024]{2,1,0:T(8,128)}), f32[4,16,1024]{2,1,0:T(8,128)S(1)}, u32[]{:S(2)}, u32[]{:S(2)}) async-start(f32[4,16,1024]{2,1,0:T(8,128)} %get-tuple-element.13), calls=%async_computation.1 | async-start | bytes 524288 | tf_op jit(solution)/shard_map/all_to_all | solution.py:277
  29.9 3.2 %collective-permute-start.2 = (f32[256,128]{1,0:T(8,128)S(1)}, f32[256,128]{1,0:T(8,128)S(1)}, u32[]{:S(2)}, u32[]{:S(2)}) collective-permute-start(f32[256,128]{1,0:T(8,128)S(1)} %get-tuple-element.14.feat_ref), channel_id=1, source_target_pairs={{0,2},{4,6},{8,10},{12,14},{2,0},{6,4},{10,8},{14,12},{1,3},{5,7},... | collective-permute-start | bytes 393224 | tf_op jit(solution)/shard_map/ppermute | solution.py:243
  33.1 2.5 %collective-permute-done.2.other_ref = f32[256,128]{1,0:T(8,128)S(1)} collective-permute-done((f32[256,128]{1,0:T(8,128)S(1)}, f32[256,128]{1,0:T(8,128)S(1)}, u32[]{:S(2)}, u32[]{:S(2)}) %collective-permute-start.2) | collective-permute-done | bytes 131104 | tf_op jit(solution)/shard_map/ppermute | solution.py:243
  35.6 3.0 %all-to-all-done.1.received_ref = f32[4,16,1024]{2,1,0:T(8,128)S(1)} async-done(((f32[4,16,1024]{2,1,0:T(8,128)}), f32[4,16,1024]{2,1,0:T(8,128)S(1)}, u32[]{:S(2)}, u32[]{:S(2)}) %all-to-all-start.1) | async-done | bytes 262176 | tf_op jit(solution)/shard_map/all_to_all | solution.py:277
  38.7 0.7 shard_map.30
  39.4 3.9 %all-to-all-start.2 = ((f32[4,16,1024]{2,1,0:T(8,128)}), f32[4,16,1024]{2,1,0:T(8,128)S(1)}, u32[]{:S(2)}, u32[]{:S(2)}) async-start(f32[4,16,1024]{2,1,0:T(8,128)} %get-tuple-element.15), calls=%async_computation.2 | async-start | bytes 524288 | tf_op jit(solution)/shard_map/all_to_all | solution.py:287
  43.3 5.1 %collective-permute-start.3 = (f32[256,128]{1,0:T(8,128)S(1)}, f32[256,128]{1,0:T(8,128)S(1)}, u32[]{:S(2)}, u32[]{:S(2)}) collective-permute-start(f32[256,128]{1,0:T(8,128)S(1)} %get-tuple-element.16.feat_ref), channel_id=1, source_target_pairs={{2,4},{6,8},{10,12},{14,0},{4,2},{8,6},{12,10},{0,14},{3,5},{7,9},... | collective-permute-start | bytes 393224 | tf_op jit(solution)/shard_map/ppermute | solution.py:243
  48.4 2.3 %collective-permute-done.3.other_ref = f32[256,128]{1,0:T(8,128)S(1)} collective-permute-done((f32[256,128]{1,0:T(8,128)S(1)}, f32[256,128]{1,0:T(8,128)S(1)}, u32[]{:S(2)}, u32[]{:S(2)}) %collective-permute-start.3) | collective-permute-done | bytes 131104 | tf_op jit(solution)/shard_map/ppermute | solution.py:243
  50.8 1.2 %all-to-all-done.2.received_ref = f32[4,16,1024]{2,1,0:T(8,128)S(1)} async-done(((f32[4,16,1024]{2,1,0:T(8,128)}), f32[4,16,1024]{2,1,0:T(8,128)S(1)}, u32[]{:S(2)}, u32[]{:S(2)}) %all-to-all-start.2) | async-done | bytes 262176 | tf_op jit(solution)/shard_map/all_to_all | solution.py:287
  52.0 1.0 %shard_map.31 = (f32[4,4,16,1024]{3,2,1,0:T(8,128)}, f32[256,128]{1,0:T(8,128)S(1)}) custom-call(f32[4,16,1024]{2,1,0:T(8,128)S(1)} %all-to-all-done.2.received_ref, f32[256,128]{1,0:T(8,128)S(1)} %get-tuple-element.16.feat_ref, f32[256,128]{1,0:T(8,128)S(1)} %collective-permute-done.3.other_ref), custom_call_target="tpu_custom_call" | custom-call | flops 1048576 | bytes 2097152 | tf_op jit(solution)/shard_map/pallas_call | solution.py:60
  53.0 3.9 %all-to-all-start.3 = ((f32[4,4,16,1024]{3,2,1,0:T(8,128)}), f32[4,4,16,1024]{3,2,1,0:T(8,128)S(1)}, u32[]{:S(2)}, u32[]{:S(2)}) async-start(f32[4,4,16,1024]{3,2,1,0:T(8,128)} %get-tuple-element.17), calls=%async_computation.3 | async-start | bytes 2097152 | tf_op jit(solution)/shard_map/all_to_all | solution.py:298
  56.9 5.2 %collective-permute-start.4 = (f32[256,128]{1,0:T(8,128)S(1)}, f32[256,128]{1,0:T(8,128)S(1)}, u32[]{:S(2)}, u32[]{:S(2)}) collective-permute-start(f32[256,128]{1,0:T(8,128)S(1)} %get-tuple-element.18.feat_ref), channel_id=1, source_target_pairs={{2,12},{4,10},{0,6},{8,14},{12,2},{10,4},{6,0},{14,8},{3,13},{5,11... | collective-permute-start | bytes 393224 | tf_op jit(solution)/shard_map/ppermute | solution.py:243
  62.1 3.3 %collective-permute-done.4.other_ref = f32[256,128]{1,0:T(8,128)S(1)} collective-permute-done((f32[256,128]{1,0:T(8,128)S(1)}, f32[256,128]{1,0:T(8,128)S(1)}, u32[]{:S(2)}, u32[]{:S(2)}) %collective-permute-start.4) | collective-permute-done | bytes 131104 | tf_op jit(solution)/shard_map/ppermute | solution.py:243
  65.4 2.9 %shard_map.32.delta_ref = f32[64,4096]{1,0:T(8,128)S(1)} custom-call(f32[256,128]{1,0:T(8,128)S(1)} %get-tuple-element.18.feat_ref, f32[256,128]{1,0:T(8,128)S(1)} %collective-permute-done.4.other_ref, f32[64,4096]{1,0:T(8,128)S(1)} %bitcast.6, bf16[2,128,4096]{2,1,0:T(8,128)(2,1)} %bitcast.8), custom_call_target="tpu_custom_call" | custom-call | flops 734003200 | bytes 8388608 | tf_op jit(solution)/shard_map/pallas_call | solution.py:60
  68.3 0.0 all-to-all-done.3.average_ref
  68.3 0.9 shard_map.33
  69.2 11.0 %all_to_all.30.parts_ref = f32[4,24,128]{2,1,0:T(8,128)S(1)} all-to-all(f32[4,24,128]{2,1,0:T(8,128)S(1)} %get-tuple-element.19), channel_id=1, replica_groups=mesh['x'=4,'zh'=4,'zl'=2,'y'=8,'core'=2] {'zl','core'}, dimensions={0} | all-to-all | bytes 98304 | tf_op jit(solution)/shard_map/all_to_all | solution.py:321
  80.2 14.5 %all_to_all.31.parts_ref = f32[8,24,128]{2,1,0:T(8,128)S(1)} all-to-all(f32[8,24,128]{2,1,0:T(8,128)S(1)} %shard_map.34), channel_id=1, replica_groups=mesh['x'=4,'zh'=4,'zl'=2,'y'=8,'core'=2] {'y'}, dimensions={0} | all-to-all | bytes 196608 | tf_op jit(solution)/shard_map/all_to_all | solution.py:323
  94.7 3.5 %shard_map.35 = f32[64,4096]{1,0:T(8,128)} custom-call(f32[8,24,128]{2,1,0:T(8,128)S(1)} %all_to_all.31.parts_ref, f32[64,4096]{1,0:T(8,128)S(1)} %get-tuple-element.20.mixed_ref), custom_call_target="tpu_custom_call" | custom-call | flops 419430400 | bytes 3145728 | tf_op jit(solution)/shard_map/pallas_call | solution.py:60
  (2 shorter events, 0.0 us)
Async XLA Ops:
  0.0 5.0 %copy-start = (f32[1,64,4096]{2,1,0:T(8,128)S(1)}, f32[1,64,4096]{2,1,0:T(8,128)}, u32[]{:S(2)}) copy-start(f32[1,64,4096]{2,1,0:T(8,128)} %param.2) | copy-start | bytes 3145732
  0.0 23.0 %all-to-all-start = ((f32[4,16,4096]{2,1,0:T(8,128)}), f32[4,16,4096]{2,1,0:T(8,128)S(1)}, u32[]{:S(2)}, u32[]{:S(2)}) async-start(f32[4,16,4096]{2,1,0:T(8,128)} %bitcast.4), calls=%async_computation | async-start | bytes 2097152 | tf_op jit(solution)/shard_map/all_to_all | solution.py:256
  7.9 8.5 %collective-permute-start = (f32[256,128]{1,0:T(8,128)S(1)}, f32[256,128]{1,0:T(8,128)S(1)}, u32[]{:S(2)}, u32[]{:S(2)}) collective-permute-start(f32[256,128]{1,0:T(8,128)S(1)} %shard_map.28), channel_id=1, source_target_pairs={{0,1},{1,0},{2,3},{3,2},{4,5},{5,4},{6,7},{7,6},{8,9},{9,8},{10,11... | collective-permute-start | bytes 393224 | tf_op jit(solution)/shard_map/ppermute | solution.py:267
  16.4 6.6 %collective-permute-start.1 = (f32[256,128]{1,0:T(8,128)S(1)}, f32[256,128]{1,0:T(8,128)S(1)}, u32[]{:S(2)}, u32[]{:S(2)}) collective-permute-start(f32[256,128]{1,0:T(8,128)S(1)} %add.3.feat_ref), channel_id=1, source_target_pairs={{0,16},{16,0},{1,17},{17,1},{2,18},{18,2},{3,19},{19,3},{4,20},{20... | collective-permute-start | bytes 393224 | tf_op jit(solution)/shard_map/ppermute | solution.py:272
  23.7 14.9 %all-to-all-start.1 = ((f32[4,16,1024]{2,1,0:T(8,128)}), f32[4,16,1024]{2,1,0:T(8,128)S(1)}, u32[]{:S(2)}, u32[]{:S(2)}) async-start(f32[4,16,1024]{2,1,0:T(8,128)} %get-tuple-element.13), calls=%async_computation.1 | async-start | bytes 524288 | tf_op jit(solution)/shard_map/all_to_all | solution.py:277
  29.9 5.7 %collective-permute-start.2 = (f32[256,128]{1,0:T(8,128)S(1)}, f32[256,128]{1,0:T(8,128)S(1)}, u32[]{:S(2)}, u32[]{:S(2)}) collective-permute-start(f32[256,128]{1,0:T(8,128)S(1)} %get-tuple-element.14.feat_ref), channel_id=1, source_target_pairs={{0,2},{4,6},{8,10},{12,14},{2,0},{6,4},{10,8},{14,12},{1,3},{5,7},... | collective-permute-start | bytes 393224 | tf_op jit(solution)/shard_map/ppermute | solution.py:243
  39.4 12.6 %all-to-all-start.2 = ((f32[4,16,1024]{2,1,0:T(8,128)}), f32[4,16,1024]{2,1,0:T(8,128)S(1)}, u32[]{:S(2)}, u32[]{:S(2)}) async-start(f32[4,16,1024]{2,1,0:T(8,128)} %get-tuple-element.15), calls=%async_computation.2 | async-start | bytes 524288 | tf_op jit(solution)/shard_map/all_to_all | solution.py:287
  43.3 7.4 %collective-permute-start.3 = (f32[256,128]{1,0:T(8,128)S(1)}, f32[256,128]{1,0:T(8,128)S(1)}, u32[]{:S(2)}, u32[]{:S(2)}) collective-permute-start(f32[256,128]{1,0:T(8,128)S(1)} %get-tuple-element.16.feat_ref), channel_id=1, source_target_pairs={{2,4},{6,8},{10,12},{14,0},{4,2},{8,6},{12,10},{0,14},{3,5},{7,9},... | collective-permute-start | bytes 393224 | tf_op jit(solution)/shard_map/ppermute | solution.py:243
  53.0 15.3 %all-to-all-start.3 = ((f32[4,4,16,1024]{3,2,1,0:T(8,128)}), f32[4,4,16,1024]{3,2,1,0:T(8,128)S(1)}, u32[]{:S(2)}, u32[]{:S(2)}) async-start(f32[4,4,16,1024]{3,2,1,0:T(8,128)} %get-tuple-element.17), calls=%async_computation.3 | async-start | bytes 2097152 | tf_op jit(solution)/shard_map/all_to_all | solution.py:298
  56.9 8.5 %collective-permute-start.4 = (f32[256,128]{1,0:T(8,128)S(1)}, f32[256,128]{1,0:T(8,128)S(1)}, u32[]{:S(2)}, u32[]{:S(2)}) collective-permute-start(f32[256,128]{1,0:T(8,128)S(1)} %get-tuple-element.18.feat_ref), channel_id=1, source_target_pairs={{2,12},{4,10},{0,6},{8,14},{12,2},{10,4},{6,0},{14,8},{3,13},{5,11... | collective-permute-start | bytes 393224 | tf_op jit(solution)/shard_map/ppermute | solution.py:243

commit v7 on v6

--- a/solution.py
+++ b/solution.py
@@ -174,8 +174,7 @@
     gram = both[:64, :64] + ((high_mid + both[64:128, :64]) + small)
     lower = jnp.concatenate([gram[:32, :32], gram[32:, :32], gram[32:, 32:]], axis=0)
     packed = jnp.concatenate([lower[24 * part : 24 * part + 24] for part in range(4)], axis=1)
-    for copy in range(4):
-        gram_ref[copy] = packed
+    gram_ref[...] = packed
 
 
 def inverse_factor(gram):
@@ -233,9 +232,9 @@
         copy.wait()
 
 
-def fold_kernel(parts_ref, out_ref):
-    total = (parts_ref[0] + parts_ref[1]) + (parts_ref[2] + parts_ref[3])
-    for index in range(8):
+def fold_kernel(left_ref, right_ref, out_ref):
+    total = left_ref[...] + right_ref[...]
+    for index in range(16):
         out_ref[index] = total
 
 
@@ -311,16 +310,22 @@
     mixed, gram = kernel_call(
         gram_kernel,
         (IN_VMEM, IN_VMEM),
-        [((rank, width), IN_VMEM), ((4, 24, 128), IN_VMEM)],
+        [((rank, width), IN_VMEM), ((24, 128), IN_VMEM)],
         (average, delta),
         400 * mega,
         3 * mega,
         (),
         GRAM_LIMIT,
     )
-    gram = lax.all_to_all(gram, ("zl", "core"), 0, 0)
-    (gram,) = kernel_call(fold_kernel, (IN_VMEM,), [((8, 24, 128), IN_VMEM)], (gram,), mega, mega)
-    parts = lax.all_to_all(gram, "y", 0, 0)
+    (gram,) = kernel_call(
+        fold_kernel,
+        (IN_VMEM, IN_VMEM),
+        [((16, 24, 128), IN_VMEM)],
+        (gram, lax.ppermute(gram, "core", SWAP)),
+        mega,
+        mega,
+    )
+    parts = lax.all_to_all(gram, ("zl", "y"), 0, 0)
     (result,) = kernel_call(
         functools.partial(finish_kernel, total_feat=total_feat),
         (IN_VMEM, IN_VMEM),

time: 100 us -> 98.2 us (0.982)
  the two profiles are of different devices: /device:TPU:1 before, /device:TPU:10 now
where the time goes in v7:
time: 98.2 us; the launch traced here: 97.6 us
  starting transfers between devices  42.9 us (44%)
  waiting for transfers between devices  25 us (25%)
  blocking collectives  16.8 us (17%)
  Pallas kernels  12.7 us (13%)
    all_to_all x1, blocking collectives, per_device(): parts = lax.all_to_all(gram, ('zl', 'y'), 0, 0)  16.8 us
    all_to_all x2, starting transfers between devices, per_device(): pieces = lax.all_to_all(pieces, 'zh', 0, 0)  13.1 us
    pallas_call x8, Pallas kernels, kernel_call(): pl.pallas_call(body, out_shape=tuple((f32(*shape) for shape, _ in outs)),...  12.7 us
    ppermute x3, starting transfers between devices, across(): return lax.ppermute(value, 'y', pairs + [(b, a) for a, b in pairs])  11.9 us
    ppermute x3, waiting for transfers between devices, across(): return lax.ppermute(value, 'y', pairs + [(b, a) for a, b in pairs])  11.8 us
    all_to_all x2, waiting for transfers between devices, per_device(): pieces = lax.all_to_all(pieces, 'zh', 0, 0)  7.01 us
    all_to_all x1, starting transfers between devices, per_device(): arrived = lax.all_to_all(start.reshape(4, 16, width), 'x', 0, 0)  4.96 us
    all_to_all x1, starting transfers between devices, per_device(): average = lax.all_to_all(chunk, 'x', 0, 0)  4.86 us
  transfers between devices with their start and end apart: 10, of which 8 were waited for; matrix products, arithmetic and copies ran while one was open for 0% of the time, Pallas kernels for 6%

profile of v7, /device:TPU:10, one launch (start us, length us, event | category | flops | bytes accessed | tf_op | source)
XLA Modules:
  0.0 97.6 jit_solution(5666528246908127866)
XLA Ops:
  0.0 0.0 copy-start
  0.0 5.0 %all-to-all-start = ((f32[4,16,4096]{2,1,0:T(8,128)}), f32[4,16,4096]{2,1,0:T(8,128)S(1)}, u32[]{:S(2)}, u32[]{:S(2)}) async-start(f32[4,16,4096]{2,1,0:T(8,128)} %bitcast.4), calls=%async_computation | async-start | bytes 2097152 | tf_op jit(solution)/shard_map/all_to_all | solution.py:255
  5.0 0.0 copy-done
  5.0 2.9 %shard_map.28 = f32[256,128]{1,0:T(8,128)S(1)} custom-call(f32[64,4096]{1,0:T(8,128)S(1)} %bitcast.5, bf16[2,128,4096]{2,1,0:T(8,128)(2,1)} %bitcast.7), custom_call_target="tpu_custom_call" | custom-call | flops 734003200 | bytes 8388608 | tf_op jit(solution)/shard_map/pallas_call | solution.py:60
  7.9 1.9 %collective-permute-start = (f32[256,128]{1,0:T(8,128)S(1)}, f32[256,128]{1,0:T(8,128)S(1)}, u32[]{:S(2)}, u32[]{:S(2)}) collective-permute-start(f32[256,128]{1,0:T(8,128)S(1)} %shard_map.28), channel_id=1, source_target_pairs={{0,1},{1,0},{2,3},{3,2},{4,5},{5,4},{6,7},{7,6},{8,9},{9,8},{10,11... | collective-permute-start | bytes 393224 | tf_op jit(solution)/shard_map/ppermute | solution.py:266
  9.8 1.3 %collective-permute-done = f32[256,128]{1,0:T(8,128)S(1)} collective-permute-done((f32[256,128]{1,0:T(8,128)S(1)}, f32[256,128]{1,0:T(8,128)S(1)}, u32[]{:S(2)}, u32[]{:S(2)}) %collective-permute-start) | collective-permute-done | bytes 131104 | tf_op jit(solution)/shard_map/ppermute | solution.py:266
  11.2 4.3 %collective-permute-start.1 = (f32[256,128]{1,0:T(8,128)S(1)}, f32[256,128]{1,0:T(8,128)S(1)}, u32[]{:S(2)}, u32[]{:S(2)}) collective-permute-start(f32[256,128]{1,0:T(8,128)S(1)} %add.3.feat_ref), channel_id=1, source_target_pairs={{0,16},{16,0},{1,17},{17,1},{2,18},{18,2},{3,19},{19,3},{4,20},{20... | collective-permute-start | bytes 393224 | tf_op jit(solution)/shard_map/ppermute | solution.py:271
  15.4 3.8 %collective-permute-done.1.other_ref = f32[256,128]{1,0:T(8,128)S(1)} collective-permute-done((f32[256,128]{1,0:T(8,128)S(1)}, f32[256,128]{1,0:T(8,128)S(1)}, u32[]{:S(2)}, u32[]{:S(2)}) %collective-permute-start.1) | collective-permute-done | bytes 131104 | tf_op jit(solution)/shard_map/ppermute | solution.py:271
  19.2 0.0 all-to-all-done.received_ref
  19.2 0.7 shard_map.29
  20.0 9.7 %all-to-all-start.1 = ((f32[4,16,1024]{2,1,0:T(8,128)}), f32[4,16,1024]{2,1,0:T(8,128)S(1)}, u32[]{:S(2)}, u32[]{:S(2)}) async-start(f32[4,16,1024]{2,1,0:T(8,128)} %get-tuple-element.13), calls=%async_computation.1 | async-start | bytes 524288 | tf_op jit(solution)/shard_map/all_to_all | solution.py:276
  29.7 2.3 %collective-permute-start.2 = (f32[256,128]{1,0:T(8,128)S(1)}, f32[256,128]{1,0:T(8,128)S(1)}, u32[]{:S(2)}, u32[]{:S(2)}) collective-permute-start(f32[256,128]{1,0:T(8,128)S(1)} %get-tuple-element.14.feat_ref), channel_id=1, source_target_pairs={{0,2},{4,6},{8,10},{12,14},{2,0},{6,4},{10,8},{14,12},{1,3},{5,7},... | collective-permute-start | bytes 393224 | tf_op jit(solution)/shard_map/ppermute | solution.py:242
  32.0 4.5 %collective-permute-done.2.other_ref = f32[256,128]{1,0:T(8,128)S(1)} collective-permute-done((f32[256,128]{1,0:T(8,128)S(1)}, f32[256,128]{1,0:T(8,128)S(1)}, u32[]{:S(2)}, u32[]{:S(2)}) %collective-permute-start.2) | collective-permute-done | bytes 131104 | tf_op jit(solution)/shard_map/ppermute | solution.py:242
  36.5 3.8 %all-to-all-done.1.received_ref = f32[4,16,1024]{2,1,0:T(8,128)S(1)} async-done(((f32[4,16,1024]{2,1,0:T(8,128)}), f32[4,16,1024]{2,1,0:T(8,128)S(1)}, u32[]{:S(2)}, u32[]{:S(2)}) %all-to-all-start.1) | async-done | bytes 262176 | tf_op jit(solution)/shard_map/all_to_all | solution.py:276
  40.3 0.7 shard_map.30
  41.1 3.4 %all-to-all-start.2 = ((f32[4,16,1024]{2,1,0:T(8,128)}), f32[4,16,1024]{2,1,0:T(8,128)S(1)}, u32[]{:S(2)}, u32[]{:S(2)}) async-start(f32[4,16,1024]{2,1,0:T(8,128)} %get-tuple-element.15), calls=%async_computation.2 | async-start | bytes 524288 | tf_op jit(solution)/shard_map/all_to_all | solution.py:286
  44.5 3.5 %collective-permute-start.3 = (f32[256,128]{1,0:T(8,128)S(1)}, f32[256,128]{1,0:T(8,128)S(1)}, u32[]{:S(2)}, u32[]{:S(2)}) collective-permute-start(f32[256,128]{1,0:T(8,128)S(1)} %get-tuple-element.16.feat_ref), channel_id=1, source_target_pairs={{2,4},{6,8},{10,12},{14,0},{4,2},{8,6},{12,10},{0,14},{3,5},{7,9},... | collective-permute-start | bytes 393224 | tf_op jit(solution)/shard_map/ppermute | solution.py:242
  48.0 3.4 %collective-permute-done.3.other_ref = f32[256,128]{1,0:T(8,128)S(1)} collective-permute-done((f32[256,128]{1,0:T(8,128)S(1)}, f32[256,128]{1,0:T(8,128)S(1)}, u32[]{:S(2)}, u32[]{:S(2)}) %collective-permute-start.3) | collective-permute-done | bytes 131104 | tf_op jit(solution)/shard_map/ppermute | solution.py:242
  51.4 3.2 %all-to-all-done.2.received_ref = f32[4,16,1024]{2,1,0:T(8,128)S(1)} async-done(((f32[4,16,1024]{2,1,0:T(8,128)}), f32[4,16,1024]{2,1,0:T(8,128)S(1)}, u32[]{:S(2)}, u32[]{:S(2)}) %all-to-all-start.2) | async-done | bytes 262176 | tf_op jit(solution)/shard_map/all_to_all | solution.py:286
  54.6 1.0 %shard_map.31 = (f32[4,4,16,1024]{3,2,1,0:T(8,128)}, f32[256,128]{1,0:T(8,128)S(1)}) custom-call(f32[4,16,1024]{2,1,0:T(8,128)S(1)} %all-to-all-done.2.received_ref, f32[256,128]{1,0:T(8,128)S(1)} %get-tuple-element.16.feat_ref, f32[256,128]{1,0:T(8,128)S(1)} %collective-permute-done.3.other_ref), custom_call_target="tpu_custom_call" | custom-call | flops 1048576 | bytes 2097152 | tf_op jit(solution)/shard_map/pallas_call | solution.py:60
  55.6 4.9 %all-to-all-start.3 = ((f32[4,4,16,1024]{3,2,1,0:T(8,128)}), f32[4,4,16,1024]{3,2,1,0:T(8,128)S(1)}, u32[]{:S(2)}, u32[]{:S(2)}) async-start(f32[4,4,16,1024]{3,2,1,0:T(8,128)} %get-tuple-element.17), calls=%async_computation.3 | async-start | bytes 2097152 | tf_op jit(solution)/shard_map/all_to_all | solution.py:297
  60.4 6.0 %collective-permute-start.4 = (f32[256,128]{1,0:T(8,128)S(1)}, f32[256,128]{1,0:T(8,128)S(1)}, u32[]{:S(2)}, u32[]{:S(2)}) collective-permute-start(f32[256,128]{1,0:T(8,128)S(1)} %get-tuple-element.18.feat_ref), channel_id=1, source_target_pairs={{2,12},{4,10},{0,6},{8,14},{12,2},{10,4},{6,0},{14,8},{3,13},{5,11... | collective-permute-start | bytes 393224 | tf_op jit(solution)/shard_map/ppermute | solution.py:242
  66.5 3.9 %collective-permute-done.4.other_ref = f32[256,128]{1,0:T(8,128)S(1)} collective-permute-done((f32[256,128]{1,0:T(8,128)S(1)}, f32[256,128]{1,0:T(8,128)S(1)}, u32[]{:S(2)}, u32[]{:S(2)}) %collective-permute-start.4) | collective-permute-done | bytes 131104 | tf_op jit(solution)/shard_map/ppermute | solution.py:242
  70.4 2.9 %shard_map.32.delta_ref = f32[64,4096]{1,0:T(8,128)S(1)} custom-call(f32[256,128]{1,0:T(8,128)S(1)} %get-tuple-element.18.feat_ref, f32[256,128]{1,0:T(8,128)S(1)} %collective-permute-done.4.other_ref, f32[64,4096]{1,0:T(8,128)S(1)} %bitcast.6, bf16[2,128,4096]{2,1,0:T(8,128)(2,1)} %bitcast.8), custom_call_target="tpu_custom_call" | custom-call | flops 734003200 | bytes 8388608 | tf_op jit(solution)/shard_map/pallas_call | solution.py:60
  73.3 0.0 all-to-all-done.3.average_ref
  73.3 0.9 shard_map.33
  74.2 1.9 %collective-permute-start.5 = (f32[24,128]{1,0:T(8,128)S(1)}, f32[24,128]{1,0:T(8,128)S(1)}, u32[]{:S(2)}, u32[]{:S(2)}) collective-permute-start(f32[24,128]{1,0:T(8,128)S(1)} %get-tuple-element.19.left_ref), channel_id=1, source_target_pairs={{0,1},{1,0},{2,3},{3,2},{4,5},{5,4},{6,7},{7,6},{8,9},{9,8},{10,11... | collective-permute-start | bytes 36872 | tf_op jit(solution)/shard_map/ppermute | solution.py:324
  76.1 1.1 %collective-permute-done.5.right_ref = f32[24,128]{1,0:T(8,128)S(1)} collective-permute-done((f32[24,128]{1,0:T(8,128)S(1)}, f32[24,128]{1,0:T(8,128)S(1)}, u32[]{:S(2)}, u32[]{:S(2)}) %collective-permute-start.5) | collective-permute-done | bytes 12320 | tf_op jit(solution)/shard_map/ppermute | solution.py:324
  77.2 16.8 %all_to_all.25.parts_ref = f32[16,24,128]{2,1,0:T(8,128)S(1)} all-to-all(f32[16,24,128]{2,1,0:T(8,128)S(1)} %shard_map.34), channel_id=1, replica_groups=mesh['x'=4,'zh'=4,'zl'=2,'y'=8,'core'=2] {'zl','y'}, dimensions={0} | all-to-all | bytes 393216 | tf_op jit(solution)/shard_map/all_to_all | solution.py:328
  94.1 3.5 %shard_map.35 = f32[64,4096]{1,0:T(8,128)} custom-call(f32[16,24,128]{2,1,0:T(8,128)S(1)} %all_to_all.25.parts_ref, f32[64,4096]{1,0:T(8,128)S(1)} %get-tuple-element.20.mixed_ref), custom_call_target="tpu_custom_call" | custom-call | flops 419430400 | bytes 3145728 | tf_op jit(solution)/shard_map/pallas_call | solution.py:60
  (2 shorter events, 0.0 us)
Async XLA Ops:
  0.0 5.0 %copy-start = (f32[1,64,4096]{2,1,0:T(8,128)S(1)}, f32[1,64,4096]{2,1,0:T(8,128)}, u32[]{:S(2)}) copy-start(f32[1,64,4096]{2,1,0:T(8,128)} %param.2) | copy-start | bytes 3145732
  0.0 19.2 %all-to-all-start = ((f32[4,16,4096]{2,1,0:T(8,128)}), f32[4,16,4096]{2,1,0:T(8,128)S(1)}, u32[]{:S(2)}, u32[]{:S(2)}) async-start(f32[4,16,4096]{2,1,0:T(8,128)} %bitcast.4), calls=%async_computation | async-start | bytes 2097152 | tf_op jit(solution)/shard_map/all_to_all | solution.py:255
  7.9 3.2 %collective-permute-start = (f32[256,128]{1,0:T(8,128)S(1)}, f32[256,128]{1,0:T(8,128)S(1)}, u32[]{:S(2)}, u32[]{:S(2)}) collective-permute-start(f32[256,128]{1,0:T(8,128)S(1)} %shard_map.28), channel_id=1, source_target_pairs={{0,1},{1,0},{2,3},{3,2},{4,5},{5,4},{6,7},{7,6},{8,9},{9,8},{10,11... | collective-permute-start | bytes 393224 | tf_op jit(solution)/shard_map/ppermute | solution.py:266
  11.2 8.1 %collective-permute-start.1 = (f32[256,128]{1,0:T(8,128)S(1)}, f32[256,128]{1,0:T(8,128)S(1)}, u32[]{:S(2)}, u32[]{:S(2)}) collective-permute-start(f32[256,128]{1,0:T(8,128)S(1)} %add.3.feat_ref), channel_id=1, source_target_pairs={{0,16},{16,0},{1,17},{17,1},{2,18},{18,2},{3,19},{19,3},{4,20},{20... | collective-permute-start | bytes 393224 | tf_op jit(solution)/shard_map/ppermute | solution.py:271
  20.0 20.3 %all-to-all-start.1 = ((f32[4,16,1024]{2,1,0:T(8,128)}), f32[4,16,1024]{2,1,0:T(8,128)S(1)}, u32[]{:S(2)}, u32[]{:S(2)}) async-start(f32[4,16,1024]{2,1,0:T(8,128)} %get-tuple-element.13), calls=%async_computation.1 | async-start | bytes 524288 | tf_op jit(solution)/shard_map/all_to_all | solution.py:276
  29.7 6.8 %collective-permute-start.2 = (f32[256,128]{1,0:T(8,128)S(1)}, f32[256,128]{1,0:T(8,128)S(1)}, u32[]{:S(2)}, u32[]{:S(2)}) collective-permute-start(f32[256,128]{1,0:T(8,128)S(1)} %get-tuple-element.14.feat_ref), channel_id=1, source_target_pairs={{0,2},{4,6},{8,10},{12,14},{2,0},{6,4},{10,8},{14,12},{1,3},{5,7},... | collective-permute-start | bytes 393224 | tf_op jit(solution)/shard_map/ppermute | solution.py:242
  41.1 13.5 %all-to-all-start.2 = ((f32[4,16,1024]{2,1,0:T(8,128)}), f32[4,16,1024]{2,1,0:T(8,128)S(1)}, u32[]{:S(2)}, u32[]{:S(2)}) async-start(f32[4,16,1024]{2,1,0:T(8,128)} %get-tuple-element.15), calls=%async_computation.2 | async-start | bytes 524288 | tf_op jit(solution)/shard_map/all_to_all | solution.py:286
  44.5 6.9 %collective-permute-start.3 = (f32[256,128]{1,0:T(8,128)S(1)}, f32[256,128]{1,0:T(8,128)S(1)}, u32[]{:S(2)}, u32[]{:S(2)}) collective-permute-start(f32[256,128]{1,0:T(8,128)S(1)} %get-tuple-element.16.feat_ref), channel_id=1, source_target_pairs={{2,4},{6,8},{10,12},{14,0},{4,2},{8,6},{12,10},{0,14},{3,5},{7,9},... | collective-permute-start | bytes 393224 | tf_op jit(solution)/shard_map/ppermute | solution.py:242
  55.6 17.7 %all-to-all-start.3 = ((f32[4,4,16,1024]{3,2,1,0:T(8,128)}), f32[4,4,16,1024]{3,2,1,0:T(8,128)S(1)}, u32[]{:S(2)}, u32[]{:S(2)}) async-start(f32[4,4,16,1024]{3,2,1,0:T(8,128)} %get-tuple-element.17), calls=%async_computation.3 | async-start | bytes 2097152 | tf_op jit(solution)/shard_map/all_to_all | solution.py:297
  60.4 10.0 %collective-permute-start.4 = (f32[256,128]{1,0:T(8,128)S(1)}, f32[256,128]{1,0:T(8,128)S(1)}, u32[]{:S(2)}, u32[]{:S(2)}) collective-permute-start(f32[256,128]{1,0:T(8,128)S(1)} %get-tuple-element.18.feat_ref), channel_id=1, source_target_pairs={{2,12},{4,10},{0,6},{8,14},{12,2},{10,4},{6,0},{14,8},{3,13},{5,11... | collective-permute-start | bytes 393224 | tf_op jit(solution)/shard_map/ppermute | solution.py:242
  74.2 3.1 %collective-permute-start.5 = (f32[24,128]{1,0:T(8,128)S(1)}, f32[24,128]{1,0:T(8,128)S(1)}, u32[]{:S(2)}, u32[]{:S(2)}) collective-permute-start(f32[24,128]{1,0:T(8,128)S(1)} %get-tuple-element.19.left_ref), channel_id=1, source_target_pairs={{0,1},{1,0},{2,3},{3,2},{4,5},{5,4},{6,7},{7,6},{8,9},{9,8},{10,11... | collective-permute-start | bytes 36872 | tf_op jit(solution)/shard_map/ppermute | solution.py:324

commit v8 on v7

--- a/solution.py
+++ b/solution.py
@@ -144,13 +144,18 @@
     onto1 = feat_ref[:128, 64:] + other_ref[:128, 64:]
     cross = feat_ref[128:] + other_ref[128:]
     proj0 = onto0 * inv_scale
-    cov0 = dot(proj0, proj0, ON_ROWS)
-    proj1 = (dot(onto1, eye - step_size * cov0, PLAIN) + step_size * dot(cross, proj0, PLAIN)) * inv_scale
-    cov1 = dot(proj1, proj1, ON_ROWS)
-    mix_b = step_size * (step_size * dot(cov1, cov0, PLAIN) - cov0 - cov1)
     turned0 = proj0.T
-    mix_0 = step_size * (turned0 - step_size * dot(cov1, turned0, PLAIN))
-    mix_1 = step_size * proj1.T
+    cov0 = exact_dot(turned0, proj0)
+    onto_cross = jnp.concatenate([onto1, cross], axis=1)
+    proj1 = inv_scale * exact_dot(
+        onto_cross, jnp.concatenate([eye - step_size * cov0, step_size * proj0], axis=0)
+    )
+    turned1 = proj1.T
+    cov1 = exact_dot(turned1, proj1)
+    both = step_size * exact_dot(cov1, jnp.concatenate([turned0, cov0], axis=1))
+    mix_b = step_size * (both[:, 128:] - cov0 - cov1)
+    mix_0 = step_size * (turned0 - both[:, :128])
+    mix_1 = step_size * turned1
     left = jnp.concatenate([mix_b, mix_b, mix_b, mix_0, mix_1], axis=1)
     left = jnp.concatenate(split3(left), axis=0)
     for c, span in enumerate(spans):

time: 98.2 us -> 98.1 us (level)
  no operation moved by 1% of the time
where the time goes in v8:
time: 98.1 us; the launch traced here: 97.5 us
  starting transfers between devices  42.9 us (44%)
  waiting for transfers between devices  25 us (25%)
  blocking collectives  16.8 us (17%)
  Pallas kernels  12.6 us (13%)
    all_to_all x1, blocking collectives, per_device(): parts = lax.all_to_all(gram, ('zl', 'y'), 0, 0)  16.8 us
    all_to_all x2, starting transfers between devices, per_device(): pieces = lax.all_to_all(pieces, 'zh', 0, 0)  13.1 us
    pallas_call x8, Pallas kernels, kernel_call(): pl.pallas_call(body, out_shape=tuple((f32(*shape) for shape, _ in outs)),...  12.6 us
    ppermute x3, starting transfers between devices, across(): return lax.ppermute(value, 'y', pairs + [(b, a) for a, b in pairs])  11.9 us
    ppermute x3, waiting for transfers between devices, across(): return lax.ppermute(value, 'y', pairs + [(b, a) for a, b in pairs])  11.8 us
    all_to_all x2, waiting for transfers between devices, per_device(): pieces = lax.all_to_all(pieces, 'zh', 0, 0)  7.01 us
    all_to_all x1, starting transfers between devices, per_device(): arrived = lax.all_to_all(start.reshape(4, 16, width), 'x', 0, 0)  4.96 us
    all_to_all x1, starting transfers between devices, per_device(): average = lax.all_to_all(chunk, 'x', 0, 0)  4.86 us
  transfers between devices with their start and end apart: 10, of which 8 were waited for; matrix products, arithmetic and copies ran while one was open for 0% of the time, Pallas kernels for 6%

profile of v8, /device:TPU:10, one launch (start us, length us, event | category | flops | bytes accessed | tf_op | source)
XLA Modules:
  0.0 97.5 jit_solution(3755143470319943407)
XLA Ops:
  0.0 0.0 copy-start
  0.0 5.0 %all-to-all-start = ((f32[4,16,4096]{2,1,0:T(8,128)}), f32[4,16,4096]{2,1,0:T(8,128)S(1)}, u32[]{:S(2)}, u32[]{:S(2)}) async-start(f32[4,16,4096]{2,1,0:T(8,128)} %bitcast.4), calls=%async_computation | async-start | bytes 2097152 | tf_op jit(solution)/shard_map/all_to_all | solution.py:260
  5.0 0.0 copy-done
  5.0 2.9 %shard_map.28 = f32[256,128]{1,0:T(8,128)S(1)} custom-call(f32[64,4096]{1,0:T(8,128)S(1)} %bitcast.5, bf16[2,128,4096]{2,1,0:T(8,128)(2,1)} %bitcast.7), custom_call_target="tpu_custom_call" | custom-call | flops 734003200 | bytes 8388608 | tf_op jit(solution)/shard_map/pallas_call | solution.py:60
  7.9 1.9 %collective-permute-start = (f32[256,128]{1,0:T(8,128)S(1)}, f32[256,128]{1,0:T(8,128)S(1)}, u32[]{:S(2)}, u32[]{:S(2)}) collective-permute-start(f32[256,128]{1,0:T(8,128)S(1)} %shard_map.28), channel_id=1, source_target_pairs={{0,1},{1,0},{2,3},{3,2},{4,5},{5,4},{6,7},{7,6},{8,9},{9,8},{10,11... | collective-permute-start | bytes 393224 | tf_op jit(solution)/shard_map/ppermute | solution.py:271
  9.8 1.3 %collective-permute-done = f32[256,128]{1,0:T(8,128)S(1)} collective-permute-done((f32[256,128]{1,0:T(8,128)S(1)}, f32[256,128]{1,0:T(8,128)S(1)}, u32[]{:S(2)}, u32[]{:S(2)}) %collective-permute-start) | collective-permute-done | bytes 131104 | tf_op jit(solution)/shard_map/ppermute | solution.py:271
  11.2 4.3 %collective-permute-start.1 = (f32[256,128]{1,0:T(8,128)S(1)}, f32[256,128]{1,0:T(8,128)S(1)}, u32[]{:S(2)}, u32[]{:S(2)}) collective-permute-start(f32[256,128]{1,0:T(8,128)S(1)} %add.3.feat_ref), channel_id=1, source_target_pairs={{0,16},{16,0},{1,17},{17,1},{2,18},{18,2},{3,19},{19,3},{4,20},{20... | collective-permute-start | bytes 393224 | tf_op jit(solution)/shard_map/ppermute | solution.py:276
  15.4 3.8 %collective-permute-done.1.other_ref = f32[256,128]{1,0:T(8,128)S(1)} collective-permute-done((f32[256,128]{1,0:T(8,128)S(1)}, f32[256,128]{1,0:T(8,128)S(1)}, u32[]{:S(2)}, u32[]{:S(2)}) %collective-permute-start.1) | collective-permute-done | bytes 131104 | tf_op jit(solution)/shard_map/ppermute | solution.py:276
  19.2 0.0 all-to-all-done.received_ref
  19.2 0.7 shard_map.29
  20.0 9.7 %all-to-all-start.1 = ((f32[4,16,1024]{2,1,0:T(8,128)}), f32[4,16,1024]{2,1,0:T(8,128)S(1)}, u32[]{:S(2)}, u32[]{:S(2)}) async-start(f32[4,16,1024]{2,1,0:T(8,128)} %get-tuple-element.13), calls=%async_computation.1 | async-start | bytes 524288 | tf_op jit(solution)/shard_map/all_to_all | solution.py:281
  29.7 2.3 %collective-permute-start.2 = (f32[256,128]{1,0:T(8,128)S(1)}, f32[256,128]{1,0:T(8,128)S(1)}, u32[]{:S(2)}, u32[]{:S(2)}) collective-permute-start(f32[256,128]{1,0:T(8,128)S(1)} %get-tuple-element.14.feat_ref), channel_id=1, source_target_pairs={{0,2},{4,6},{8,10},{12,14},{2,0},{6,4},{10,8},{14,12},{1,3},{5,7},... | collective-permute-start | bytes 393224 | tf_op jit(solution)/shard_map/ppermute | solution.py:247
  32.0 4.5 %collective-permute-done.2.other_ref = f32[256,128]{1,0:T(8,128)S(1)} collective-permute-done((f32[256,128]{1,0:T(8,128)S(1)}, f32[256,128]{1,0:T(8,128)S(1)}, u32[]{:S(2)}, u32[]{:S(2)}) %collective-permute-start.2) | collective-permute-done | bytes 131104 | tf_op jit(solution)/shard_map/ppermute | solution.py:247
  36.5 3.8 %all-to-all-done.1.received_ref = f32[4,16,1024]{2,1,0:T(8,128)S(1)} async-done(((f32[4,16,1024]{2,1,0:T(8,128)}), f32[4,16,1024]{2,1,0:T(8,128)S(1)}, u32[]{:S(2)}, u32[]{:S(2)}) %all-to-all-start.1) | async-done | bytes 262176 | tf_op jit(solution)/shard_map/all_to_all | solution.py:281
  40.3 0.7 shard_map.30
  41.1 3.4 %all-to-all-start.2 = ((f32[4,16,1024]{2,1,0:T(8,128)}), f32[4,16,1024]{2,1,0:T(8,128)S(1)}, u32[]{:S(2)}, u32[]{:S(2)}) async-start(f32[4,16,1024]{2,1,0:T(8,128)} %get-tuple-element.15), calls=%async_computation.2 | async-start | bytes 524288 | tf_op jit(solution)/shard_map/all_to_all | solution.py:291
  44.5 3.5 %collective-permute-start.3 = (f32[256,128]{1,0:T(8,128)S(1)}, f32[256,128]{1,0:T(8,128)S(1)}, u32[]{:S(2)}, u32[]{:S(2)}) collective-permute-start(f32[256,128]{1,0:T(8,128)S(1)} %get-tuple-element.16.feat_ref), channel_id=1, source_target_pairs={{2,4},{6,8},{10,12},{14,0},{4,2},{8,6},{12,10},{0,14},{3,5},{7,9},... | collective-permute-start | bytes 393224 | tf_op jit(solution)/shard_map/ppermute | solution.py:247
  48.0 3.4 %collective-permute-done.3.other_ref = f32[256,128]{1,0:T(8,128)S(1)} collective-permute-done((f32[256,128]{1,0:T(8,128)S(1)}, f32[256,128]{1,0:T(8,128)S(1)}, u32[]{:S(2)}, u32[]{:S(2)}) %collective-permute-start.3) | collective-permute-done | bytes 131104 | tf_op jit(solution)/shard_map/ppermute | solution.py:247
  51.4 3.2 %all-to-all-done.2.received_ref = f32[4,16,1024]{2,1,0:T(8,128)S(1)} async-done(((f32[4,16,1024]{2,1,0:T(8,128)}), f32[4,16,1024]{2,1,0:T(8,128)S(1)}, u32[]{:S(2)}, u32[]{:S(2)}) %all-to-all-start.2) | async-done | bytes 262176 | tf_op jit(solution)/shard_map/all_to_all | solution.py:291
  54.6 1.0 %shard_map.31 = (f32[4,4,16,1024]{3,2,1,0:T(8,128)}, f32[256,128]{1,0:T(8,128)S(1)}) custom-call(f32[4,16,1024]{2,1,0:T(8,128)S(1)} %all-to-all-done.2.received_ref, f32[256,128]{1,0:T(8,128)S(1)} %get-tuple-element.16.feat_ref, f32[256,128]{1,0:T(8,128)S(1)} %collective-permute-done.3.other_ref), custom_call_target="tpu_custom_call" | custom-call | flops 1048576 | bytes 2097152 | tf_op jit(solution)/shard_map/pallas_call | solution.py:60
  55.6 4.9 %all-to-all-start.3 = ((f32[4,4,16,1024]{3,2,1,0:T(8,128)}), f32[4,4,16,1024]{3,2,1,0:T(8,128)S(1)}, u32[]{:S(2)}, u32[]{:S(2)}) async-start(f32[4,4,16,1024]{3,2,1,0:T(8,128)} %get-tuple-element.17), calls=%async_computation.3 | async-start | bytes 2097152 | tf_op jit(solution)/shard_map/all_to_all | solution.py:302
  60.4 6.0 %collective-permute-start.4 = (f32[256,128]{1,0:T(8,128)S(1)}, f32[256,128]{1,0:T(8,128)S(1)}, u32[]{:S(2)}, u32[]{:S(2)}) collective-permute-start(f32[256,128]{1,0:T(8,128)S(1)} %get-tuple-element.18.feat_ref), channel_id=1, source_target_pairs={{2,12},{4,10},{0,6},{8,14},{12,2},{10,4},{6,0},{14,8},{3,13},{5,11... | collective-permute-start | bytes 393224 | tf_op jit(solution)/shard_map/ppermute | solution.py:247
  66.5 3.9 %collective-permute-done.4.other_ref = f32[256,128]{1,0:T(8,128)S(1)} collective-permute-done((f32[256,128]{1,0:T(8,128)S(1)}, f32[256,128]{1,0:T(8,128)S(1)}, u32[]{:S(2)}, u32[]{:S(2)}) %collective-permute-start.4) | collective-permute-done | bytes 131104 | tf_op jit(solution)/shard_map/ppermute | solution.py:247
  70.4 2.8 %shard_map.32.delta_ref = f32[64,4096]{1,0:T(8,128)S(1)} custom-call(f32[256,128]{1,0:T(8,128)S(1)} %get-tuple-element.18.feat_ref, f32[256,128]{1,0:T(8,128)S(1)} %collective-permute-done.4.other_ref, f32[64,4096]{1,0:T(8,128)S(1)} %bitcast.6, bf16[2,128,4096]{2,1,0:T(8,128)(2,1)} %bitcast.8), custom_call_target="tpu_custom_call" | custom-call | flops 734003200 | bytes 8388608 | tf_op jit(solution)/shard_map/pallas_call | solution.py:60
  73.2 0.0 all-to-all-done.3.average_ref
  73.2 0.9 shard_map.33
  74.1 1.9 %collective-permute-start.5 = (f32[24,128]{1,0:T(8,128)S(1)}, f32[24,128]{1,0:T(8,128)S(1)}, u32[]{:S(2)}, u32[]{:S(2)}) collective-permute-start(f32[24,128]{1,0:T(8,128)S(1)} %get-tuple-element.19.left_ref), channel_id=1, source_target_pairs={{0,1},{1,0},{2,3},{3,2},{4,5},{5,4},{6,7},{7,6},{8,9},{9,8},{10,11... | collective-permute-start | bytes 36872 | tf_op jit(solution)/shard_map/ppermute | solution.py:329
  76.0 1.1 %collective-permute-done.5.right_ref = f32[24,128]{1,0:T(8,128)S(1)} collective-permute-done((f32[24,128]{1,0:T(8,128)S(1)}, f32[24,128]{1,0:T(8,128)S(1)}, u32[]{:S(2)}, u32[]{:S(2)}) %collective-permute-start.5) | collective-permute-done | bytes 12320 | tf_op jit(solution)/shard_map/ppermute | solution.py:329
  77.2 16.8 %all_to_all.25.parts_ref = f32[16,24,128]{2,1,0:T(8,128)S(1)} all-to-all(f32[16,24,128]{2,1,0:T(8,128)S(1)} %shard_map.34), channel_id=1, replica_groups=mesh['x'=4,'zh'=4,'zl'=2,'y'=8,'core'=2] {'zl','y'}, dimensions={0} | all-to-all | bytes 393216 | tf_op jit(solution)/shard_map/all_to_all | solution.py:333
  94.0 3.5 %shard_map.35 = f32[64,4096]{1,0:T(8,128)} custom-call(f32[16,24,128]{2,1,0:T(8,128)S(1)} %all_to_all.25.parts_ref, f32[64,4096]{1,0:T(8,128)S(1)} %get-tuple-element.20.mixed_ref), custom_call_target="tpu_custom_call" | custom-call | flops 419430400 | bytes 3145728 | tf_op jit(solution)/shard_map/pallas_call | solution.py:60
  (2 shorter events, 0.0 us)
Async XLA Ops:
  0.0 5.0 %copy-start = (f32[1,64,4096]{2,1,0:T(8,128)S(1)}, f32[1,64,4096]{2,1,0:T(8,128)}, u32[]{:S(2)}) copy-start(f32[1,64,4096]{2,1,0:T(8,128)} %param.2) | copy-start | bytes 3145732
  0.0 19.2 %all-to-all-start = ((f32[4,16,4096]{2,1,0:T(8,128)}), f32[4,16,4096]{2,1,0:T(8,128)S(1)}, u32[]{:S(2)}, u32[]{:S(2)}) async-start(f32[4,16,4096]{2,1,0:T(8,128)} %bitcast.4), calls=%async_computation | async-start | bytes 2097152 | tf_op jit(solution)/shard_map/all_to_all | solution.py:260
  7.9 3.2 %collective-permute-start = (f32[256,128]{1,0:T(8,128)S(1)}, f32[256,128]{1,0:T(8,128)S(1)}, u32[]{:S(2)}, u32[]{:S(2)}) collective-permute-start(f32[256,128]{1,0:T(8,128)S(1)} %shard_map.28), channel_id=1, source_target_pairs={{0,1},{1,0},{2,3},{3,2},{4,5},{5,4},{6,7},{7,6},{8,9},{9,8},{10,11... | collective-permute-start | bytes 393224 | tf_op jit(solution)/shard_map/ppermute | solution.py:271
  11.2 8.1 %collective-permute-start.1 = (f32[256,128]{1,0:T(8,128)S(1)}, f32[256,128]{1,0:T(8,128)S(1)}, u32[]{:S(2)}, u32[]{:S(2)}) collective-permute-start(f32[256,128]{1,0:T(8,128)S(1)} %add.3.feat_ref), channel_id=1, source_target_pairs={{0,16},{16,0},{1,17},{17,1},{2,18},{18,2},{3,19},{19,3},{4,20},{20... | collective-permute-start | bytes 393224 | tf_op jit(solution)/shard_map/ppermute | solution.py:276
  20.0 20.3 %all-to-all-start.1 = ((f32[4,16,1024]{2,1,0:T(8,128)}), f32[4,16,1024]{2,1,0:T(8,128)S(1)}, u32[]{:S(2)}, u32[]{:S(2)}) async-start(f32[4,16,1024]{2,1,0:T(8,128)} %get-tuple-element.13), calls=%async_computation.1 | async-start | bytes 524288 | tf_op jit(solution)/shard_map/all_to_all | solution.py:281
  29.7 6.8 %collective-permute-start.2 = (f32[256,128]{1,0:T(8,128)S(1)}, f32[256,128]{1,0:T(8,128)S(1)}, u32[]{:S(2)}, u32[]{:S(2)}) collective-permute-start(f32[256,128]{1,0:T(8,128)S(1)} %get-tuple-element.14.feat_ref), channel_id=1, source_target_pairs={{0,2},{4,6},{8,10},{12,14},{2,0},{6,4},{10,8},{14,12},{1,3},{5,7},... | collective-permute-start | bytes 393224 | tf_op jit(solution)/shard_map/ppermute | solution.py:247
  41.1 13.5 %all-to-all-start.2 = ((f32[4,16,1024]{2,1,0:T(8,128)}), f32[4,16,1024]{2,1,0:T(8,128)S(1)}, u32[]{:S(2)}, u32[]{:S(2)}) async-start(f32[4,16,1024]{2,1,0:T(8,128)} %get-tuple-element.15), calls=%async_computation.2 | async-start | bytes 524288 | tf_op jit(solution)/shard_map/all_to_all | solution.py:291
  44.5 6.9 %collective-permute-start.3 = (f32[256,128]{1,0:T(8,128)S(1)}, f32[256,128]{1,0:T(8,128)S(1)}, u32[]{:S(2)}, u32[]{:S(2)}) collective-permute-start(f32[256,128]{1,0:T(8,128)S(1)} %get-tuple-element.16.feat_ref), channel_id=1, source_target_pairs={{2,4},{6,8},{10,12},{14,0},{4,2},{8,6},{12,10},{0,14},{3,5},{7,9},... | collective-permute-start | bytes 393224 | tf_op jit(solution)/shard_map/ppermute | solution.py:247
  55.6 17.6 %all-to-all-start.3 = ((f32[4,4,16,1024]{3,2,1,0:T(8,128)}), f32[4,4,16,1024]{3,2,1,0:T(8,128)S(1)}, u32[]{:S(2)}, u32[]{:S(2)}) async-start(f32[4,4,16,1024]{3,2,1,0:T(8,128)} %get-tuple-element.17), calls=%async_computation.3 | async-start | bytes 2097152 | tf_op jit(solution)/shard_map/all_to_all | solution.py:302
  60.4 10.0 %collective-permute-start.4 = (f32[256,128]{1,0:T(8,128)S(1)}, f32[256,128]{1,0:T(8,128)S(1)}, u32[]{:S(2)}, u32[]{:S(2)}) collective-permute-start(f32[256,128]{1,0:T(8,128)S(1)} %get-tuple-element.18.feat_ref), channel_id=1, source_target_pairs={{2,12},{4,10},{0,6},{8,14},{12,2},{10,4},{6,0},{14,8},{3,13},{5,11... | collective-permute-start | bytes 393224 | tf_op jit(solution)/shard_map/ppermute | solution.py:247
  74.1 3.1 %collective-permute-start.5 = (f32[24,128]{1,0:T(8,128)S(1)}, f32[24,128]{1,0:T(8,128)S(1)}, u32[]{:S(2)}, u32[]{:S(2)}) collective-permute-start(f32[24,128]{1,0:T(8,128)S(1)} %get-tuple-element.19.left_ref), channel_id=1, source_target_pairs={{0,1},{1,0},{2,3},{3,2},{4,5},{5,4},{6,7},{7,6},{8,9},{9,8},{10,11... | collective-permute-start | bytes 36872 | tf_op jit(solution)/shard_map/ppermute | solution.py:329

commit v9 on v7

--- a/solution.py
+++ b/solution.py
@@ -220,11 +220,14 @@
         axis=0,
     )
     inverse = inverse_factor(gram)
+    left = jnp.concatenate(split3(jnp.concatenate([inverse] * 3, axis=1)), axis=0)
     width = result.shape[1] // CHUNKS
     copies = []
     for c in range(CHUNKS):
         span = slice(width * c, width * c + width)
-        result[:, span] = exact_dot(inverse, mixed_ref[:, span])
+        right = jnp.concatenate(split3(mixed_ref[:, span]), axis=0)
+        three = dot(left, right, PLAIN, None)
+        result[:, span] = three[:64] + (three[64:128] + three[128:])
         copy = pltpu.make_async_copy(result.at[:, span], out_ref.at[:, span], sems.at[c])
         copy.start()
         copies.append(copy)

time: 98.2 us -> 98.1 us (level)
  no operation moved by 1% of the time
where the time goes in v9:
time: 98.1 us; the launch traced here: 97.5 us
  starting transfers between devices  42.9 us (44%)
  waiting for transfers between devices  25 us (25%)
  blocking collectives  16.8 us (17%)
  Pallas kernels  12.6 us (13%)
    all_to_all x1, blocking collectives, per_device(): parts = lax.all_to_all(gram, ('zl', 'y'), 0, 0)  16.8 us
    all_to_all x2, starting transfers between devices, per_device(): pieces = lax.all_to_all(pieces, 'zh', 0, 0)  13.1 us
    pallas_call x8, Pallas kernels, kernel_call(): pl.pallas_call(body, out_shape=tuple((f32(*shape) for shape, _ in outs)),...  12.6 us
    ppermute x3, starting transfers between devices, across(): return lax.ppermute(value, 'y', pairs + [(b, a) for a, b in pairs])  11.9 us
    ppermute x3, waiting for transfers between devices, across(): return lax.ppermute(value, 'y', pairs + [(b, a) for a, b in pairs])  11.8 us
    all_to_all x2, waiting for transfers between devices, per_device(): pieces = lax.all_to_all(pieces, 'zh', 0, 0)  7.01 us
    all_to_all x1, starting transfers between devices, per_device(): arrived = lax.all_to_all(start.reshape(4, 16, width), 'x', 0, 0)  4.96 us
    all_to_all x1, starting transfers between devices, per_device(): average = lax.all_to_all(chunk, 'x', 0, 0)  4.86 us
  transfers between devices with their start and end apart: 10, of which 8 were waited for; matrix products, arithmetic and copies ran while one was open for 0% of the time, Pallas kernels for 6%

profile of v9, /device:TPU:10, one launch (start us, length us, event | category | flops | bytes accessed | tf_op | source)
XLA Modules:
  0.0 97.5 jit_solution(3229840012734273892)
XLA Ops:
  0.0 0.0 copy-start
  0.0 5.0 %all-to-all-start = ((f32[4,16,4096]{2,1,0:T(8,128)}), f32[4,16,4096]{2,1,0:T(8,128)S(1)}, u32[]{:S(2)}, u32[]{:S(2)}) async-start(f32[4,16,4096]{2,1,0:T(8,128)} %bitcast.4), calls=%async_computation | async-start | bytes 2097152 | tf_op jit(solution)/shard_map/all_to_all | solution.py:258
  5.0 0.0 copy-done
  5.0 2.9 %shard_map.28 = f32[256,128]{1,0:T(8,128)S(1)} custom-call(f32[64,4096]{1,0:T(8,128)S(1)} %bitcast.5, bf16[2,128,4096]{2,1,0:T(8,128)(2,1)} %bitcast.7), custom_call_target="tpu_custom_call" | custom-call | flops 734003200 | bytes 8388608 | tf_op jit(solution)/shard_map/pallas_call | solution.py:60
  7.9 1.9 %collective-permute-start = (f32[256,128]{1,0:T(8,128)S(1)}, f32[256,128]{1,0:T(8,128)S(1)}, u32[]{:S(2)}, u32[]{:S(2)}) collective-permute-start(f32[256,128]{1,0:T(8,128)S(1)} %shard_map.28), channel_id=1, source_target_pairs={{0,1},{1,0},{2,3},{3,2},{4,5},{5,4},{6,7},{7,6},{8,9},{9,8},{10,11... | collective-permute-start | bytes 393224 | tf_op jit(solution)/shard_map/ppermute | solution.py:269
  9.8 1.3 %collective-permute-done = f32[256,128]{1,0:T(8,128)S(1)} collective-permute-done((f32[256,128]{1,0:T(8,128)S(1)}, f32[256,128]{1,0:T(8,128)S(1)}, u32[]{:S(2)}, u32[]{:S(2)}) %collective-permute-start) | collective-permute-done | bytes 131104 | tf_op jit(solution)/shard_map/ppermute | solution.py:269
  11.2 4.3 %collective-permute-start.1 = (f32[256,128]{1,0:T(8,128)S(1)}, f32[256,128]{1,0:T(8,128)S(1)}, u32[]{:S(2)}, u32[]{:S(2)}) collective-permute-start(f32[256,128]{1,0:T(8,128)S(1)} %add.3.feat_ref), channel_id=1, source_target_pairs={{0,16},{16,0},{1,17},{17,1},{2,18},{18,2},{3,19},{19,3},{4,20},{20... | collective-permute-start | bytes 393224 | tf_op jit(solution)/shard_map/ppermute | solution.py:274
  15.4 3.8 %collective-permute-done.1.other_ref = f32[256,128]{1,0:T(8,128)S(1)} collective-permute-done((f32[256,128]{1,0:T(8,128)S(1)}, f32[256,128]{1,0:T(8,128)S(1)}, u32[]{:S(2)}, u32[]{:S(2)}) %collective-permute-start.1) | collective-permute-done | bytes 131104 | tf_op jit(solution)/shard_map/ppermute | solution.py:274
  19.2 0.0 all-to-all-done.received_ref
  19.2 0.7 shard_map.29
  20.0 9.7 %all-to-all-start.1 = ((f32[4,16,1024]{2,1,0:T(8,128)}), f32[4,16,1024]{2,1,0:T(8,128)S(1)}, u32[]{:S(2)}, u32[]{:S(2)}) async-start(f32[4,16,1024]{2,1,0:T(8,128)} %get-tuple-element.13), calls=%async_computation.1 | async-start | bytes 524288 | tf_op jit(solution)/shard_map/all_to_all | solution.py:279
  29.7 2.3 %collective-permute-start.2 = (f32[256,128]{1,0:T(8,128)S(1)}, f32[256,128]{1,0:T(8,128)S(1)}, u32[]{:S(2)}, u32[]{:S(2)}) collective-permute-start(f32[256,128]{1,0:T(8,128)S(1)} %get-tuple-element.14.feat_ref), channel_id=1, source_target_pairs={{0,2},{4,6},{8,10},{12,14},{2,0},{6,4},{10,8},{14,12},{1,3},{5,7},... | collective-permute-start | bytes 393224 | tf_op jit(solution)/shard_map/ppermute | solution.py:245
  32.0 4.5 %collective-permute-done.2.other_ref = f32[256,128]{1,0:T(8,128)S(1)} collective-permute-done((f32[256,128]{1,0:T(8,128)S(1)}, f32[256,128]{1,0:T(8,128)S(1)}, u32[]{:S(2)}, u32[]{:S(2)}) %collective-permute-start.2) | collective-permute-done | bytes 131104 | tf_op jit(solution)/shard_map/ppermute | solution.py:245
  36.5 3.8 %all-to-all-done.1.received_ref = f32[4,16,1024]{2,1,0:T(8,128)S(1)} async-done(((f32[4,16,1024]{2,1,0:T(8,128)}), f32[4,16,1024]{2,1,0:T(8,128)S(1)}, u32[]{:S(2)}, u32[]{:S(2)}) %all-to-all-start.1) | async-done | bytes 262176 | tf_op jit(solution)/shard_map/all_to_all | solution.py:279
  40.3 0.7 shard_map.30
  41.1 3.4 %all-to-all-start.2 = ((f32[4,16,1024]{2,1,0:T(8,128)}), f32[4,16,1024]{2,1,0:T(8,128)S(1)}, u32[]{:S(2)}, u32[]{:S(2)}) async-start(f32[4,16,1024]{2,1,0:T(8,128)} %get-tuple-element.15), calls=%async_computation.2 | async-start | bytes 524288 | tf_op jit(solution)/shard_map/all_to_all | solution.py:289
  44.5 3.5 %collective-permute-start.3 = (f32[256,128]{1,0:T(8,128)S(1)}, f32[256,128]{1,0:T(8,128)S(1)}, u32[]{:S(2)}, u32[]{:S(2)}) collective-permute-start(f32[256,128]{1,0:T(8,128)S(1)} %get-tuple-element.16.feat_ref), channel_id=1, source_target_pairs={{2,4},{6,8},{10,12},{14,0},{4,2},{8,6},{12,10},{0,14},{3,5},{7,9},... | collective-permute-start | bytes 393224 | tf_op jit(solution)/shard_map/ppermute | solution.py:245
  48.0 3.4 %collective-permute-done.3.other_ref = f32[256,128]{1,0:T(8,128)S(1)} collective-permute-done((f32[256,128]{1,0:T(8,128)S(1)}, f32[256,128]{1,0:T(8,128)S(1)}, u32[]{:S(2)}, u32[]{:S(2)}) %collective-permute-start.3) | collective-permute-done | bytes 131104 | tf_op jit(solution)/shard_map/ppermute | solution.py:245
  51.4 3.2 %all-to-all-done.2.received_ref = f32[4,16,1024]{2,1,0:T(8,128)S(1)} async-done(((f32[4,16,1024]{2,1,0:T(8,128)}), f32[4,16,1024]{2,1,0:T(8,128)S(1)}, u32[]{:S(2)}, u32[]{:S(2)}) %all-to-all-start.2) | async-done | bytes 262176 | tf_op jit(solution)/shard_map/all_to_all | solution.py:289
  54.6 1.0 %shard_map.31 = (f32[4,4,16,1024]{3,2,1,0:T(8,128)}, f32[256,128]{1,0:T(8,128)S(1)}) custom-call(f32[4,16,1024]{2,1,0:T(8,128)S(1)} %all-to-all-done.2.received_ref, f32[256,128]{1,0:T(8,128)S(1)} %get-tuple-element.16.feat_ref, f32[256,128]{1,0:T(8,128)S(1)} %collective-permute-done.3.other_ref), custom_call_target="tpu_custom_call" | custom-call | flops 1048576 | bytes 2097152 | tf_op jit(solution)/shard_map/pallas_call | solution.py:60
  55.6 4.9 %all-to-all-start.3 = ((f32[4,4,16,1024]{3,2,1,0:T(8,128)}), f32[4,4,16,1024]{3,2,1,0:T(8,128)S(1)}, u32[]{:S(2)}, u32[]{:S(2)}) async-start(f32[4,4,16,1024]{3,2,1,0:T(8,128)} %get-tuple-element.17), calls=%async_computation.3 | async-start | bytes 2097152 | tf_op jit(solution)/shard_map/all_to_all | solution.py:300
  60.4 6.0 %collective-permute-start.4 = (f32[256,128]{1,0:T(8,128)S(1)}, f32[256,128]{1,0:T(8,128)S(1)}, u32[]{:S(2)}, u32[]{:S(2)}) collective-permute-start(f32[256,128]{1,0:T(8,128)S(1)} %get-tuple-element.18.feat_ref), channel_id=1, source_target_pairs={{2,12},{4,10},{0,6},{8,14},{12,2},{10,4},{6,0},{14,8},{3,13},{5,11... | collective-permute-start | bytes 393224 | tf_op jit(solution)/shard_map/ppermute | solution.py:245
  66.5 3.9 %collective-permute-done.4.other_ref = f32[256,128]{1,0:T(8,128)S(1)} collective-permute-done((f32[256,128]{1,0:T(8,128)S(1)}, f32[256,128]{1,0:T(8,128)S(1)}, u32[]{:S(2)}, u32[]{:S(2)}) %collective-permute-start.4) | collective-permute-done | bytes 131104 | tf_op jit(solution)/shard_map/ppermute | solution.py:245
  70.4 2.9 %shard_map.32.delta_ref = f32[64,4096]{1,0:T(8,128)S(1)} custom-call(f32[256,128]{1,0:T(8,128)S(1)} %get-tuple-element.18.feat_ref, f32[256,128]{1,0:T(8,128)S(1)} %collective-permute-done.4.other_ref, f32[64,4096]{1,0:T(8,128)S(1)} %bitcast.6, bf16[2,128,4096]{2,1,0:T(8,128)(2,1)} %bitcast.8), custom_call_target="tpu_custom_call" | custom-call | flops 734003200 | bytes 8388608 | tf_op jit(solution)/shard_map/pallas_call | solution.py:60
  73.3 0.0 all-to-all-done.3.average_ref
  73.3 0.9 shard_map.33
  74.2 1.9 %collective-permute-start.5 = (f32[24,128]{1,0:T(8,128)S(1)}, f32[24,128]{1,0:T(8,128)S(1)}, u32[]{:S(2)}, u32[]{:S(2)}) collective-permute-start(f32[24,128]{1,0:T(8,128)S(1)} %get-tuple-element.19.left_ref), channel_id=1, source_target_pairs={{0,1},{1,0},{2,3},{3,2},{4,5},{5,4},{6,7},{7,6},{8,9},{9,8},{10,11... | collective-permute-start | bytes 36872 | tf_op jit(solution)/shard_map/ppermute | solution.py:327
  76.1 1.1 %collective-permute-done.5.right_ref = f32[24,128]{1,0:T(8,128)S(1)} collective-permute-done((f32[24,128]{1,0:T(8,128)S(1)}, f32[24,128]{1,0:T(8,128)S(1)}, u32[]{:S(2)}, u32[]{:S(2)}) %collective-permute-start.5) | collective-permute-done | bytes 12320 | tf_op jit(solution)/shard_map/ppermute | solution.py:327
  77.2 16.8 %all_to_all.25.parts_ref = f32[16,24,128]{2,1,0:T(8,128)S(1)} all-to-all(f32[16,24,128]{2,1,0:T(8,128)S(1)} %shard_map.34), channel_id=1, replica_groups=mesh['x'=4,'zh'=4,'zl'=2,'y'=8,'core'=2] {'zl','y'}, dimensions={0} | all-to-all | bytes 393216 | tf_op jit(solution)/shard_map/all_to_all | solution.py:331
  94.1 3.4 %shard_map.35 = f32[64,4096]{1,0:T(8,128)} custom-call(f32[16,24,128]{2,1,0:T(8,128)S(1)} %all_to_all.25.parts_ref, f32[64,4096]{1,0:T(8,128)S(1)} %get-tuple-element.20.mixed_ref), custom_call_target="tpu_custom_call" | custom-call | flops 419430400 | bytes 3145728 | tf_op jit(solution)/shard_map/pallas_call | solution.py:60
  (2 shorter events, 0.0 us)
Async XLA Ops:
  0.0 5.0 %copy-start = (f32[1,64,4096]{2,1,0:T(8,128)S(1)}, f32[1,64,4096]{2,1,0:T(8,128)}, u32[]{:S(2)}) copy-start(f32[1,64,4096]{2,1,0:T(8,128)} %param.2) | copy-start | bytes 3145732
  0.0 19.2 %all-to-all-start = ((f32[4,16,4096]{2,1,0:T(8,128)}), f32[4,16,4096]{2,1,0:T(8,128)S(1)}, u32[]{:S(2)}, u32[]{:S(2)}) async-start(f32[4,16,4096]{2,1,0:T(8,128)} %bitcast.4), calls=%async_computation | async-start | bytes 2097152 | tf_op jit(solution)/shard_map/all_to_all | solution.py:258
  7.9 3.2 %collective-permute-start = (f32[256,128]{1,0:T(8,128)S(1)}, f32[256,128]{1,0:T(8,128)S(1)}, u32[]{:S(2)}, u32[]{:S(2)}) collective-permute-start(f32[256,128]{1,0:T(8,128)S(1)} %shard_map.28), channel_id=1, source_target_pairs={{0,1},{1,0},{2,3},{3,2},{4,5},{5,4},{6,7},{7,6},{8,9},{9,8},{10,11... | collective-permute-start | bytes 393224 | tf_op jit(solution)/shard_map/ppermute | solution.py:269
  11.2 8.1 %collective-permute-start.1 = (f32[256,128]{1,0:T(8,128)S(1)}, f32[256,128]{1,0:T(8,128)S(1)}, u32[]{:S(2)}, u32[]{:S(2)}) collective-permute-start(f32[256,128]{1,0:T(8,128)S(1)} %add.3.feat_ref), channel_id=1, source_target_pairs={{0,16},{16,0},{1,17},{17,1},{2,18},{18,2},{3,19},{19,3},{4,20},{20... | collective-permute-start | bytes 393224 | tf_op jit(solution)/shard_map/ppermute | solution.py:274
  20.0 20.3 %all-to-all-start.1 = ((f32[4,16,1024]{2,1,0:T(8,128)}), f32[4,16,1024]{2,1,0:T(8,128)S(1)}, u32[]{:S(2)}, u32[]{:S(2)}) async-start(f32[4,16,1024]{2,1,0:T(8,128)} %get-tuple-element.13), calls=%async_computation.1 | async-start | bytes 524288 | tf_op jit(solution)/shard_map/all_to_all | solution.py:279
  29.7 6.8 %collective-permute-start.2 = (f32[256,128]{1,0:T(8,128)S(1)}, f32[256,128]{1,0:T(8,128)S(1)}, u32[]{:S(2)}, u32[]{:S(2)}) collective-permute-start(f32[256,128]{1,0:T(8,128)S(1)} %get-tuple-element.14.feat_ref), channel_id=1, source_target_pairs={{0,2},{4,6},{8,10},{12,14},{2,0},{6,4},{10,8},{14,12},{1,3},{5,7},... | collective-permute-start | bytes 393224 | tf_op jit(solution)/shard_map/ppermute | solution.py:245
  41.1 13.5 %all-to-all-start.2 = ((f32[4,16,1024]{2,1,0:T(8,128)}), f32[4,16,1024]{2,1,0:T(8,128)S(1)}, u32[]{:S(2)}, u32[]{:S(2)}) async-start(f32[4,16,1024]{2,1,0:T(8,128)} %get-tuple-element.15), calls=%async_computation.2 | async-start | bytes 524288 | tf_op jit(solution)/shard_map/all_to_all | solution.py:289
  44.5 6.9 %collective-permute-start.3 = (f32[256,128]{1,0:T(8,128)S(1)}, f32[256,128]{1,0:T(8,128)S(1)}, u32[]{:S(2)}, u32[]{:S(2)}) collective-permute-start(f32[256,128]{1,0:T(8,128)S(1)} %get-tuple-element.16.feat_ref), channel_id=1, source_target_pairs={{2,4},{6,8},{10,12},{14,0},{4,2},{8,6},{12,10},{0,14},{3,5},{7,9},... | collective-permute-start | bytes 393224 | tf_op jit(solution)/shard_map/ppermute | solution.py:245
  55.6 17.7 %all-to-all-start.3 = ((f32[4,4,16,1024]{3,2,1,0:T(8,128)}), f32[4,4,16,1024]{3,2,1,0:T(8,128)S(1)}, u32[]{:S(2)}, u32[]{:S(2)}) async-start(f32[4,4,16,1024]{3,2,1,0:T(8,128)} %get-tuple-element.17), calls=%async_computation.3 | async-start | bytes 2097152 | tf_op jit(solution)/shard_map/all_to_all | solution.py:300
  60.4 10.0 %collective-permute-start.4 = (f32[256,128]{1,0:T(8,128)S(1)}, f32[256,128]{1,0:T(8,128)S(1)}, u32[]{:S(2)}, u32[]{:S(2)}) collective-permute-start(f32[256,128]{1,0:T(8,128)S(1)} %get-tuple-element.18.feat_ref), channel_id=1, source_target_pairs={{2,12},{4,10},{0,6},{8,14},{12,2},{10,4},{6,0},{14,8},{3,13},{5,11... | collective-permute-start | bytes 393224 | tf_op jit(solution)/shard_map/ppermute | solution.py:245
  74.2 3.1 %collective-permute-start.5 = (f32[24,128]{1,0:T(8,128)S(1)}, f32[24,128]{1,0:T(8,128)S(1)}, u32[]{:S(2)}, u32[]{:S(2)}) collective-permute-start(f32[24,128]{1,0:T(8,128)S(1)} %get-tuple-element.19.left_ref), channel_id=1, source_target_pairs={{0,1},{1,0},{2,3},{3,2},{4,5},{5,4},{6,7},{7,6},{8,9},{9,8},{10,11... | collective-permute-start | bytes 36872 | tf_op jit(solution)/shard_map/ppermute | solution.py:327
